TPU v7x, 256 devices: a whole 4x4x8 slice. The times are simulated.
256 devices in a mesh: ctx: 16 (over z_hi, x), dp: 16 (over z_lo, y, core).
Axes of the slice: x: 4, y: 4, z: 8 (z_hi: 4, z_lo: 2; z = z_hi * 2 + z_lo), core: 2. Of those that a mesh axis runs over, the one named last changes fastest.
Arguments:
- doc_states: bfloat16 [4096, 4096], P('dp', 'ctx'), may hold values from -3 to 3
- context: bfloat16 [128, 4096], P('ctx'), may hold values from -6 to 6
- norm_gain: float32 [4096], replicated, may hold values from 0.5 to 1.5
- w_query: bfloat16 [4096, 2048], P(None, 'ctx'), may hold values from -0.09375 to 0.09375
- w_key: bfloat16 [4096, 2048], P(None, 'ctx'), may hold values from -0.09375 to 0.09375
- w_value: bfloat16 [4096, 2048], P(None, 'ctx'), may hold values from -0.09375 to 0.09375
- w_out: bfloat16 [2048, 4096], P('ctx'), may hold values from -0.125 to 0.125
- partners: int32 [64], P('dp'), may hold values from 0 to 63, as said below
Outputs:
- loss: float32 [], replicated
- grad_context: float32 [128, 4096], P('ctx')
- grad_query: float32 [4096, 2048], P('dp', 'ctx')
- grad_key: float32 [4096, 2048], P('dp', 'ctx')
- grad_value: float32 [4096, 2048], P('dp', 'ctx')
- grad_out: float32 [2048, 4096], P('ctx', 'dp')
Inputs may be any that keep to these rules, and one draw needn't show every extreme that they name: partners[i] != i, and every document is the partner of exactly one document.
All inputs are finite; a program needn't handle non-finite values.
Results may differ from a plain program's by a relative error of at most 0.017.
Values may be sent and summed in bfloat16 or wider, within the bound.
No kernel may reach another device: no remote copies, remote signals or barrier semaphores. Data moves between devices by JAX's collectives and lax.ppermute only.
A program may use at most 64 MiB of HBM per device.

v0:
```python
import functools

import jax
import jax.numpy as jnp
from jax import lax
from jax.experimental import pallas as pl
from jax.experimental.pallas import tpu as pltpu
from jax.sharding import Mesh, PartitionSpec as P

HD = 128
DOC_LEN = 64

EPS = 1e-05
TEMPERATURE = 0.05
LOSS_SCALE = 65536.0
EXACT = lax.Precision.HIGHEST
FACTOR = HD**-0.5

CTX = ("zh", "x")
DP = ("zl", "y", "co")
EVERY = CTX + DP

f32 = jnp.float32
bf16 = jnp.bfloat16

ROWS_BY_ROWS = (((1,), (1,)), ((), ()))
COLS_BY_COLS = (((0,), (0,)), ((), ()))


def wide(a):
    return a.astype(f32)


def dot(a, b):
    return jnp.dot(a, b, preferred_element_type=f32)


def dot_nt(a, b, precision=None):
    return lax.dot_general(a, b, ROWS_BY_ROWS, precision=precision, preferred_element_type=f32)


def dot_tn(a, b, precision=None):
    return lax.dot_general(a, b, COLS_BY_COLS, precision=precision, preferred_element_type=f32)


def split(a, count):
    out = []
    for _ in range(count):
        head = a.astype(bf16)
        out.append(head)
        a = a - wide(head)
    return out


def stacked_pieces(a, count):
    return jnp.concatenate(split(a, count), axis=0)


def folded(a, count):
    rows = a.shape[0] // count
    return sum(a[i * rows : (i + 1) * rows] for i in reversed(range(count)))


def iota(shape, axis):
    return lax.broadcasted_iota(jnp.int32, shape, axis)


def as_row(column):
    n = column.shape[0]
    return jnp.sum(jnp.where(iota((n, n), 0) == iota((n, n), 1), column, 0.0), 0, keepdims=True)


def position():
    return [lax.axis_index(a) for a in EVERY]


def inverse_rms(a):
    return lax.rsqrt(jnp.mean(a * a, axis=-1, keepdims=True) + EPS)


def probabilities(q, k, ctx_keys):
    n = q.shape[0]
    same = iota((n, n), 0) // DOC_LEN == iota((n, n), 1) // DOC_LEN
    ctx_exps = jnp.exp(dot_nt(q, ctx_keys) * FACTOR)
    own_exps = jnp.where(same, jnp.exp(dot_nt(q, k) * FACTOR), 0.0)
    total = jnp.sum(ctx_exps, 1, keepdims=True) + jnp.sum(own_exps, 1, keepdims=True)
    return ctx_exps / total, own_exps / total


def call(kernel, out_shape, in_specs, scratch=(), vmem=16, flops=10**9):
    in_specs = [
        pl.BlockSpec(memory_space=pl.ANY if s == "a" else pltpu.VMEM) for s in in_specs
    ]
    return pl.pallas_call(
        kernel,
        out_shape=out_shape,
        in_specs=in_specs,
        out_specs=jax.tree.map(lambda _: pl.BlockSpec(memory_space=pltpu.VMEM), out_shape),
        scratch_shapes=scratch,
        compiler_params=pltpu.CompilerParams(vmem_limit_bytes=vmem * 2**20),
        cost_estimate=pl.CostEstimate(flops=flops, bytes_accessed=4 * 10**6, transcendentals=0),
    )


def shape(*dims, dtype=f32):
    return jax.ShapeDtypeStruct(dims, dtype)


def forward_kernel(gain, partners, wq, wk, wv, wo, ctx, z0, z1, z2, z3, *refs):
    qkv, own, branch, mix, normed, ctx_columns, weights, last, sems = refs
    pos = position()
    fetch = [
        pltpu.make_async_copy(w, weights.at[:, pl.ds(i * HD, HD)], sems.at[i])
        for i, w in enumerate((wq, wk, wv))
    ]
    fetch.append(pltpu.make_async_copy(wo, last, sems.at[3]))
    for copy in fetch:
        copy.start()
    tok, feat = qkv.shape[0], z0.shape[2]
    blocks = []
    for along_x, ref in enumerate((z0, z1, z2, z3)):
        blocks += [(ref, i, along_x, i) for i in range(4)]
        for i in range(4):
            place = ((pos[0] - i) & 3) * 4 + ((pos[1] - along_x) & 3)
            ctx_columns[pl.ds(pl.multiple_of(place * 8, 8), 8), :] = wide(ref[i, tok:, :])[:8]
    ctx_inv = jnp.sum(wide(ctx[:, 2 * HD :]), axis=1, keepdims=True)
    dp = (pos[2] * 4 + pos[3]) * 2 + pos[4]
    here = pl.ds(pl.multiple_of(dp * feat, feat), feat)
    ctx_columns[...] = ctx_columns[...] * ctx_inv * gain[:, here]
    docs = tok // DOC_LEN
    averaging = jnp.where(iota((8, tok), 0) == iota((8, tok), 1) // DOC_LEN, 1 / DOC_LEN, 0.0)
    averaging = averaging.astype(bf16)
    squares = jnp.zeros((tok, 1), f32)
    for ref, i, _, _ in blocks:
        rows = wide(ref[i, :tok, :])
        squares = squares + jnp.sum(rows * rows, axis=1, keepdims=True)
    inv = lax.rsqrt(squares / (16 * feat) + EPS)
    total = jnp.zeros((tok, 3 * HD), f32)
    for copy in fetch[:3]:
        copy.wait()
    for ref, i, along_x, along_z in blocks:
        place = ((pos[0] - along_z) & 3) * 4 + ((pos[1] - along_x) & 3)
        here = pl.ds(pl.multiple_of(place * feat, feat), feat)
        rows = ref[i, :tok, :]
        ready = (wide(rows) * inv * gain[:, here]).astype(bf16)
        normed[:, here] = ready
        total = total + dot(ready, weights[here, :])
        own[:, here] = dot(averaging, rows)[:docs]
    total = total.astype(bf16)
    qkv[...] = total
    q, k, v = total[:, :HD], total[:, HD : 2 * HD], total[:, 2 * HD :]
    ctx_probs, own_probs = probabilities(q, k, ctx[:, :HD])
    ctx_weights = ctx_probs.astype(bf16)
    mixture = dot(ctx_weights, ctx[:, HD : 2 * HD]) + dot(own_probs.astype(bf16), v)
    mean = dot(averaging, mixture.astype(bf16))
    mix[:, :HD] = mean[:docs]
    mix[:, HD : 2 * HD] = dot(averaging, ctx_weights)[:docs] * DOC_LEN
    mix[:, 2 * HD :] = jnp.broadcast_to(wide(partners[...]), (docs, HD))
    fetch[3].wait()
    branch[...] = folded(dot(stacked_pieces(mean, 3), last[...]), 3)[:docs]


def by_token(a):
    rows = [jnp.broadcast_to(a[i : i + 1], (DOC_LEN, a.shape[1])) for i in range(4)]
    return jnp.concatenate(rows, axis=0)


def backward(own, ctx, upstream, grads, grad_ctx_keys):
    q, k, v = (own[:, j * HD : (j + 1) * HD] for j in range(3))
    ctx_probs, own_probs = probabilities(q, k, ctx[:, :HD])
    ctx_dweights = by_token(dot_nt(upstream.astype(bf16), ctx[:, HD : 2 * HD]))
    own_dweights = by_token(dot_nt(upstream.astype(bf16), v))
    inner = jnp.sum(ctx_probs * ctx_dweights, 1, keepdims=True)
    inner = inner + jnp.sum(own_probs * own_dweights, 1, keepdims=True)
    ctx_dscores = (ctx_probs * (ctx_dweights - inner) * FACTOR).astype(bf16)
    own_dscores = (own_probs * (own_dweights - inner) * FACTOR).astype(bf16)
    grad_ctx_keys[...] = dot_tn(ctx_dscores, q)
    grads[:, :HD] = (dot(ctx_dscores, ctx[:, :HD]) + dot(own_dscores, k)).astype(bf16)
    grads[:, HD : 2 * HD] = dot_tn(own_dscores, q).astype(bf16)
    grad_v = dot_tn(own_probs.astype(bf16), by_token(upstream).astype(bf16))
    grads[:, 2 * HD :] = grad_v.astype(bf16)


def loss_kernel(wo, mine, theirs, ctx, own, *refs):
    loss, grad_out, grads, grad_ctx_keys, grad_ctx_values, pooled, mix, weights, extra, slope, up = refs
    pos = position()
    width = wo.shape[1]
    co, y, dp = pos[4], pos[3], (pos[2] * 4 + pos[3]) * 2 + pos[4]
    for i in range(8):
        messages, core = (mine, co) if i < 4 else (theirs, 1 - co)
        here = pl.ds(pl.multiple_of((core * 4 + ((y - i % 4) & 3)) * 8, 8), 8)
        pooled[here, :] = messages[i % 4, :, :width]
        mix[here, :] = messages[i % 4, :, width : width + HD]
        weights[here, :] = messages[i % 4, :, width + HD : width + 2 * HD]
        extra[here, :] = messages[i % 4, :, width + 2 * HD :]
    n = pooled.shape[0]
    vectors = pooled[...]
    length = jnp.sqrt(jnp.sum(vectors * vectors, axis=1, keepdims=True) + 1e-06)
    unit = vectors / length
    parts = stacked_pieces(vectors, 3)
    products = dot_nt(parts, parts)
    gram = jnp.zeros((n, n), f32)
    for i, j in ((2, 1), (1, 2), (2, 0), (1, 1), (0, 2), (1, 0), (0, 1), (0, 0)):
        gram = gram + products[i * n : (i + 1) * n, j * n : (j + 1) * n]
    scores = gram / (length * as_row(length)) / TEMPERATURE
    diagonal = iota((n, n), 0) == iota((n, n), 1)

    def document(axis):
        at = iota((n, n), axis)
        return (((at >> 2) & 1) * 32 + ((at >> 3) & 3) * 8 + (at >> 5) * 4 + (at & 3)).astype(f32)

    partners = extra[:, 0:1]
    chosen = jnp.where(partners == document(1), 1.0, 0.0)
    chosen_back = jnp.where(as_row(partners) == document(0), 1.0, 0.0)
    exps = jnp.where(diagonal, 0.0, jnp.exp(scores))
    sums = jnp.sum(exps, axis=1, keepdims=True)
    picked = jnp.sum(scores * chosen, axis=1, keepdims=True)
    loss[...] = jnp.sum(jnp.log(sums) - picked, axis=0, keepdims=True) / n
    coeff = (exps / sums - chosen) / n * LOSS_SCALE
    coeff_back = (exps / as_row(sums) - chosen_back) / n * LOSS_SCALE
    lead, second, third = split(coeff + coeff_back, 3)
    units = split(unit, 3)
    left = jnp.concatenate([third, second, second, lead, lead, lead], axis=1)
    right = jnp.concatenate([units[i] for i in (0, 1, 0, 2, 1, 0)], axis=0)
    grad_unit = dot(left, right) / TEMPERATURE
    radial = jnp.sum(unit * grad_unit, axis=1, keepdims=True)
    slope[...] = (grad_unit - unit * radial) / length
    part = slope[:, pl.ds(pl.multiple_of(dp * (width // 16), width // 16), width // 16)]
    grad_out[...] = dot_tn(mix[...], part, EXACT)
    upstream = folded(dot_nt(stacked_pieces(slope[...] / DOC_LEN, 3), wo[...]), 3)
    up[...] = wide(upstream.astype(bf16))
    grad_ctx_values[...] = dot_tn(weights[...], up[...], EXACT)
    upstream = up[pl.ds(pl.multiple_of(co * (n // 2) + y * 8, 8), 8), :]
    upstream = jnp.where(pos[2] == 0, upstream[:4], upstream[4:])
    upstream = jnp.concatenate([upstream, upstream], axis=0)
    backward(own, ctx, upstream, grads, grad_ctx_keys)


def context_kernel(own, one, two, three, values, wk, wv, total, out0, out1, out2, out3, part):
    pos = position()
    half = part.shape[1]
    grad = (own[...] + two[...]) + (one[...] + three[...])
    grad = jnp.concatenate([grad, values[...]], axis=1)
    total[...] = grad
    here = pl.ds(pl.multiple_of(pos[4] * half, half), half)
    got = dot_nt(stacked_pieces(grad[:, :HD], 2), wk[here, :])
    got = got + dot_nt(stacked_pieces(grad[:, HD:], 2), wv[here, :])
    part[...] = folded(got, 2)
    for k, out in enumerate((out0, out1, out2, out3)):
        at = (pos[1] + k) & 3
        rows = [part[pl.ds(pl.multiple_of(z * 32 + at * 8, 8), 8), :] for z in range(4)]
        out[...] = jnp.concatenate(rows, axis=0).astype(out.dtype)


def middle_kernel(own, one, two, three, out0, out1, out2, out3, total):
    pos = position()
    total[...] = (own[...] + wide(two[...])) + (wide(one[...]) + wide(three[...]))
    for k, out in enumerate((out0, out1, out2, out3)):
        at = (pos[0] + k) & 3
        out[...] = total[pl.ds(pl.multiple_of(at * 8, 8), 8), :]


def finish_kernel(context, gain, mine, theirs, out):
    pos = position()
    half = mine.shape[1]
    low = pos[4] == 0
    grad = jnp.concatenate(
        [jnp.where(low, mine[...], theirs[...]), jnp.where(low, theirs[...], mine[...])], axis=1
    )
    rows = wide(context[...])
    inv = inverse_rms(rows)
    scaled = gain[...] * grad
    out[...] = inv * scaled - rows * inv**3 * jnp.mean(rows * scaled, axis=1, keepdims=True)


def weight_kernel(side, normed, grads, out):
    feat = out.shape[1]
    core = position()[4]
    core = core if side == 0 else 1 - core
    right = grads[...]
    for i in range(8):
        here = pl.ds(pl.multiple_of((i * 2 + core) * feat, feat), feat)
        out[i] = dot_tn(normed[:, here], right).astype(bf16)


def weight_y_kernel(mine, came, out0, out1, out2, out3):
    y = position()[3]
    for k, out in enumerate((out0, out1, out2, out3)):
        for zl in range(2):
            chip = zl * 4 + ((y + k) & 3)
            out[zl] = (wide(mine[chip]) + wide(came[chip])).astype(out.dtype)


def weight_z_kernel(own, one, two, three, mine, theirs):
    pos = position()
    for zl in range(2):
        got = (own[zl] + wide(two[zl])) + (wide(one[zl]) + wide(three[zl]))

        @pl.when(pos[2] == zl)
        def _():
            mine[...] = got

        @pl.when(pos[2] != zl)
        def _():
            theirs[...] = got.astype(bf16)


def weight_last_kernel(mine, theirs, ctx_columns, grad_ctx, grad_query, grad_key, grad_value):
    total = mine[...] + wide(theirs[...])
    columns = ctx_columns[...].astype(bf16)
    lead, rest = split(grad_ctx[...], 2)
    from_ctx = dot_tn(columns, rest) + dot_tn(columns, lead)
    grad_query[...] = total[:, :HD]
    grad_key[...] = total[:, HD : 2 * HD] + from_ctx[:, :HD]
    grad_value[...] = total[:, 2 * HD :] + from_ctx[:, HD:]


def shift(a, axis, k):
    return lax.ppermute(a, axis, [(i, (i + k) % 4) for i in range(4)])


def others(a, axis):
    return [shift(a, axis, k) for k in (1, 2, 3)]


def other(a, axis):
    return lax.ppermute(a, axis, [(0, 1), (1, 0)])


def pair(a, axis):
    b = other(a, axis)
    first = lax.axis_index(axis) == 0
    return jnp.where(first, jnp.concatenate([a, b]), jnp.concatenate([b, a]))


def ring_sum(a, axis):
    one, two, three = others(a, axis)
    return (a + two) + (one + three)


def hlo_split(a, count):
    out = []
    for _ in range(count):
        out.append(lax.reduce_precision(a, 8, 7))
        a = a - out[-1]
    return out


def spread(block, axis, size):
    copies = jnp.broadcast_to(block[None], (size,) + block.shape)
    return lax.all_to_all(copies, axis, 0, 0)


def shards(doc_states, context, gain, w_query, w_key, w_value, w_out, partners):
    tok, feat = doc_states.shape
    docs = tok // DOC_LEN
    width = w_query.shape[0]
    gain_row = gain.reshape(1, width)

    ctx_part = lax.dynamic_slice_in_dim(context, lax.axis_index(DP) * feat, feat, 1)
    block = jnp.concatenate([doc_states, ctx_part, jnp.zeros_like(ctx_part)], axis=0)
    block = jnp.stack([block] + others(block, "zh"))
    rows = [block] + others(block, "x")

    swap = [(c * 16 + d, d * 16 + c) for c in range(16) for d in range(16)]
    named_rows = wide(lax.ppermute(context, EVERY, swap))
    named_rows, _ = lax.optimization_barrier((named_rows, block))
    inv = inverse_rms(named_rows)
    named_rows = (named_rows * inv * gain).astype(bf16)
    few = [dot(named_rows, w_key), dot(named_rows, w_value)] + hlo_split(inv, 3)
    few = jnp.concatenate([a.astype(bf16) for a in few], axis=1)
    few = jnp.pad(few, ((0, 0), (0, 3 * HD - few.shape[1])))
    ctx_kv = spread(few, DP, 16).reshape(-1, 3 * HD)

    qkv, own_mean, branch, mix, normed, ctx_columns = call(
        forward_kernel,
        (
            shape(tok, 3 * HD, dtype=bf16),
            shape(docs, width),
            shape(docs, width),
            shape(docs, 3 * HD),
            shape(tok, width, dtype=bf16),
            shape(HD, feat),
        ),
        ["v"] * 2 + ["a"] * 4 + ["v"] * 5,
        scratch=[
            pltpu.VMEM((width, 3 * HD), bf16),
            pltpu.VMEM((HD, width), bf16),
            pltpu.SemaphoreType.DMA((4,)),
        ],
        vmem=24,
    )(gain_row, partners[:, None], w_query, w_key, w_value, w_out, ctx_kv, *rows)

    pooled = own_mean + ring_sum(ring_sum(branch, "x"), "zh")
    message = jnp.concatenate([pooled, mix], axis=1)
    message = pair(message, "zl")
    messages = jnp.stack([message] + others(message, "y"))
    total = 64
    loss, grad_out, grads, grad_ctx_keys, grad_ctx_values = call(
        loss_kernel,
        (
            shape(1, 1),
            shape(HD, feat),
            shape(tok, 3 * HD, dtype=bf16),
            shape(HD, HD),
            shape(HD, HD),
        ),
        ["v"] * 5,
        scratch=[
            pltpu.VMEM((total, width), f32),
            pltpu.VMEM((total, HD), f32),
            pltpu.VMEM((total, HD), f32),
            pltpu.VMEM((total, HD), f32),
            pltpu.VMEM((total, width), f32),
            pltpu.VMEM((total, HD), f32),
        ],
        vmem=24,
    )(w_out, messages, other(messages, "co"), ctx_kv, qkv)

    half = width // 2
    rows = 4 * context.shape[0]
    came = other(grad_ctx_keys, "co")
    came, grads = lax.optimization_barrier((came, grads))
    grad_ctx_keys = grad_ctx_keys + came
    grad_ctx_keys = grad_ctx_keys + other(grad_ctx_keys, "zl")
    by_y = others(grad_ctx_keys, "y")
    grad_ctx, part, *sent = call(
        context_kernel,
        (shape(HD, 2 * HD), shape(rows, half)) + (shape(rows, half, dtype=bf16),) * 3,
        ["v"] * 7,
        scratch=[pltpu.VMEM((4 * rows, half), f32)],
    )(grad_ctx_keys, *by_y, grad_ctx_values, w_key, w_value)
    came = [shift(a, "x", k) for k, a in zip((1, 2, 3), sent)]
    part, *sent = call(
        middle_kernel,
        (shape(rows // 4, half),) * 4,
        ["v"] * 4,
        scratch=[pltpu.VMEM((rows, half), f32)],
    )(part, *came)
    one, two, three = [shift(a, "zh", k) for k, a in zip((1, 2, 3), sent)]
    part = (part + two) + (one + three)
    grad_context = call(finish_kernel, shape(*context.shape), ["v"] * 4, flops=10**9)(
        context, gain_row, part, other(part, "co")
    )

    theirs, mine = (
        call(
            functools.partial(weight_kernel, side),
            shape(8, feat, 3 * HD, dtype=bf16),
            ["v"] * 2,
        )(normed, grads)
        for side in (1, 0)
    )
    came, _ = lax.optimization_barrier((other(theirs, "co"), by_y[0]))
    mine, *sent = call(
        weight_y_kernel,
        (shape(2, feat, 3 * HD),) + (shape(2, feat, 3 * HD, dtype=bf16),) * 3,
        ["v"] * 2,
    )(mine, came)
    came = [shift(a, "y", k) for k, a in zip((1, 2, 3), sent)]
    mine, theirs = call(
        weight_z_kernel,
        (shape(feat, 3 * HD), shape(feat, 3 * HD, dtype=bf16)),
        ["v"] * 4,
    )(mine, *came)
    grad_query, grad_key, grad_value = call(
        weight_last_kernel, (shape(feat, HD),) * 3, ["v"] * 4
    )(mine, other(theirs, "zl"), ctx_columns, grad_ctx)
    return loss.reshape(()), grad_context, grad_query, grad_key, grad_value, grad_out


def solution(mesh):
    split = Mesh(mesh.devices.reshape(4, 4, 2, 4, 2), EVERY)
    in_specs = (
        P(DP, CTX),
        P(CTX, None),
        P(),
        P(None, CTX),
        P(None, CTX),
        P(None, CTX),
        P(CTX, None),
        P(DP),
    )
    out_specs = (P(), P(CTX, None), P(DP, CTX), P(DP, CTX), P(DP, CTX), P(CTX, DP))
    return jax.shard_map(
        shards, mesh=split, in_specs=in_specs, out_specs=out_specs, check_vma=False
    )
```

profile of v0, /device:TPU:1, one launch (start us, length us, event | category | flops | bytes accessed | tf_op | source)
XLA Modules:
  0.0 155.4 jit_solution(11049317390616682763)
XLA Ops:
  0.7 0.8 constant_dynamic-slice_fusion
  1.6 1.0 fusion.4
  2.6 3.9 %collective-permute-start.1 = (bf16[272,256]{1,0:T(8,128)(2,1)S(1)}, bf16[272,256]{1,0:T(8,128)(2,1)S(1)}, u32[]{:S(2)}, u32[]{:S(2)}) collective-permute-start(bf16[272,256]{1,0:T(8,128)(2,1)S(1)} %get-tuple-element.73), channel_id=1, source_target_pairs={{0,64},{64,128},{128,192},{192,0},{1,65},{65,129},{129,193},{193,1... | collective-permute-start | bytes 417800 | tf_op jit(solution)/shard_map/ppermute | solution.py:319
  6.5 5.1 %collective-permute-start.2 = (bf16[272,256]{1,0:T(8,128)(2,1)S(1)}, bf16[272,256]{1,0:T(8,128)(2,1)S(1)}, u32[]{:S(2)}, u32[]{:S(2)}) collective-permute-start(bf16[272,256]{1,0:T(8,128)(2,1)S(1)} %get-tuple-element.73), channel_id=1, source_target_pairs={{0,128},{64,192},{128,0},{192,64},{1,129},{65,193},{129,1},{193,65... | collective-permute-start | bytes 417800 | tf_op jit(solution)/shard_map/ppermute | solution.py:319
  11.6 2.4 %collective-permute-start.3 = (bf16[272,256]{1,0:T(8,128)(2,1)S(1)}, bf16[272,256]{1,0:T(8,128)(2,1)S(1)}, u32[]{:S(2)}, u32[]{:S(2)}) collective-permute-start(bf16[272,256]{1,0:T(8,128)(2,1)S(1)} %get-tuple-element.73), channel_id=1, source_target_pairs={{0,192},{64,0},{128,64},{192,128},{1,193},{65,1},{129,65},{193,129... | collective-permute-start | bytes 417800 | tf_op jit(solution)/shard_map/ppermute | solution.py:319
  14.0 4.5 %collective-permute-start = (bf16[8,4096]{1,0:T(8,128)(2,1)}, bf16[8,4096]{1,0:T(8,128)(2,1)S(1)}, u32[]{:S(2)}, u32[]{:S(2)}) collective-permute-start(bf16[8,4096]{1,0:T(8,128)(2,1)} %context.1), channel_id=1, source_target_pairs={{0,0},{1,16},{2,32},{3,48},{4,64},{5,80},{6,96},{7,112},{8,128},{9... | collective-permute-start | bytes 196616 | tf_op jit(solution)/shard_map/ppermute | solution.py:366
  18.5 2.4 %collective-permute-done = bf16[8,4096]{1,0:T(8,128)(2,1)S(1)} collective-permute-done((bf16[8,4096]{1,0:T(8,128)(2,1)}, bf16[8,4096]{1,0:T(8,128)(2,1)S(1)}, u32[]{:S(2)}, u32[]{:S(2)}) %collective-permute-start) | collective-permute-done | bytes 65568 | tf_op jit(solution)/shard_map/ppermute | solution.py:366
  21.0 4.3 %collective-permute-done.3 = bf16[272,256]{1,0:T(8,128)(2,1)S(1)} collective-permute-done((bf16[272,256]{1,0:T(8,128)(2,1)S(1)}, bf16[272,256]{1,0:T(8,128)(2,1)S(1)}, u32[]{:S(2)}, u32[]{:S(2)}) %collective-permute-start.3) | collective-permute-done | bytes 139296 | tf_op jit(solution)/shard_map/ppermute | solution.py:319
  25.3 1.3 collective-permute-start.4
  26.6 2.5 %collective-permute-start.5 = (bf16[4,272,256]{2,1,0:T(8,128)(2,1)S(1)}, bf16[4,272,256]{2,1,0:T(8,128)(2,1)}, u32[]{:S(2)}, u32[]{:S(2)}) collective-permute-start(bf16[4,272,256]{2,1,0:T(8,128)(2,1)S(1)} %pad_maximum_fusion.1.z0), channel_id=1, source_target_pairs={{0,32},{16,48},{32,0},{48,16},{1,33},{17,49},{33,1},{49,17},{2,34}... | collective-permute-start | bytes 1671176 | tf_op jit(solution)/shard_map/ppermute | solution.py:319
  29.1 1.2 collective-permute-start.6
  31.2 0.7 broadcast_in_dim.16
  31.9 9.5 %all-to-all-start = ((bf16[16,8,384]{2,1,0:T(8,128)(2,1)}), bf16[16,8,384]{2,1,0:T(8,128)(2,1)S(1)}, u32[]{:S(2)}, u32[]{:S(2)}) async-start(bf16[16,8,384]{2,1,0:T(8,128)(2,1)} %broadcast_in_dim.16), calls=%async_computation | async-start | bytes 196608 | tf_op jit(solution)/shard_map/all_to_all | solution.py:351
  41.5 5.8 %all-to-all-done = bf16[16,8,384]{2,1,0:T(8,128)(2,1)S(1)} async-done(((bf16[16,8,384]{2,1,0:T(8,128)(2,1)}), bf16[16,8,384]{2,1,0:T(8,128)(2,1)S(1)}, u32[]{:S(2)}, u32[]{:S(2)}) %all-to-all-start) | async-done | bytes 98336 | tf_op jit(solution)/shard_map/all_to_all | solution.py:351
  47.3 6.3 %collective-permute-done.5.z2 = bf16[4,272,256]{2,1,0:T(8,128)(2,1)} collective-permute-done((bf16[4,272,256]{2,1,0:T(8,128)(2,1)S(1)}, bf16[4,272,256]{2,1,0:T(8,128)(2,1)}, u32[]{:S(2)}, u32[]{:S(2)}) %collective-permute-start.5) | collective-permute-done | bytes 557088 | tf_op jit(solution)/shard_map/ppermute | solution.py:319
  53.6 1.2 copy-done.2
  54.8 1.1 copy-done.5
  55.9 1.2 copy-done.6
  57.1 1.2 copy-done.7
  58.3 5.4 %shard_map.127 = (bf16[256,384]{1,0:T(8,128)(2,1)S(1)}, f32[4,4096]{1,0:T(4,128)S(1)}, f32[4,4096]{1,0:T(4,128)S(1)}, f32[4,384]{1,0:T(4,128)S(1)}, bf16[256,409...) custom-call(f32[1,4096]{1,0:T(1,128)S(1)} %bitcast.21, s32[4,1]{1,0:T(4,128)S(1)} %copy.16.partners, ...), custom_call_target="tpu_custom_call" | custom-call | flops 1000000000 | bytes 4000000 | tf_op jit(solution)/shard_map/pallas_call | solution.py:375
  63.7 1.8 %collective-permute-start.7 = (f32[4,4096]{1,0:T(4,128)S(1)}, f32[4,4096]{1,0:T(4,128)S(1)}, u32[]{:S(2)}, u32[]{:S(2)}) collective-permute-start(f32[4,4096]{1,0:T(4,128)S(1)} %get-tuple-element.41), channel_id=1, source_target_pairs={{0,32},{16,48},{32,0},{48,16},{1,33},{17,49},{33,1},{49,17},{2,34}... | collective-permute-start | bytes 196616 | tf_op jit(solution)/shard_map/ppermute | solution.py:319
  65.6 1.4 collective-permute-start.8
  67.0 1.2 collective-permute-start.9
  68.4 2.2 %collective-permute-done.8 = f32[4,4096]{1,0:T(4,128)S(1)} collective-permute-done((f32[4,4096]{1,0:T(4,128)S(1)}, f32[4,4096]{1,0:T(4,128)S(1)}, u32[]{:S(2)}, u32[]{:S(2)}) %collective-permute-start.8) | collective-permute-done | bytes 65568 | tf_op jit(solution)/shard_map/ppermute | solution.py:319
  70.7 4.3 %collective-permute-start.10 = (f32[4,4096]{1,0:T(4,128)S(1)}, f32[4,4096]{1,0:T(4,128)S(1)}, u32[]{:S(2)}, u32[]{:S(2)}) collective-permute-start(f32[4,4096]{1,0:T(4,128)S(1)} %add_add_fusion.2), channel_id=1, source_target_pairs={{0,128},{64,192},{128,0},{192,64},{1,129},{65,193},{129,1},{193,65... | collective-permute-start | bytes 196616 | tf_op jit(solution)/shard_map/ppermute | solution.py:319
  74.9 7.0 %collective-permute-start.11 = (f32[4,4096]{1,0:T(4,128)S(1)}, f32[4,4096]{1,0:T(4,128)S(1)}, u32[]{:S(2)}, u32[]{:S(2)}) collective-permute-start(f32[4,4096]{1,0:T(4,128)S(1)} %add_add_fusion.2), channel_id=1, source_target_pairs={{0,64},{64,128},{128,192},{192,0},{1,65},{65,129},{129,193},{193,1... | collective-permute-start | bytes 196616 | tf_op jit(solution)/shard_map/ppermute | solution.py:319
  81.9 1.7 %collective-permute-done.11 = f32[4,4096]{1,0:T(4,128)S(1)} collective-permute-done((f32[4,4096]{1,0:T(4,128)S(1)}, f32[4,4096]{1,0:T(4,128)S(1)}, u32[]{:S(2)}, u32[]{:S(2)}) %collective-permute-start.11) | collective-permute-done | bytes 65568 | tf_op jit(solution)/shard_map/ppermute | solution.py:319
  83.6 2.5 %collective-permute-done.12 = f32[4,4096]{1,0:T(4,128)S(1)} collective-permute-done((f32[4,4096]{1,0:T(4,128)S(1)}, f32[4,4096]{1,0:T(4,128)S(1)}, u32[]{:S(2)}, u32[]{:S(2)}) %collective-permute-start.12) | collective-permute-done | bytes 65568 | tf_op jit(solution)/shard_map/ppermute | solution.py:319
  86.2 0.7 fusion.3
  86.8 3.5 %collective-permute-done.13 = f32[4,4480]{1,0:T(4,128)} collective-permute-done((f32[4,4480]{1,0:T(4,128)}, f32[4,4480]{1,0:T(4,128)}, u32[]{:S(2)}, u32[]{:S(2)}) %collective-permute-start.13) | collective-permute-done | bytes 71712 | tf_op jit(solution)/shard_map/ppermute | solution.py:327
  90.3 1.0 maximum_select_fusion.1
  91.4 0.4 collective-permute-start.14
  91.8 1.8 %collective-permute-start.15 = (f32[8,4480]{1,0:T(8,128)S(1)}, f32[8,4480]{1,0:T(8,128)S(1)}, u32[]{:S(2)}, u32[]{:S(2)}) collective-permute-start(f32[8,4480]{1,0:T(8,128)S(1)} %maximum_select_fusion.1), channel_id=1, source_target_pairs={{0,4},{2,6},{4,0},{6,2},{1,5},{3,7},{5,1},{7,3},{8,12},{10,14},{12... | collective-permute-start | bytes 430088 | tf_op jit(solution)/shard_map/ppermute | solution.py:319
  93.6 0.7 collective-permute-start.16
  94.3 1.0 maximum_select_fusion
  95.4 2.8 %collective-permute-done.14 = f32[8,4480]{1,0:T(8,128)S(1)} collective-permute-done((f32[8,4480]{1,0:T(8,128)S(1)}, f32[8,4480]{1,0:T(8,128)S(1)}, u32[]{:S(2)}, u32[]{:S(2)}) %collective-permute-start.14) | collective-permute-done | bytes 143392 | tf_op jit(solution)/shard_map/ppermute | solution.py:319
  98.1 0.6 collective-permute-done.16
  98.8 5.9 %collective-permute-start.17 = (f32[4,8,4480]{2,1,0:T(8,128)S(1)}, f32[4,8,4480]{2,1,0:T(8,128)S(1)}, u32[]{:S(2)}, u32[]{:S(2)}) collective-permute-start(f32[4,8,4480]{2,1,0:T(8,128)S(1)} %pad_maximum_fusion.mine), channel_id=1, source_target_pairs={{0,1},{1,0},{2,3},{3,2},{4,5},{5,4},{6,7},{7,6},{8,9},{9,8},{10,11... | collective-permute-start | bytes 1720328 | tf_op jit(solution)/shard_map/ppermute | solution.py:327
  104.7 1.6 %collective-permute-done.17.theirs = f32[4,8,4480]{2,1,0:T(8,128)S(1)} collective-permute-done((f32[4,8,4480]{2,1,0:T(8,128)S(1)}, f32[4,8,4480]{2,1,0:T(8,128)S(1)}, u32[]{:S(2)}, u32[]{:S(2)}) %collective-permute-start.17) | collective-permute-done | bytes 573472 | tf_op jit(solution)/shard_map/ppermute | solution.py:327
  106.3 4.9 %shard_map.128 = (f32[1,1]{1,0:T(1,128)}, f32[128,256]{1,0:T(8,128)}, bf16[256,384]{1,0:T(8,128)(2,1)S(1)}, f32[128,128]{1,0:T(8,128)S(1)}, f32[128,128]{1,0:T(8,128)S(1)}) custom-call(bf16[128,4096]{1,0:T(8,128)(2,1)S(1)} %copy-done.8, f32[4,8,4480]{2,1,0:T(8,128)S(1)} %pad_maximum_fusion.mine, f32[4,8,4480]{2,1,0:T(8,128)S(1)} %collective-permute-done.17.theirs, ...), custom_call_target="tpu_custom_call" | custom-call | flops 1000000000 | bytes 4000000 | tf_op jit(solution)/shard_map/pallas_call | solution.py:399
  111.6 0.9 collective-permute-done.18
  112.5 0.8 shard_map.133
  113.3 0.4 collective-permute-start.30
  113.9 3.5 %collective-permute-done.19 = f32[128,128]{1,0:T(8,128)S(1)} collective-permute-done((f32[128,128]{1,0:T(8,128)S(1)}, f32[128,128]{1,0:T(8,128)S(1)}, u32[]{:S(2)}, u32[]{:S(2)}) %collective-permute-start.19) | collective-permute-done | bytes 65568 | tf_op jit(solution)/shard_map/ppermute | solution.py:327
  117.7 0.8 shard_map.132.mine
  118.4 3.3 %collective-permute-start.21 = (f32[128,128]{1,0:T(8,128)S(1)}, f32[128,128]{1,0:T(8,128)S(1)}, u32[]{:S(2)}, u32[]{:S(2)}) collective-permute-start(f32[128,128]{1,0:T(8,128)S(1)} %add.82.own), channel_id=1, source_target_pairs={{0,4},{2,6},{4,0},{6,2},{1,5},{3,7},{5,1},{7,3},{8,12},{10,14},{12... | collective-permute-start | bytes 196616 | tf_op jit(solution)/shard_map/ppermute | solution.py:319
  122.2 1.4 collective-permute-start.31
  123.6 0.8 collective-permute-start.32
  124.4 1.7 %collective-permute-start.33 = (bf16[2,256,384]{2,1,0:T(8,128)(2,1)S(1)}, bf16[2,256,384]{2,1,0:T(8,128)(2,1)S(1)}, u32[]{:S(2)}, u32[]{:S(2)}) collective-permute-start(bf16[2,256,384]{2,1,0:T(8,128)(2,1)S(1)} %get-tuple-element.63), channel_id=1, source_target_pairs={{0,6},{2,0},{4,2},{6,4},{1,7},{3,1},{5,3},{7,5},{8,14},{10,8},{12,... | collective-permute-start | bytes 1179656 | tf_op jit(solution)/shard_map/ppermute | solution.py:319
  126.1 0.8 shard_map.129
  127.0 3.4 %collective-permute-start.24 = (bf16[32,2048]{1,0:T(8,128)(2,1)S(1)}, bf16[32,2048]{1,0:T(8,128)(2,1)S(1)}, u32[]{:S(2)}, u32[]{:S(2)}) collective-permute-start(bf16[32,2048]{1,0:T(8,128)(2,1)S(1)} %get-tuple-element.51), channel_id=1, source_target_pairs={{0,32},{16,48},{32,0},{48,16},{1,33},{17,49},{33,1},{49,17},{2,34}... | collective-permute-start | bytes 393224 | tf_op jit(solution)/shard_map/ppermute | solution.py:319
  130.4 1.9 %collective-permute-done.23.one = bf16[32,2048]{1,0:T(8,128)(2,1)S(1)} collective-permute-done((bf16[32,2048]{1,0:T(8,128)(2,1)S(1)}, bf16[32,2048]{1,0:T(8,128)(2,1)S(1)}, u32[]{:S(2)}, u32[]{:S(2)}) %collective-permute-start.23) | collective-permute-done | bytes 131104 | tf_op jit(solution)/shard_map/ppermute | solution.py:319
  132.3 1.0 collective-permute-start.25
  133.3 0.9 collective-permute-done.24.two
  134.2 3.3 %collective-permute-done.25.three = bf16[32,2048]{1,0:T(8,128)(2,1)S(1)} collective-permute-done((bf16[32,2048]{1,0:T(8,128)(2,1)S(1)}, bf16[32,2048]{1,0:T(8,128)(2,1)S(1)}, u32[]{:S(2)}, u32[]{:S(2)}) %collective-permute-start.25) | collective-permute-done | bytes 131104 | tf_op jit(solution)/shard_map/ppermute | solution.py:319
  137.6 2.3 %collective-permute-start.26 = (f32[8,2048]{1,0:T(8,128)S(1)}, f32[8,2048]{1,0:T(8,128)S(1)}, u32[]{:S(2)}, u32[]{:S(2)}) collective-permute-start(f32[8,2048]{1,0:T(8,128)S(1)} %get-tuple-element.54), channel_id=1, source_target_pairs={{0,128},{64,192},{128,0},{192,64},{1,129},{65,193},{129,1},{193,65... | collective-permute-start | bytes 196616 | tf_op jit(solution)/shard_map/ppermute | solution.py:319
  139.9 1.4 collective-permute-start.27
  141.3 2.2 %collective-permute-start.28 = (f32[8,2048]{1,0:T(8,128)S(1)}, f32[8,2048]{1,0:T(8,128)S(1)}, u32[]{:S(2)}, u32[]{:S(2)}) collective-permute-start(f32[8,2048]{1,0:T(8,128)S(1)} %get-tuple-element.56), channel_id=1, source_target_pairs={{0,192},{64,0},{128,64},{192,128},{1,193},{65,1},{129,65},{193,129... | collective-permute-start | bytes 196616 | tf_op jit(solution)/shard_map/ppermute | solution.py:319
  143.8 1.5 collective-permute-start.34
  145.3 0.9 collective-permute-done.27
  146.3 6.4 %collective-permute-start.29 = (f32[8,2048]{1,0:T(8,128)S(1)}, f32[8,2048]{1,0:T(8,128)S(1)}, u32[]{:S(2)}, u32[]{:S(2)}) collective-permute-start(f32[8,2048]{1,0:T(8,128)S(1)} %add_add_fusion.mine), channel_id=1, source_target_pairs={{0,1},{1,0},{2,3},{3,2},{4,5},{5,4},{6,7},{7,6},{8,9},{9,8},{10,11... | collective-permute-start | bytes 196616 | tf_op jit(solution)/shard_map/ppermute | solution.py:327
  152.8 0.9 collective-permute-done.29.theirs
  153.7 0.8 shard_map.131
  154.5 0.9 shard_map.136
  (71 shorter events, 3.3 us)
Async XLA Ops:
  0.6 29.9 %copy-start.9 = (f32[4096]{0:T(1024)S(1)}, f32[4096]{0:T(1024)}, u32[]{:S(2)}) copy-start(f32[4096]{0:T(1024)} %param.10) | copy-start | bytes 49156
  0.6 29.8 %copy-start.1 = (bf16[4096,128]{1,0:T(8,128)(2,1)S(1)}, bf16[4096,128]{1,0:T(8,128)(2,1)}, u32[]{:S(2)}) copy-start(bf16[4096,128]{1,0:T(8,128)(2,1)} %wv.3) | copy-start | bytes 3145732
  0.7 30.1 %copy-start = (bf16[4096,128]{1,0:T(8,128)(2,1)S(1)}, bf16[4096,128]{1,0:T(8,128)(2,1)}, u32[]{:S(2)}) copy-start(bf16[4096,128]{1,0:T(8,128)(2,1)} %wk.3) | copy-start | bytes 3145732
  2.6 18.4 %collective-permute-start.1 = (bf16[272,256]{1,0:T(8,128)(2,1)S(1)}, bf16[272,256]{1,0:T(8,128)(2,1)S(1)}, u32[]{:S(2)}, u32[]{:S(2)}) collective-permute-start(bf16[272,256]{1,0:T(8,128)(2,1)S(1)} %get-tuple-element.73), channel_id=1, source_target_pairs={{0,64},{64,128},{128,192},{192,0},{1,65},{65,129},{129,193},{193,1... | collective-permute-start | bytes 417800 | tf_op jit(solution)/shard_map/ppermute | solution.py:319
  6.5 14.5 %collective-permute-start.2 = (bf16[272,256]{1,0:T(8,128)(2,1)S(1)}, bf16[272,256]{1,0:T(8,128)(2,1)S(1)}, u32[]{:S(2)}, u32[]{:S(2)}) collective-permute-start(bf16[272,256]{1,0:T(8,128)(2,1)S(1)} %get-tuple-element.73), channel_id=1, source_target_pairs={{0,128},{64,192},{128,0},{192,64},{1,129},{65,193},{129,1},{193,65... | collective-permute-start | bytes 417800 | tf_op jit(solution)/shard_map/ppermute | solution.py:319
  11.6 13.6 %collective-permute-start.3 = (bf16[272,256]{1,0:T(8,128)(2,1)S(1)}, bf16[272,256]{1,0:T(8,128)(2,1)S(1)}, u32[]{:S(2)}, u32[]{:S(2)}) collective-permute-start(bf16[272,256]{1,0:T(8,128)(2,1)S(1)} %get-tuple-element.73), channel_id=1, source_target_pairs={{0,192},{64,0},{128,64},{192,128},{1,193},{65,1},{129,65},{193,129... | collective-permute-start | bytes 417800 | tf_op jit(solution)/shard_map/ppermute | solution.py:319
  14.0 7.0 %collective-permute-start = (bf16[8,4096]{1,0:T(8,128)(2,1)}, bf16[8,4096]{1,0:T(8,128)(2,1)S(1)}, u32[]{:S(2)}, u32[]{:S(2)}) collective-permute-start(bf16[8,4096]{1,0:T(8,128)(2,1)} %context.1), channel_id=1, source_target_pairs={{0,0},{1,16},{2,32},{3,48},{4,64},{5,80},{6,96},{7,112},{8,128},{9... | collective-permute-start | bytes 196616 | tf_op jit(solution)/shard_map/ppermute | solution.py:366
  25.3 28.3 %copy-start.4 = (bf16[4,272,256]{2,1,0:T(8,128)(2,1)}, bf16[4,272,256]{2,1,0:T(8,128)(2,1)S(1)}, u32[]{:S(2)}) copy-start(bf16[4,272,256]{2,1,0:T(8,128)(2,1)S(1)} %pad_maximum_fusion.1.z0) | copy-start | bytes 1671172
  25.3 16.1 %copy-start.13 = (s32[4]{0:T(128)S(1)}, s32[4]{0:T(128)}, u32[]{:S(2)}) copy-start(s32[4]{0:T(128)} %param.15) | copy-start | bytes 52
  25.3 21.9 %collective-permute-start.4 = (bf16[4,272,256]{2,1,0:T(8,128)(2,1)S(1)}, bf16[4,272,256]{2,1,0:T(8,128)(2,1)}, u32[]{:S(2)}, u32[]{:S(2)}) collective-permute-start(bf16[4,272,256]{2,1,0:T(8,128)(2,1)S(1)} %pad_maximum_fusion.1.z0), channel_id=1, source_target_pairs={{0,16},{16,32},{32,48},{48,0},{1,17},{17,33},{33,49},{49,1},{2,18}... | collective-permute-start | bytes 1671176 | tf_op jit(solution)/shard_map/ppermute | solution.py:319
  26.6 27.0 %collective-permute-start.5 = (bf16[4,272,256]{2,1,0:T(8,128)(2,1)S(1)}, bf16[4,272,256]{2,1,0:T(8,128)(2,1)}, u32[]{:S(2)}, u32[]{:S(2)}) collective-permute-start(bf16[4,272,256]{2,1,0:T(8,128)(2,1)S(1)} %pad_maximum_fusion.1.z0), channel_id=1, source_target_pairs={{0,32},{16,48},{32,0},{48,16},{1,33},{17,49},{33,1},{49,17},{2,34}... | collective-permute-start | bytes 1671176 | tf_op jit(solution)/shard_map/ppermute | solution.py:319
  29.1 24.5 %collective-permute-start.6 = (bf16[4,272,256]{2,1,0:T(8,128)(2,1)S(1)}, bf16[4,272,256]{2,1,0:T(8,128)(2,1)}, u32[]{:S(2)}, u32[]{:S(2)}) collective-permute-start(bf16[4,272,256]{2,1,0:T(8,128)(2,1)S(1)} %pad_maximum_fusion.1.z0), channel_id=1, source_target_pairs={{0,48},{16,0},{32,16},{48,32},{1,49},{17,1},{33,17},{49,33},{2,50}... | collective-permute-start | bytes 1671176 | tf_op jit(solution)/shard_map/ppermute | solution.py:319
  31.9 15.4 %all-to-all-start = ((bf16[16,8,384]{2,1,0:T(8,128)(2,1)}), bf16[16,8,384]{2,1,0:T(8,128)(2,1)S(1)}, u32[]{:S(2)}, u32[]{:S(2)}) async-start(bf16[16,8,384]{2,1,0:T(8,128)(2,1)} %broadcast_in_dim.16), calls=%async_computation | async-start | bytes 196608 | tf_op jit(solution)/shard_map/all_to_all | solution.py:351
  53.6 1.2 copy-start.2
  54.8 1.1 copy-start.5
  55.9 1.2 copy-start.6
  57.1 1.2 copy-start.7
  63.7 22.4 %copy-start.11 = (f32[128,256]{1,0:T(8,128)}, f32[128,256]{1,0:T(8,128)S(1)}, u32[]{:S(2)}) copy-start(f32[128,256]{1,0:T(8,128)S(1)} %get-tuple-element.66.ctx_columns) | copy-start | bytes 393220
  63.7 4.7 %collective-permute-start.7 = (f32[4,4096]{1,0:T(4,128)S(1)}, f32[4,4096]{1,0:T(4,128)S(1)}, u32[]{:S(2)}, u32[]{:S(2)}) collective-permute-start(f32[4,4096]{1,0:T(4,128)S(1)} %get-tuple-element.41), channel_id=1, source_target_pairs={{0,32},{16,48},{32,0},{48,16},{1,33},{17,49},{33,1},{49,17},{2,34}... | collective-permute-start | bytes 196616 | tf_op jit(solution)/shard_map/ppermute | solution.py:319
  65.6 5.0 %collective-permute-start.8 = (f32[4,4096]{1,0:T(4,128)S(1)}, f32[4,4096]{1,0:T(4,128)S(1)}, u32[]{:S(2)}, u32[]{:S(2)}) collective-permute-start(f32[4,4096]{1,0:T(4,128)S(1)} %get-tuple-element.41), channel_id=1, source_target_pairs={{0,16},{16,32},{32,48},{48,0},{1,17},{17,33},{33,49},{49,1},{2,18}... | collective-permute-start | bytes 196616 | tf_op jit(solution)/shard_map/ppermute | solution.py:319
  67.0 3.6 %collective-permute-start.9 = (f32[4,4096]{1,0:T(4,128)S(1)}, f32[4,4096]{1,0:T(4,128)S(1)}, u32[]{:S(2)}, u32[]{:S(2)}) collective-permute-start(f32[4,4096]{1,0:T(4,128)S(1)} %get-tuple-element.41), channel_id=1, source_target_pairs={{0,48},{16,0},{32,16},{48,32},{1,49},{17,1},{33,17},{49,33},{2,50}... | collective-permute-start | bytes 196616 | tf_op jit(solution)/shard_map/ppermute | solution.py:319
  70.7 11.3 %collective-permute-start.10 = (f32[4,4096]{1,0:T(4,128)S(1)}, f32[4,4096]{1,0:T(4,128)S(1)}, u32[]{:S(2)}, u32[]{:S(2)}) collective-permute-start(f32[4,4096]{1,0:T(4,128)S(1)} %add_add_fusion.2), channel_id=1, source_target_pairs={{0,128},{64,192},{128,0},{192,64},{1,129},{65,193},{129,1},{193,65... | collective-permute-start | bytes 196616 | tf_op jit(solution)/shard_map/ppermute | solution.py:319
  74.9 8.7 %collective-permute-start.11 = (f32[4,4096]{1,0:T(4,128)S(1)}, f32[4,4096]{1,0:T(4,128)S(1)}, u32[]{:S(2)}, u32[]{:S(2)}) collective-permute-start(f32[4,4096]{1,0:T(4,128)S(1)} %add_add_fusion.2), channel_id=1, source_target_pairs={{0,64},{64,128},{128,192},{192,0},{1,65},{65,129},{129,193},{193,1... | collective-permute-start | bytes 196616 | tf_op jit(solution)/shard_map/ppermute | solution.py:319
  81.9 4.2 %collective-permute-start.12 = (f32[4,4096]{1,0:T(4,128)S(1)}, f32[4,4096]{1,0:T(4,128)S(1)}, u32[]{:S(2)}, u32[]{:S(2)}) collective-permute-start(f32[4,4096]{1,0:T(4,128)S(1)} %add_add_fusion.2), channel_id=1, source_target_pairs={{0,192},{64,0},{128,64},{192,128},{1,193},{65,1},{129,65},{193,129... | collective-permute-start | bytes 196616 | tf_op jit(solution)/shard_map/ppermute | solution.py:319
  86.8 3.5 %collective-permute-start.13 = (f32[4,4480]{1,0:T(4,128)}, f32[4,4480]{1,0:T(4,128)}, u32[]{:S(2)}, u32[]{:S(2)}) collective-permute-start(f32[4,4480]{1,0:T(4,128)} %get-tuple-element.75), channel_id=1, source_target_pairs={{0,8},{8,0},{1,9},{9,1},{2,10},{10,2},{3,11},{11,3},{4,12},{12,4},... | collective-permute-start | bytes 215048 | tf_op jit(solution)/shard_map/ppermute | solution.py:327
  86.8 19.5 %copy-start.8 = (bf16[128,4096]{1,0:T(8,128)(2,1)S(1)}, bf16[128,4096]{1,0:T(8,128)(2,1)}, u32[]{:S(2)}) copy-start(bf16[128,4096]{1,0:T(8,128)(2,1)} %wo.3) | copy-start | bytes 3145732
  91.4 6.8 %collective-permute-start.14 = (f32[8,4480]{1,0:T(8,128)S(1)}, f32[8,4480]{1,0:T(8,128)S(1)}, u32[]{:S(2)}, u32[]{:S(2)}) collective-permute-start(f32[8,4480]{1,0:T(8,128)S(1)} %maximum_select_fusion.1), channel_id=1, source_target_pairs={{0,2},{2,4},{4,6},{6,0},{1,3},{3,5},{5,7},{7,1},{8,10},{10,12},{12... | collective-permute-start | bytes 430088 | tf_op jit(solution)/shard_map/ppermute | solution.py:319
  91.8 6.3 %collective-permute-start.15 = (f32[8,4480]{1,0:T(8,128)S(1)}, f32[8,4480]{1,0:T(8,128)S(1)}, u32[]{:S(2)}, u32[]{:S(2)}) collective-permute-start(f32[8,4480]{1,0:T(8,128)S(1)} %maximum_select_fusion.1), channel_id=1, source_target_pairs={{0,4},{2,6},{4,0},{6,2},{1,5},{3,7},{5,1},{7,3},{8,12},{10,14},{12... | collective-permute-start | bytes 430088 | tf_op jit(solution)/shard_map/ppermute | solution.py:319
  93.6 5.1 %collective-permute-start.16 = (f32[8,4480]{1,0:T(8,128)S(1)}, f32[8,4480]{1,0:T(8,128)S(1)}, u32[]{:S(2)}, u32[]{:S(2)}) collective-permute-start(f32[8,4480]{1,0:T(8,128)S(1)} %maximum_select_fusion.1), channel_id=1, source_target_pairs={{0,6},{2,0},{4,2},{6,4},{1,7},{3,1},{5,3},{7,5},{8,14},{10,8},{12,... | collective-permute-start | bytes 430088 | tf_op jit(solution)/shard_map/ppermute | solution.py:319
  98.8 7.5 %collective-permute-start.17 = (f32[4,8,4480]{2,1,0:T(8,128)S(1)}, f32[4,8,4480]{2,1,0:T(8,128)S(1)}, u32[]{:S(2)}, u32[]{:S(2)}) collective-permute-start(f32[4,8,4480]{2,1,0:T(8,128)S(1)} %pad_maximum_fusion.mine), channel_id=1, source_target_pairs={{0,1},{1,0},{2,3},{3,2},{4,5},{5,4},{6,7},{7,6},{8,9},{9,8},{10,11... | collective-permute-start | bytes 1720328 | tf_op jit(solution)/shard_map/ppermute | solution.py:327
  111.3 1.3 collective-permute-start.18
  113.3 8.5 %collective-permute-start.30 = (bf16[8,256,384]{2,1,0:T(8,128)(2,1)S(1)}, bf16[8,256,384]{2,1,0:T(8,128)(2,1)S(1)}, u32[]{:S(2)}, u32[]{:S(2)}) collective-permute-start(bf16[8,256,384]{2,1,0:T(8,128)(2,1)S(1)} %shard_map.133), channel_id=1, source_target_pairs={{0,1},{1,0},{2,3},{3,2},{4,5},{5,4},{6,7},{7,6},{8,9},{9,8},{10,11... | collective-permute-start | bytes 4718600 | tf_op jit(solution)/shard_map/ppermute | solution.py:327
  113.8 3.6 %collective-permute-start.19 = (f32[128,128]{1,0:T(8,128)S(1)}, f32[128,128]{1,0:T(8,128)S(1)}, u32[]{:S(2)}, u32[]{:S(2)}) collective-permute-start(f32[128,128]{1,0:T(8,128)S(1)} %add.81), channel_id=1, source_target_pairs={{0,8},{8,0},{1,9},{9,1},{2,10},{10,2},{3,11},{11,3},{4,12},{12,4},... | collective-permute-start | bytes 196616 | tf_op jit(solution)/shard_map/ppermute | solution.py:327
  117.4 4.4 %collective-permute-start.20 = (f32[128,128]{1,0:T(8,128)S(1)}, f32[128,128]{1,0:T(8,128)S(1)}, u32[]{:S(2)}, u32[]{:S(2)}) collective-permute-start(f32[128,128]{1,0:T(8,128)S(1)} %add.82.own), channel_id=1, source_target_pairs={{0,2},{2,4},{4,6},{6,0},{1,3},{3,5},{5,7},{7,1},{8,10},{10,12},{12... | collective-permute-start | bytes 196616 | tf_op jit(solution)/shard_map/ppermute | solution.py:319
  118.4 7.7 %copy-start.3 = (bf16[4096,128]{1,0:T(8,128)(2,1)S(1)}, bf16[4096,128]{1,0:T(8,128)(2,1)}, u32[]{:S(2)}) copy-start(bf16[4096,128]{1,0:T(8,128)(2,1)} %wv.3) | copy-start | bytes 3145732
  118.4 7.7 %collective-permute-start.21 = (f32[128,128]{1,0:T(8,128)S(1)}, f32[128,128]{1,0:T(8,128)S(1)}, u32[]{:S(2)}, u32[]{:S(2)}) collective-permute-start(f32[128,128]{1,0:T(8,128)S(1)} %add.82.own), channel_id=1, source_target_pairs={{0,4},{2,6},{4,0},{6,2},{1,5},{3,7},{5,1},{7,3},{8,12},{10,14},{12... | collective-permute-start | bytes 196616 | tf_op jit(solution)/shard_map/ppermute | solution.py:319
  121.7 4.4 %collective-permute-start.22 = (f32[128,128]{1,0:T(8,128)S(1)}, f32[128,128]{1,0:T(8,128)S(1)}, u32[]{:S(2)}, u32[]{:S(2)}) collective-permute-start(f32[128,128]{1,0:T(8,128)S(1)} %add.82.own), channel_id=1, source_target_pairs={{0,6},{2,0},{4,2},{6,4},{1,7},{3,1},{5,3},{7,5},{8,14},{10,8},{12,... | collective-permute-start | bytes 196616 | tf_op jit(solution)/shard_map/ppermute | solution.py:319
  122.2 19.1 %collective-permute-start.31 = (bf16[2,256,384]{2,1,0:T(8,128)(2,1)S(1)}, bf16[2,256,384]{2,1,0:T(8,128)(2,1)S(1)}, u32[]{:S(2)}, u32[]{:S(2)}) collective-permute-start(bf16[2,256,384]{2,1,0:T(8,128)(2,1)S(1)} %get-tuple-element.61), channel_id=1, source_target_pairs={{0,2},{2,4},{4,6},{6,0},{1,3},{3,5},{5,7},{7,1},{8,10},{10,12},{12... | collective-permute-start | bytes 1179656 | tf_op jit(solution)/shard_map/ppermute | solution.py:319
  123.6 19.9 %collective-permute-start.32 = (bf16[2,256,384]{2,1,0:T(8,128)(2,1)S(1)}, bf16[2,256,384]{2,1,0:T(8,128)(2,1)S(1)}, u32[]{:S(2)}, u32[]{:S(2)}) collective-permute-start(bf16[2,256,384]{2,1,0:T(8,128)(2,1)S(1)} %get-tuple-element.62), channel_id=1, source_target_pairs={{0,4},{2,6},{4,0},{6,2},{1,5},{3,7},{5,1},{7,3},{8,12},{10,14},{12... | collective-permute-start | bytes 1179656 | tf_op jit(solution)/shard_map/ppermute | solution.py:319
  124.4 19.1 %collective-permute-start.33 = (bf16[2,256,384]{2,1,0:T(8,128)(2,1)S(1)}, bf16[2,256,384]{2,1,0:T(8,128)(2,1)S(1)}, u32[]{:S(2)}, u32[]{:S(2)}) collective-permute-start(bf16[2,256,384]{2,1,0:T(8,128)(2,1)S(1)} %get-tuple-element.63), channel_id=1, source_target_pairs={{0,6},{2,0},{4,2},{6,4},{1,7},{3,1},{5,3},{7,5},{8,14},{10,8},{12,... | collective-permute-start | bytes 1179656 | tf_op jit(solution)/shard_map/ppermute | solution.py:319
  126.9 5.4 %collective-permute-start.23 = (bf16[32,2048]{1,0:T(8,128)(2,1)S(1)}, bf16[32,2048]{1,0:T(8,128)(2,1)S(1)}, u32[]{:S(2)}, u32[]{:S(2)}) collective-permute-start(bf16[32,2048]{1,0:T(8,128)(2,1)S(1)} %get-tuple-element.50), channel_id=1, source_target_pairs={{0,16},{16,32},{32,48},{48,0},{1,17},{17,33},{33,49},{49,1},{2,18}... | collective-permute-start | bytes 393224 | tf_op jit(solution)/shard_map/ppermute | solution.py:319
  127.0 7.2 %collective-permute-start.24 = (bf16[32,2048]{1,0:T(8,128)(2,1)S(1)}, bf16[32,2048]{1,0:T(8,128)(2,1)S(1)}, u32[]{:S(2)}, u32[]{:S(2)}) collective-permute-start(bf16[32,2048]{1,0:T(8,128)(2,1)S(1)} %get-tuple-element.51), channel_id=1, source_target_pairs={{0,32},{16,48},{32,0},{48,16},{1,33},{17,49},{33,1},{49,17},{2,34}... | collective-permute-start | bytes 393224 | tf_op jit(solution)/shard_map/ppermute | solution.py:319
  132.3 5.2 %collective-permute-start.25 = (bf16[32,2048]{1,0:T(8,128)(2,1)S(1)}, bf16[32,2048]{1,0:T(8,128)(2,1)S(1)}, u32[]{:S(2)}, u32[]{:S(2)}) collective-permute-start(bf16[32,2048]{1,0:T(8,128)(2,1)S(1)} %get-tuple-element.52), channel_id=1, source_target_pairs={{0,48},{16,0},{32,16},{48,32},{1,49},{17,1},{33,17},{49,33},{2,50}... | collective-permute-start | bytes 393224 | tf_op jit(solution)/shard_map/ppermute | solution.py:319
  137.6 7.8 %collective-permute-start.26 = (f32[8,2048]{1,0:T(8,128)S(1)}, f32[8,2048]{1,0:T(8,128)S(1)}, u32[]{:S(2)}, u32[]{:S(2)}) collective-permute-start(f32[8,2048]{1,0:T(8,128)S(1)} %get-tuple-element.54), channel_id=1, source_target_pairs={{0,128},{64,192},{128,0},{192,64},{1,129},{65,193},{129,1},{193,65... | collective-permute-start | bytes 196616 | tf_op jit(solution)/shard_map/ppermute | solution.py:319
  139.9 6.4 %collective-permute-start.27 = (f32[8,2048]{1,0:T(8,128)S(1)}, f32[8,2048]{1,0:T(8,128)S(1)}, u32[]{:S(2)}, u32[]{:S(2)}) collective-permute-start(f32[8,2048]{1,0:T(8,128)S(1)} %get-tuple-element.55), channel_id=1, source_target_pairs={{0,64},{64,128},{128,192},{192,0},{1,65},{65,129},{129,193},{193,1... | collective-permute-start | bytes 196616 | tf_op jit(solution)/shard_map/ppermute | solution.py:319
  141.3 5.0 %collective-permute-start.28 = (f32[8,2048]{1,0:T(8,128)S(1)}, f32[8,2048]{1,0:T(8,128)S(1)}, u32[]{:S(2)}, u32[]{:S(2)}) collective-permute-start(f32[8,2048]{1,0:T(8,128)S(1)} %get-tuple-element.56), channel_id=1, source_target_pairs={{0,192},{64,0},{128,64},{192,128},{1,193},{65,1},{129,65},{193,129... | collective-permute-start | bytes 196616 | tf_op jit(solution)/shard_map/ppermute | solution.py:319
  143.5 10.2 %copy-start.10 = (bf16[8,4096]{1,0:T(8,128)(2,1)S(1)}, bf16[8,4096]{1,0:T(8,128)(2,1)}, u32[]{:S(2)}) copy-start(bf16[8,4096]{1,0:T(8,128)(2,1)} %context.1) | copy-start | bytes 196612
  143.8 10.7 %collective-permute-start.34 = (bf16[256,384]{1,0:T(8,128)(2,1)S(1)}, bf16[256,384]{1,0:T(8,128)(2,1)S(1)}, u32[]{:S(2)}, u32[]{:S(2)}) collective-permute-start(bf16[256,384]{1,0:T(8,128)(2,1)S(1)} %get-tuple-element.65), channel_id=1, source_target_pairs={{0,8},{8,0},{1,9},{9,1},{2,10},{10,2},{3,11},{11,3},{4,12},{12,4},... | collective-permute-start | bytes 589832 | tf_op jit(solution)/shard_map/ppermute | solution.py:327
  146.3 8.2 %copy-start.12 = (f32[128,256]{1,0:T(8,128)S(1)}, f32[128,256]{1,0:T(8,128)}, u32[]{:S(2)}) copy-start(f32[128,256]{1,0:T(8,128)} %copy-done.11) | copy-start | bytes 393220
  146.3 7.3 %collective-permute-start.29 = (f32[8,2048]{1,0:T(8,128)S(1)}, f32[8,2048]{1,0:T(8,128)S(1)}, u32[]{:S(2)}, u32[]{:S(2)}) collective-permute-start(f32[8,2048]{1,0:T(8,128)S(1)} %add_add_fusion.mine), channel_id=1, source_target_pairs={{0,1},{1,0},{2,3},{3,2},{4,5},{5,4},{6,7},{7,6},{8,9},{9,8},{10,11... | collective-permute-start | bytes 196616 | tf_op jit(solution)/shard_map/ppermute | solution.py:327
where the time goes:
time: 156 us; the launch traced here: 155 us
  starting transfers between devices  81.7 us (52%)
  waiting for transfers between devices  46.3 us (30%)
  Pallas kernels  15.1 us (10%)
  local copies, waits for them, and re-layouts  6.64 us (4%)
  other arithmetic  4.14 us (3%)
    ppermute x27, starting transfers between devices, shift(): return lax.ppermute(a, axis, [(i, (i + k) % 4) for i in range(4)])  52.9 us
    ppermute x27, waiting for transfers between devices, shift(): return lax.ppermute(a, axis, [(i, (i + k) % 4) for i in range(4)])  27.7 us
    ppermute x7, starting transfers between devices, other(): return lax.ppermute(a, axis, [(0, 1), (1, 0)])  14.8 us
    ppermute x7, waiting for transfers between devices, other(): return lax.ppermute(a, axis, [(0, 1), (1, 0)])  10.4 us
    all_to_all x1, starting transfers between devices, spread(): return lax.all_to_all(copies, axis, 0, 0)  9.54 us
    all_to_all x1, waiting for transfers between devices, spread(): return lax.all_to_all(copies, axis, 0, 0)  5.76 us
    pallas_call x1, Pallas kernels, shards(): call(forward_kernel, (shape(tok, 3 * HD, dtype=bf16), shape(docs, width),...  5.37 us
    pallas_call x1, Pallas kernels, shards(): call(loss_kernel, (shape(1, 1), shape(HD, feat), shape(tok, 3 * HD, dtype...  4.94 us
  transfers between devices with their start and end apart: 36, of which 20 were waited for; matrix products, arithmetic and copies ran while one was open for 2% of the time, Pallas kernels for 2%

commit v1 on v0

--- a/solution.py
+++ b/solution.py
@@ -88,9 +88,8 @@
 
 
 def call(kernel, out_shape, in_specs, scratch=(), vmem=16, flops=10**9):
-    in_specs = [
-        pl.BlockSpec(memory_space=pl.ANY if s == "a" else pltpu.VMEM) for s in in_specs
-    ]
+    spaces = {"a": pl.ANY, "h": pltpu.HBM, "v": pltpu.VMEM}
+    in_specs = [pl.BlockSpec(memory_space=spaces[s]) for s in in_specs]
     return pl.pallas_call(
         kernel,
         out_shape=out_shape,
@@ -106,23 +105,26 @@
     return jax.ShapeDtypeStruct(dims, dtype)
 
 
-def forward_kernel(gain, partners, wq, wk, wv, wo, ctx, z0, z1, z2, z3, *refs):
-    qkv, own, branch, mix, normed, ctx_columns, weights, last, sems = refs
-    pos = position()
-    fetch = [
-        pltpu.make_async_copy(w, weights.at[:, pl.ds(i * HD, HD)], sems.at[i])
-        for i, w in enumerate((wq, wk, wv))
-    ]
-    fetch.append(pltpu.make_async_copy(wo, last, sems.at[3]))
+def forward_kernel(gain, partners, ctx, wq, wk, wv, wo, *refs):
+    pieces, refs = refs[:8], refs[8:]
+    qkv, own, branch, mix, normed, ctx_columns, weights, last, blocks, sems = refs
+    pos = position()
+    tok, feat = qkv.shape[0], blocks.shape[2]
+    fetch = []
+    for i, (near, far) in enumerate(zip(pieces[:4], pieces[4:])):
+        fetch.append((near, blocks.at[4 * i]))
+        fetch.append((far, blocks.at[pl.ds(4 * i + 1, 3)]))
+    fetch += [(w, weights.at[:, pl.ds(i * HD, HD)]) for i, w in enumerate((wq, wk, wv))]
+    fetch.append((wo, last))
+    fetch = [pltpu.make_async_copy(a, b, sems.at[i]) for i, (a, b) in enumerate(fetch)]
     for copy in fetch:
         copy.start()
-    tok, feat = qkv.shape[0], z0.shape[2]
-    blocks = []
-    for along_x, ref in enumerate((z0, z1, z2, z3)):
-        blocks += [(ref, i, along_x, i) for i in range(4)]
-        for i in range(4):
-            place = ((pos[0] - i) & 3) * 4 + ((pos[1] - along_x) & 3)
-            ctx_columns[pl.ds(pl.multiple_of(place * 8, 8), 8), :] = wide(ref[i, tok:, :])[:8]
+    for copy in fetch[:8]:
+        copy.wait()
+    places = [((pos[0] - i % 4) & 3) * 4 + ((pos[1] - i // 4) & 3) for i in range(16)]
+    for i, place in enumerate(places):
+        here = pl.ds(pl.multiple_of(place * 8, 8), 8)
+        ctx_columns[here, :] = wide(blocks[i, tok:, :])[:8]
     ctx_inv = jnp.sum(wide(ctx[:, 2 * HD :]), axis=1, keepdims=True)
     dp = (pos[2] * 4 + pos[3]) * 2 + pos[4]
     here = pl.ds(pl.multiple_of(dp * feat, feat), feat)
@@ -131,17 +133,16 @@
     averaging = jnp.where(iota((8, tok), 0) == iota((8, tok), 1) // DOC_LEN, 1 / DOC_LEN, 0.0)
     averaging = averaging.astype(bf16)
     squares = jnp.zeros((tok, 1), f32)
-    for ref, i, _, _ in blocks:
-        rows = wide(ref[i, :tok, :])
+    for i in range(16):
+        rows = wide(blocks[i, :tok, :])
         squares = squares + jnp.sum(rows * rows, axis=1, keepdims=True)
     inv = lax.rsqrt(squares / (16 * feat) + EPS)
     total = jnp.zeros((tok, 3 * HD), f32)
-    for copy in fetch[:3]:
+    for copy in fetch[8:11]:
         copy.wait()
-    for ref, i, along_x, along_z in blocks:
-        place = ((pos[0] - along_z) & 3) * 4 + ((pos[1] - along_x) & 3)
+    for i, place in enumerate(places):
         here = pl.ds(pl.multiple_of(place * feat, feat), feat)
-        rows = ref[i, :tok, :]
+        rows = blocks[i, :tok, :]
         ready = (wide(rows) * inv * gain[:, here]).astype(bf16)
         normed[:, here] = ready
         total = total + dot(ready, weights[here, :])
@@ -156,7 +157,7 @@
     mix[:, :HD] = mean[:docs]
     mix[:, HD : 2 * HD] = dot(averaging, ctx_weights)[:docs] * DOC_LEN
     mix[:, 2 * HD :] = jnp.broadcast_to(wide(partners[...]), (docs, HD))
-    fetch[3].wait()
+    fetch[11].wait()
     branch[...] = folded(dot(stacked_pieces(mean, 3), last[...]), 3)[:docs]
 
 
@@ -359,12 +360,12 @@
 
     ctx_part = lax.dynamic_slice_in_dim(context, lax.axis_index(DP) * feat, feat, 1)
     block = jnp.concatenate([doc_states, ctx_part, jnp.zeros_like(ctx_part)], axis=0)
-    block = jnp.stack([block] + others(block, "zh"))
-    rows = [block] + others(block, "x")
+    from_zh = jnp.stack(others(block, "zh"))
+    rows = [block] + others(block, "x") + [from_zh] + others(from_zh, "x")
 
     swap = [(c * 16 + d, d * 16 + c) for c in range(16) for d in range(16)]
     named_rows = wide(lax.ppermute(context, EVERY, swap))
-    named_rows, _ = lax.optimization_barrier((named_rows, block))
+    named_rows, _ = lax.optimization_barrier((named_rows, from_zh))
     inv = inverse_rms(named_rows)
     named_rows = (named_rows * inv * gain).astype(bf16)
     few = [dot(named_rows, w_key), dot(named_rows, w_value)] + hlo_split(inv, 3)
@@ -382,18 +383,21 @@
             shape(tok, width, dtype=bf16),
             shape(HD, feat),
         ),
-        ["v"] * 2 + ["a"] * 4 + ["v"] * 5,
+        ["v"] * 3 + ["h"] * 4 + ["a"] * 8,
         scratch=[
             pltpu.VMEM((width, 3 * HD), bf16),
             pltpu.VMEM((HD, width), bf16),
-            pltpu.SemaphoreType.DMA((4,)),
+            pltpu.VMEM((16,) + block.shape, bf16),
+            pltpu.SemaphoreType.DMA((12,)),
         ],
         vmem=24,
-    )(gain_row, partners[:, None], w_query, w_key, w_value, w_out, ctx_kv, *rows)
-
-    pooled = own_mean + ring_sum(ring_sum(branch, "x"), "zh")
-    message = jnp.concatenate([pooled, mix], axis=1)
-    message = pair(message, "zl")
+    )(gain_row, partners[:, None], ctx_kv, w_query, w_key, w_value, w_out, *rows)
+
+    branch = ring_sum(branch, "x") + own_mean / 4
+    message = spread(jnp.concatenate([branch, mix], axis=1), ("zh", "zl"), 8)
+    message = message.reshape(4, 2 * docs, -1)
+    mix = lax.dynamic_index_in_dim(message[:, :, width:], lax.axis_index("zh"), 0, keepdims=False)
+    message = jnp.concatenate([jnp.sum(message[:, :, :width], axis=0), mix], axis=1)
     messages = jnp.stack([message] + others(message, "y"))
     total = 64
     loss, grad_out, grads, grad_ctx_keys, grad_ctx_values = call(

time: 156 us -> 170 us (1.090)
  waiting for transfers between devices: 46.3 us -> 57.3 us
  local copies, waits for them, and re-layouts: 6.64 us -> 16.2 us
  starting transfers between devices: 81.7 us -> 76.1 us
    all_to_all x1 -> x2, waiting for transfers between devices: 5.76 us -> 17 us  [spread(): return lax.all_to_all(copies, axis, 0, 0)]
    ppermute x27, starting transfers between devices: 52.9 us -> 42.2 us  [shift(): return lax.ppermute(a, axis, [(i, (i + k) % 4) for i in range(4)])]
    all_to_all x1 -> x2, starting transfers between devices: 9.54 us -> 20.2 us  [spread(): return lax.all_to_all(copies, axis, 0, 0)]
    unnamed x28 -> x44, local copies, waits for them, and re-layouts: 4.78 us -> 10.5 us
    ppermute x7 -> x6, starting transfers between devices: 14.8 us -> 9.17 us  [other(): return lax.ppermute(a, axis, [(0, 1), (1, 0)])]
    ppermute x7 -> x6, waiting for transfers between devices: 10.4 us -> 6.68 us  [other(): return lax.ppermute(a, axis, [(0, 1), (1, 0)])]
    ppermute x27, waiting for transfers between devices: 27.7 us -> 31.3 us  [shift(): return lax.ppermute(a, axis, [(i, (i + k) % 4) for i in range(4)])]
    reshape x0 -> x1, local copies, waits for them, and re-layouts: none -> 2.08 us  [shards(): message = message.reshape(4, 2 * docs, -1)]
  transfers between devices with their start and end apart: 36 -> 36, of which waited for: 20 -> 20; matrix products, arithmetic and copies ran while one was open for 2% -> 1% of each run, Pallas kernels for 2% -> 2%
where the time goes in v1:
time: 170 us
  starting transfers between devices  76.1 us (45%)
  waiting for transfers between devices  57.3 us (34%)
  local copies, waits for them, and re-layouts  16.2 us (10%)
  Pallas kernels  15.3 us (9%)
  other arithmetic  2.55 us (1%)
    ppermute x27, starting transfers between devices, shift(): return lax.ppermute(a, axis, [(i, (i + k) % 4) for i in range(4)])  42.2 us
    ppermute x27, waiting for transfers between devices, shift(): return lax.ppermute(a, axis, [(i, (i + k) % 4) for i in range(4)])  31.3 us
    all_to_all x2, starting transfers between devices, spread(): return lax.all_to_all(copies, axis, 0, 0)  20.2 us
    all_to_all x2, waiting for transfers between devices, spread(): return lax.all_to_all(copies, axis, 0, 0)  17 us
    unnamed x44, local copies, waits for them, and re-layouts  10.5 us
    ppermute x6, starting transfers between devices, other(): return lax.ppermute(a, axis, [(0, 1), (1, 0)])  9.17 us
    ppermute x6, waiting for transfers between devices, other(): return lax.ppermute(a, axis, [(0, 1), (1, 0)])  6.68 us
    pallas_call x1, Pallas kernels, shards(): call(forward_kernel, (shape(tok, 3 * HD, dtype=bf16), shape(docs, width),...  5.6 us
  transfers between devices with their start and end apart: 36, of which 20 were waited for; matrix products, arithmetic and copies ran while one was open for 1% of the time, Pallas kernels for 2%

profile of v1, /device:TPU:1, one launch (start us, length us, event | category | flops | bytes accessed | tf_op | source)
XLA Modules:
  0.0 169.7 jit_solution(655627279780310225)
XLA Ops:
  0.7 0.8 constant_dynamic-slice_fusion
  1.6 1.0 maximum_maximum_fusion.refs_0_
  2.6 3.9 %collective-permute-start.1 = (bf16[272,256]{1,0:T(8,128)(2,1)S(1)}, bf16[272,256]{1,0:T(8,128)(2,1)S(1)}, u32[]{:S(2)}, u32[]{:S(2)}) collective-permute-start(bf16[272,256]{1,0:T(8,128)(2,1)S(1)} %maximum_maximum_fusion.refs_0_), channel_id=1, source_target_pairs={{0,64},{64,128},{128,192},{192,0},{1,65},{65,129},{129,193},{193,1... | collective-permute-start | bytes 417800 | tf_op jit(solution)/shard_map/ppermute | solution.py:320
  6.5 5.1 %collective-permute-start.2 = (bf16[272,256]{1,0:T(8,128)(2,1)S(1)}, bf16[272,256]{1,0:T(8,128)(2,1)S(1)}, u32[]{:S(2)}, u32[]{:S(2)}) collective-permute-start(bf16[272,256]{1,0:T(8,128)(2,1)S(1)} %maximum_maximum_fusion.refs_0_), channel_id=1, source_target_pairs={{0,128},{64,192},{128,0},{192,64},{1,129},{65,193},{129,1},{193,65... | collective-permute-start | bytes 417800 | tf_op jit(solution)/shard_map/ppermute | solution.py:320
  11.6 2.4 %collective-permute-start.3 = (bf16[272,256]{1,0:T(8,128)(2,1)S(1)}, bf16[272,256]{1,0:T(8,128)(2,1)S(1)}, u32[]{:S(2)}, u32[]{:S(2)}) collective-permute-start(bf16[272,256]{1,0:T(8,128)(2,1)S(1)} %maximum_maximum_fusion.refs_0_), channel_id=1, source_target_pairs={{0,192},{64,0},{128,64},{192,128},{1,193},{65,1},{129,65},{193,129... | collective-permute-start | bytes 417800 | tf_op jit(solution)/shard_map/ppermute | solution.py:320
  14.0 4.5 %collective-permute-start = (bf16[8,4096]{1,0:T(8,128)(2,1)}, bf16[8,4096]{1,0:T(8,128)(2,1)S(1)}, u32[]{:S(2)}, u32[]{:S(2)}) collective-permute-start(bf16[8,4096]{1,0:T(8,128)(2,1)} %context.1), channel_id=1, source_target_pairs={{0,0},{1,16},{2,32},{3,48},{4,64},{5,80},{6,96},{7,112},{8,128},{9... | collective-permute-start | bytes 196616 | tf_op jit(solution)/shard_map/ppermute | solution.py:367
  18.6 2.3 %collective-permute-done = bf16[8,4096]{1,0:T(8,128)(2,1)S(1)} collective-permute-done((bf16[8,4096]{1,0:T(8,128)(2,1)}, bf16[8,4096]{1,0:T(8,128)(2,1)S(1)}, u32[]{:S(2)}, u32[]{:S(2)}) %collective-permute-start) | collective-permute-done | bytes 65568 | tf_op jit(solution)/shard_map/ppermute | solution.py:367
  21.0 4.3 %collective-permute-done.3 = bf16[272,256]{1,0:T(8,128)(2,1)S(1)} collective-permute-done((bf16[272,256]{1,0:T(8,128)(2,1)S(1)}, bf16[272,256]{1,0:T(8,128)(2,1)S(1)}, u32[]{:S(2)}, u32[]{:S(2)}) %collective-permute-start.3) | collective-permute-done | bytes 139296 | tf_op jit(solution)/shard_map/ppermute | solution.py:320
  25.3 1.3 collective-permute-start.7
  26.6 2.5 %collective-permute-start.8 = (bf16[3,272,256]{2,1,0:T(8,128)(2,1)S(1)}, bf16[3,272,256]{2,1,0:T(8,128)(2,1)}, u32[]{:S(2)}, u32[]{:S(2)}) collective-permute-start(bf16[3,272,256]{2,1,0:T(8,128)(2,1)S(1)} %pad_maximum_fusion.1.refs_4_), channel_id=1, source_target_pairs={{0,32},{16,48},{32,0},{48,16},{1,33},{17,49},{33,1},{49,17},{2,34}... | collective-permute-start | bytes 1253384 | tf_op jit(solution)/shard_map/ppermute | solution.py:320
  29.1 1.2 collective-permute-start.9
  30.4 1.0 convolution_convert_fusion
  32.6 9.5 %all-to-all-start = ((bf16[16,8,384]{2,1,0:T(8,128)(2,1)}), bf16[16,8,384]{2,1,0:T(8,128)(2,1)S(1)}, u32[]{:S(2)}, u32[]{:S(2)}) async-start(bf16[16,8,384]{2,1,0:T(8,128)(2,1)} %broadcast_in_dim.10), calls=%async_computation | async-start | bytes 196608 | tf_op jit(solution)/shard_map/all_to_all | solution.py:352
  42.1 1.6 collective-permute-start.5
  43.7 0.9 collective-permute-start.6
  44.7 5.8 %collective-permute-done.5.refs_2_ = bf16[272,256]{1,0:T(8,128)(2,1)S(1)} collective-permute-done((bf16[272,256]{1,0:T(8,128)(2,1)S(1)}, bf16[272,256]{1,0:T(8,128)(2,1)S(1)}, u32[]{:S(2)}, u32[]{:S(2)}) %collective-permute-start.5) | collective-permute-done | bytes 139296 | tf_op jit(solution)/shard_map/ppermute | solution.py:320
  51.1 1.5 collective-permute-done.6.refs_3_
  54.1 1.2 copy-done.2
  55.3 1.0 copy-done.5
  56.3 1.2 copy-done.6
  57.6 1.2 copy-done.7
  58.8 1.0 copy-done.10
  59.8 0.9 copy-done.13
  60.7 0.9 copy-done.15
  61.6 5.6 %shard_map.127 = (bf16[256,384]{1,0:T(8,128)(2,1)S(1)}, f32[4,4096]{1,0:T(4,128)S(1)}, f32[4,4096]{1,0:T(4,128)S(1)}, f32[4,384]{1,0:T(4,128)S(1)}, bf16[256,409...) custom-call(f32[1,4096]{1,0:T(1,128)S(1)} %bitcast.20, s32[4,1]{1,0:T(4,128)S(1)} %copy.16.partners, ...), custom_call_target="tpu_custom_call" | custom-call | flops 1000000000 | bytes 4000000 | tf_op jit(solution)/shard_map/pallas_call | solution.py:376
  67.2 2.6 %collective-permute-start.10 = (f32[4,4096]{1,0:T(4,128)S(1)}, f32[4,4096]{1,0:T(4,128)S(1)}, u32[]{:S(2)}, u32[]{:S(2)}) collective-permute-start(f32[4,4096]{1,0:T(4,128)S(1)} %get-tuple-element.40), channel_id=1, source_target_pairs={{0,32},{16,48},{32,0},{48,16},{1,33},{17,49},{33,1},{49,17},{2,34}... | collective-permute-start | bytes 196616 | tf_op jit(solution)/shard_map/ppermute | solution.py:320
  69.9 1.4 collective-permute-start.11
  71.3 1.2 collective-permute-start.12
  72.5 2.1 %collective-permute-done.11 = f32[4,4096]{1,0:T(4,128)S(1)} collective-permute-done((f32[4,4096]{1,0:T(4,128)S(1)}, f32[4,4096]{1,0:T(4,128)S(1)}, u32[]{:S(2)}, u32[]{:S(2)}) %collective-permute-start.11) | collective-permute-done | bytes 65568 | tf_op jit(solution)/shard_map/ppermute | solution.py:320
  74.7 0.9 broadcast_in_dim.11
  75.6 10.6 %all-to-all-start.1 = ((f32[8,4,4480]{2,1,0:T(4,128)}), f32[8,4,4480]{2,1,0:T(4,128)}, u32[]{:S(2)}, u32[]{:S(2)}) async-start(f32[8,4,4480]{2,1,0:T(4,128)} %broadcast_in_dim.11), calls=%async_computation.1 | async-start | bytes 1146880 | tf_op jit(solution)/shard_map/all_to_all | solution.py:352
  86.3 17.0 %all-to-all-done.1 = f32[8,4,4480]{2,1,0:T(4,128)} async-done(((f32[8,4,4480]{2,1,0:T(4,128)}), f32[8,4,4480]{2,1,0:T(4,128)}, u32[]{:S(2)}, u32[]{:S(2)}) %all-to-all-start.1) | async-done | bytes 573472 | tf_op jit(solution)/shard_map/all_to_all | solution.py:352
  103.2 2.1 %reshape.92 = f32[4,8,4480]{2,1,0:T(8,128)} reshape(f32[8,4,4480]{2,1,0:T(4,128)} %all-to-all-done.1) | data formatting | bytes 1146880 | tf_op jit(solution)/shard_map/reshape | solution.py:398
  105.3 1.2 slice_reduce_fusion
  106.5 0.8 slice.9
  107.4 2.1 %collective-permute-start.15 = (f32[8,4480]{1,0:T(8,128)S(1)}, f32[8,4480]{1,0:T(8,128)S(1)}, u32[]{:S(2)}, u32[]{:S(2)}) collective-permute-start(f32[8,4480]{1,0:T(8,128)S(1)} %get-tuple-element.73), channel_id=1, source_target_pairs={{0,6},{2,0},{4,2},{6,4},{1,7},{3,1},{5,3},{7,5},{8,14},{10,8},{12,... | collective-permute-start | bytes 430088 | tf_op jit(solution)/shard_map/ppermute | solution.py:320
  109.6 3.3 %collective-permute-done.14 = f32[8,4480]{1,0:T(8,128)S(1)} collective-permute-done((f32[8,4480]{1,0:T(8,128)S(1)}, f32[8,4480]{1,0:T(8,128)S(1)}, u32[]{:S(2)}, u32[]{:S(2)}) %collective-permute-start.14) | collective-permute-done | bytes 143392 | tf_op jit(solution)/shard_map/ppermute | solution.py:320
  113.4 2.9 %collective-permute-done.13 = f32[8,4480]{1,0:T(8,128)S(1)} collective-permute-done((f32[8,4480]{1,0:T(8,128)S(1)}, f32[8,4480]{1,0:T(8,128)S(1)}, u32[]{:S(2)}, u32[]{:S(2)}) %collective-permute-start.13) | collective-permute-done | bytes 143392 | tf_op jit(solution)/shard_map/ppermute | solution.py:320
  116.3 3.1 %collective-permute-start.16 = (f32[4,8,4480]{2,1,0:T(8,128)S(1)}, f32[4,8,4480]{2,1,0:T(8,128)S(1)}, u32[]{:S(2)}, u32[]{:S(2)}) collective-permute-start(f32[4,8,4480]{2,1,0:T(8,128)S(1)} %pad_maximum_fusion.mine), channel_id=1, source_target_pairs={{0,1},{1,0},{2,3},{3,2},{4,5},{5,4},{6,7},{7,6},{8,9},{9,8},{10,11... | collective-permute-start | bytes 1720328 | tf_op jit(solution)/shard_map/ppermute | solution.py:328
  119.5 1.6 collective-permute-done.16.theirs
  121.1 0.9 copy-done.18
  122.0 4.9 %shard_map.128 = (f32[1,1]{1,0:T(1,128)}, f32[128,256]{1,0:T(8,128)}, bf16[256,384]{1,0:T(8,128)(2,1)S(1)}, f32[128,128]{1,0:T(8,128)S(1)}, f32[128,128]{1,0:T(8,128)S(1)}) custom-call(bf16[128,4096]{1,0:T(8,128)(2,1)S(1)} %copy-done.8, f32[4,8,4480]{2,1,0:T(8,128)S(1)} %pad_maximum_fusion.mine, f32[4,8,4480]{2,1,0:T(8,128)S(1)} %collective-permute-done.16.theirs, ...), custom_call_target="tpu_custom_call" | custom-call | flops 1000000000 | bytes 4000000 | tf_op jit(solution)/shard_map/pallas_call | solution.py:403
  127.3 0.9 collective-permute-done.17
  128.2 0.8 shard_map.133
  129.8 3.3 %collective-permute-done.18 = f32[128,128]{1,0:T(8,128)S(1)} collective-permute-done((f32[128,128]{1,0:T(8,128)S(1)}, f32[128,128]{1,0:T(8,128)S(1)}, u32[]{:S(2)}, u32[]{:S(2)}) %collective-permute-start.18) | collective-permute-done | bytes 65568 | tf_op jit(solution)/shard_map/ppermute | solution.py:328
  134.0 1.5 collective-permute-start.20
  135.4 1.6 collective-permute-start.21
  138.0 1.7 collective-permute-start.31
  139.6 2.0 %collective-permute-start.32 = (bf16[2,256,384]{2,1,0:T(8,128)(2,1)S(1)}, bf16[2,256,384]{2,1,0:T(8,128)(2,1)S(1)}, u32[]{:S(2)}, u32[]{:S(2)}) collective-permute-start(bf16[2,256,384]{2,1,0:T(8,128)(2,1)S(1)} %get-tuple-element.63), channel_id=1, source_target_pairs={{0,6},{2,0},{4,2},{6,4},{1,7},{3,1},{5,3},{7,5},{8,14},{10,8},{12,... | collective-permute-start | bytes 1179656 | tf_op jit(solution)/shard_map/ppermute | solution.py:320
  141.6 0.8 shard_map.129
  142.4 1.8 %collective-permute-start.22 = (bf16[32,2048]{1,0:T(8,128)(2,1)S(1)}, bf16[32,2048]{1,0:T(8,128)(2,1)S(1)}, u32[]{:S(2)}, u32[]{:S(2)}) collective-permute-start(bf16[32,2048]{1,0:T(8,128)(2,1)S(1)} %get-tuple-element.50), channel_id=1, source_target_pairs={{0,16},{16,32},{32,48},{48,0},{1,17},{17,33},{33,49},{49,1},{2,18}... | collective-permute-start | bytes 393224 | tf_op jit(solution)/shard_map/ppermute | solution.py:320
  144.1 1.9 %collective-permute-start.23 = (bf16[32,2048]{1,0:T(8,128)(2,1)S(1)}, bf16[32,2048]{1,0:T(8,128)(2,1)S(1)}, u32[]{:S(2)}, u32[]{:S(2)}) collective-permute-start(bf16[32,2048]{1,0:T(8,128)(2,1)S(1)} %get-tuple-element.51), channel_id=1, source_target_pairs={{0,32},{16,48},{32,0},{48,16},{1,33},{17,49},{33,1},{49,17},{2,34}... | collective-permute-start | bytes 393224 | tf_op jit(solution)/shard_map/ppermute | solution.py:320
  146.0 1.8 %collective-permute-done.22.one = bf16[32,2048]{1,0:T(8,128)(2,1)S(1)} collective-permute-done((bf16[32,2048]{1,0:T(8,128)(2,1)S(1)}, bf16[32,2048]{1,0:T(8,128)(2,1)S(1)}, u32[]{:S(2)}, u32[]{:S(2)}) %collective-permute-start.22) | collective-permute-done | bytes 131104 | tf_op jit(solution)/shard_map/ppermute | solution.py:320
  147.8 1.2 collective-permute-start.24
  149.0 0.9 collective-permute-done.23.two
  149.8 3.3 %collective-permute-done.24.three = bf16[32,2048]{1,0:T(8,128)(2,1)S(1)} collective-permute-done((bf16[32,2048]{1,0:T(8,128)(2,1)S(1)}, bf16[32,2048]{1,0:T(8,128)(2,1)S(1)}, u32[]{:S(2)}, u32[]{:S(2)}) %collective-permute-start.24) | collective-permute-done | bytes 131104 | tf_op jit(solution)/shard_map/ppermute | solution.py:320
  153.9 1.7 collective-permute-start.26
  155.5 1.9 %collective-permute-start.27 = (f32[8,2048]{1,0:T(8,128)S(1)}, f32[8,2048]{1,0:T(8,128)S(1)}, u32[]{:S(2)}, u32[]{:S(2)}) collective-permute-start(f32[8,2048]{1,0:T(8,128)S(1)} %get-tuple-element.56), channel_id=1, source_target_pairs={{0,192},{64,0},{128,64},{192,128},{1,193},{65,1},{129,65},{193,129... | collective-permute-start | bytes 196616 | tf_op jit(solution)/shard_map/ppermute | solution.py:320
  158.8 1.9 %collective-permute-done.25 = f32[8,2048]{1,0:T(8,128)S(1)} collective-permute-done((f32[8,2048]{1,0:T(8,128)S(1)}, f32[8,2048]{1,0:T(8,128)S(1)}, u32[]{:S(2)}, u32[]{:S(2)}) %collective-permute-start.25) | collective-permute-done | bytes 65568 | tf_op jit(solution)/shard_map/ppermute | solution.py:320
  160.7 1.8 %collective-permute-done.27 = f32[8,2048]{1,0:T(8,128)S(1)} collective-permute-done((f32[8,2048]{1,0:T(8,128)S(1)}, f32[8,2048]{1,0:T(8,128)S(1)}, u32[]{:S(2)}, u32[]{:S(2)}) %collective-permute-start.27) | collective-permute-done | bytes 65568 | tf_op jit(solution)/shard_map/ppermute | solution.py:320
  162.6 4.5 %collective-permute-start.28 = (f32[8,2048]{1,0:T(8,128)S(1)}, f32[8,2048]{1,0:T(8,128)S(1)}, u32[]{:S(2)}, u32[]{:S(2)}) collective-permute-start(f32[8,2048]{1,0:T(8,128)S(1)} %add_add_fusion.mine), channel_id=1, source_target_pairs={{0,1},{1,0},{2,3},{3,2},{4,5},{5,4},{6,7},{7,6},{8,9},{9,8},{10,11... | collective-permute-start | bytes 196616 | tf_op jit(solution)/shard_map/ppermute | solution.py:328
  167.1 0.9 collective-permute-done.28.theirs
  168.0 0.8 shard_map.131
  168.8 0.9 shard_map.136
  (90 shorter events, 9.6 us)
Async XLA Ops:
  0.6 30.8 %copy-start.11 = (f32[4096]{0:T(1024)S(1)}, f32[4096]{0:T(1024)}, u32[]{:S(2)}) copy-start(f32[4096]{0:T(1024)} %param.10) | copy-start | bytes 49156
  0.6 29.7 %copy-start.1 = (bf16[4096,128]{1,0:T(8,128)(2,1)S(1)}, bf16[4096,128]{1,0:T(8,128)(2,1)}, u32[]{:S(2)}) copy-start(bf16[4096,128]{1,0:T(8,128)(2,1)} %wv.3) | copy-start | bytes 3145732
  0.7 30.8 %copy-start = (bf16[4096,128]{1,0:T(8,128)(2,1)S(1)}, bf16[4096,128]{1,0:T(8,128)(2,1)}, u32[]{:S(2)}) copy-start(bf16[4096,128]{1,0:T(8,128)(2,1)} %wk.3) | copy-start | bytes 3145732
  2.6 18.4 %collective-permute-start.1 = (bf16[272,256]{1,0:T(8,128)(2,1)S(1)}, bf16[272,256]{1,0:T(8,128)(2,1)S(1)}, u32[]{:S(2)}, u32[]{:S(2)}) collective-permute-start(bf16[272,256]{1,0:T(8,128)(2,1)S(1)} %maximum_maximum_fusion.refs_0_), channel_id=1, source_target_pairs={{0,64},{64,128},{128,192},{192,0},{1,65},{65,129},{129,193},{193,1... | collective-permute-start | bytes 417800 | tf_op jit(solution)/shard_map/ppermute | solution.py:320
  6.5 14.5 %collective-permute-start.2 = (bf16[272,256]{1,0:T(8,128)(2,1)S(1)}, bf16[272,256]{1,0:T(8,128)(2,1)S(1)}, u32[]{:S(2)}, u32[]{:S(2)}) collective-permute-start(bf16[272,256]{1,0:T(8,128)(2,1)S(1)} %maximum_maximum_fusion.refs_0_), channel_id=1, source_target_pairs={{0,128},{64,192},{128,0},{192,64},{1,129},{65,193},{129,1},{193,65... | collective-permute-start | bytes 417800 | tf_op jit(solution)/shard_map/ppermute | solution.py:320
  11.6 13.6 %collective-permute-start.3 = (bf16[272,256]{1,0:T(8,128)(2,1)S(1)}, bf16[272,256]{1,0:T(8,128)(2,1)S(1)}, u32[]{:S(2)}, u32[]{:S(2)}) collective-permute-start(bf16[272,256]{1,0:T(8,128)(2,1)S(1)} %maximum_maximum_fusion.refs_0_), channel_id=1, source_target_pairs={{0,192},{64,0},{128,64},{192,128},{1,193},{65,1},{129,65},{193,129... | collective-permute-start | bytes 417800 | tf_op jit(solution)/shard_map/ppermute | solution.py:320
  14.0 7.0 %collective-permute-start = (bf16[8,4096]{1,0:T(8,128)(2,1)}, bf16[8,4096]{1,0:T(8,128)(2,1)S(1)}, u32[]{:S(2)}, u32[]{:S(2)}) collective-permute-start(bf16[8,4096]{1,0:T(8,128)(2,1)} %context.1), channel_id=1, source_target_pairs={{0,0},{1,16},{2,32},{3,48},{4,64},{5,80},{6,96},{7,112},{8,128},{9... | collective-permute-start | bytes 196616 | tf_op jit(solution)/shard_map/ppermute | solution.py:367
  18.5 25.2 %collective-permute-start.4 = (bf16[272,256]{1,0:T(8,128)(2,1)S(1)}, bf16[272,256]{1,0:T(8,128)(2,1)S(1)}, u32[]{:S(2)}, u32[]{:S(2)}) collective-permute-start(bf16[272,256]{1,0:T(8,128)(2,1)S(1)} %maximum_maximum_fusion.refs_0_), channel_id=1, source_target_pairs={{0,16},{16,32},{32,48},{48,0},{1,17},{17,33},{33,49},{49,1},{2,18}... | collective-permute-start | bytes 417800 | tf_op jit(solution)/shard_map/ppermute | solution.py:320
  25.3 28.8 %copy-start.4 = (bf16[3,272,256]{2,1,0:T(8,128)(2,1)}, bf16[3,272,256]{2,1,0:T(8,128)(2,1)S(1)}, u32[]{:S(2)}) copy-start(bf16[3,272,256]{2,1,0:T(8,128)(2,1)S(1)} %pad_maximum_fusion.1.refs_4_) | copy-start | bytes 1253380
  25.3 19.3 %copy-start.21 = (s32[4]{0:T(128)S(1)}, s32[4]{0:T(128)}, u32[]{:S(2)}) copy-start(s32[4]{0:T(128)} %param.15) | copy-start | bytes 52
  25.3 28.0 %collective-permute-start.7 = (bf16[3,272,256]{2,1,0:T(8,128)(2,1)S(1)}, bf16[3,272,256]{2,1,0:T(8,128)(2,1)S(1)}, u32[]{:S(2)}, u32[]{:S(2)}) collective-permute-start(bf16[3,272,256]{2,1,0:T(8,128)(2,1)S(1)} %pad_maximum_fusion.1.refs_4_), channel_id=1, source_target_pairs={{0,16},{16,32},{32,48},{48,0},{1,17},{17,33},{33,49},{49,1},{2,18}... | collective-permute-start | bytes 1253384 | tf_op jit(solution)/shard_map/ppermute | solution.py:320
  26.6 27.5 %collective-permute-start.8 = (bf16[3,272,256]{2,1,0:T(8,128)(2,1)S(1)}, bf16[3,272,256]{2,1,0:T(8,128)(2,1)}, u32[]{:S(2)}, u32[]{:S(2)}) collective-permute-start(bf16[3,272,256]{2,1,0:T(8,128)(2,1)S(1)} %pad_maximum_fusion.1.refs_4_), channel_id=1, source_target_pairs={{0,32},{16,48},{32,0},{48,16},{1,33},{17,49},{33,1},{49,17},{2,34}... | collective-permute-start | bytes 1253384 | tf_op jit(solution)/shard_map/ppermute | solution.py:320
  29.1 25.0 %collective-permute-start.9 = (bf16[3,272,256]{2,1,0:T(8,128)(2,1)S(1)}, bf16[3,272,256]{2,1,0:T(8,128)(2,1)}, u32[]{:S(2)}, u32[]{:S(2)}) collective-permute-start(bf16[3,272,256]{2,1,0:T(8,128)(2,1)S(1)} %pad_maximum_fusion.1.refs_4_), channel_id=1, source_target_pairs={{0,48},{16,0},{32,16},{48,32},{1,49},{17,1},{33,17},{49,33},{2,50}... | collective-permute-start | bytes 1253384 | tf_op jit(solution)/shard_map/ppermute | solution.py:320
  32.6 20.7 %all-to-all-start = ((bf16[16,8,384]{2,1,0:T(8,128)(2,1)}), bf16[16,8,384]{2,1,0:T(8,128)(2,1)S(1)}, u32[]{:S(2)}, u32[]{:S(2)}) async-start(bf16[16,8,384]{2,1,0:T(8,128)(2,1)} %broadcast_in_dim.10), calls=%async_computation | async-start | bytes 196608 | tf_op jit(solution)/shard_map/all_to_all | solution.py:352
  42.1 8.4 %collective-permute-start.5 = (bf16[272,256]{1,0:T(8,128)(2,1)S(1)}, bf16[272,256]{1,0:T(8,128)(2,1)S(1)}, u32[]{:S(2)}, u32[]{:S(2)}) collective-permute-start(bf16[272,256]{1,0:T(8,128)(2,1)S(1)} %maximum_maximum_fusion.refs_0_), channel_id=1, source_target_pairs={{0,32},{16,48},{32,0},{48,16},{1,33},{17,49},{33,1},{49,17},{2,34}... | collective-permute-start | bytes 417800 | tf_op jit(solution)/shard_map/ppermute | solution.py:320
  43.7 9.0 %collective-permute-start.6 = (bf16[272,256]{1,0:T(8,128)(2,1)S(1)}, bf16[272,256]{1,0:T(8,128)(2,1)S(1)}, u32[]{:S(2)}, u32[]{:S(2)}) collective-permute-start(bf16[272,256]{1,0:T(8,128)(2,1)S(1)} %maximum_maximum_fusion.refs_0_), channel_id=1, source_target_pairs={{0,48},{16,0},{32,16},{48,32},{1,49},{17,1},{33,17},{49,33},{2,50}... | collective-permute-start | bytes 417800 | tf_op jit(solution)/shard_map/ppermute | solution.py:320
  50.5 0.6 copy-start.12
  52.7 0.7 copy-start.14
  53.3 0.8 copy-start.9
  54.1 1.2 copy-start.2
  55.3 1.0 copy-start.5
  56.3 1.2 copy-start.6
  57.6 1.2 copy-start.7
  58.8 1.0 copy-start.10
  59.8 0.9 copy-start.13
  60.7 0.9 copy-start.15
  67.2 7.5 %copy-start.17 = (bf16[256,384]{1,0:T(8,128)(2,1)}, bf16[256,384]{1,0:T(8,128)(2,1)S(1)}, u32[]{:S(2)}) copy-start(bf16[256,384]{1,0:T(8,128)(2,1)S(1)} %get-tuple-element.43.own) | copy-start | bytes 589828
  67.2 7.5 %copy-start.19 = (f32[128,256]{1,0:T(8,128)}, f32[128,256]{1,0:T(8,128)S(1)}, u32[]{:S(2)}) copy-start(f32[128,256]{1,0:T(8,128)S(1)} %get-tuple-element.66.ctx_columns) | copy-start | bytes 393220
  67.2 5.3 %collective-permute-start.10 = (f32[4,4096]{1,0:T(4,128)S(1)}, f32[4,4096]{1,0:T(4,128)S(1)}, u32[]{:S(2)}, u32[]{:S(2)}) collective-permute-start(f32[4,4096]{1,0:T(4,128)S(1)} %get-tuple-element.40), channel_id=1, source_target_pairs={{0,32},{16,48},{32,0},{48,16},{1,33},{17,49},{33,1},{49,17},{2,34}... | collective-permute-start | bytes 196616 | tf_op jit(solution)/shard_map/ppermute | solution.py:320
  69.9 4.8 %collective-permute-start.11 = (f32[4,4096]{1,0:T(4,128)S(1)}, f32[4,4096]{1,0:T(4,128)S(1)}, u32[]{:S(2)}, u32[]{:S(2)}) collective-permute-start(f32[4,4096]{1,0:T(4,128)S(1)} %get-tuple-element.40), channel_id=1, source_target_pairs={{0,16},{16,32},{32,48},{48,0},{1,17},{17,33},{33,49},{49,1},{2,18}... | collective-permute-start | bytes 196616 | tf_op jit(solution)/shard_map/ppermute | solution.py:320
  71.3 3.4 %collective-permute-start.12 = (f32[4,4096]{1,0:T(4,128)S(1)}, f32[4,4096]{1,0:T(4,128)S(1)}, u32[]{:S(2)}, u32[]{:S(2)}) collective-permute-start(f32[4,4096]{1,0:T(4,128)S(1)} %get-tuple-element.40), channel_id=1, source_target_pairs={{0,48},{16,0},{32,16},{48,32},{1,49},{17,1},{33,17},{49,33},{2,50}... | collective-permute-start | bytes 196616 | tf_op jit(solution)/shard_map/ppermute | solution.py:320
  75.6 27.6 %all-to-all-start.1 = ((f32[8,4,4480]{2,1,0:T(4,128)}), f32[8,4,4480]{2,1,0:T(4,128)}, u32[]{:S(2)}, u32[]{:S(2)}) async-start(f32[8,4,4480]{2,1,0:T(4,128)} %broadcast_in_dim.11), calls=%async_computation.1 | async-start | bytes 1146880 | tf_op jit(solution)/shard_map/all_to_all | solution.py:352
  105.3 15.8 %copy-start.8 = (bf16[128,4096]{1,0:T(8,128)(2,1)S(1)}, bf16[128,4096]{1,0:T(8,128)(2,1)}, u32[]{:S(2)}) copy-start(bf16[128,4096]{1,0:T(8,128)(2,1)} %wo.3) | copy-start | bytes 3145732
  107.3 5.5 %collective-permute-start.14 = (f32[8,4480]{1,0:T(8,128)S(1)}, f32[8,4480]{1,0:T(8,128)S(1)}, u32[]{:S(2)}, u32[]{:S(2)}) collective-permute-start(f32[8,4480]{1,0:T(8,128)S(1)} %get-tuple-element.73), channel_id=1, source_target_pairs={{0,4},{2,6},{4,0},{6,2},{1,5},{3,7},{5,1},{7,3},{8,12},{10,14},{12... | collective-permute-start | bytes 430088 | tf_op jit(solution)/shard_map/ppermute | solution.py:320
  107.4 5.9 %collective-permute-start.15 = (f32[8,4480]{1,0:T(8,128)S(1)}, f32[8,4480]{1,0:T(8,128)S(1)}, u32[]{:S(2)}, u32[]{:S(2)}) collective-permute-start(f32[8,4480]{1,0:T(8,128)S(1)} %get-tuple-element.73), channel_id=1, source_target_pairs={{0,6},{2,0},{4,2},{6,4},{1,7},{3,1},{5,3},{7,5},{8,14},{10,8},{12,... | collective-permute-start | bytes 430088 | tf_op jit(solution)/shard_map/ppermute | solution.py:320
  109.6 6.8 %collective-permute-start.13 = (f32[8,4480]{1,0:T(8,128)S(1)}, f32[8,4480]{1,0:T(8,128)S(1)}, u32[]{:S(2)}, u32[]{:S(2)}) collective-permute-start(f32[8,4480]{1,0:T(8,128)S(1)} %get-tuple-element.73), channel_id=1, source_target_pairs={{0,2},{2,4},{4,6},{6,0},{1,3},{3,5},{5,7},{7,1},{8,10},{10,12},{12... | collective-permute-start | bytes 430088 | tf_op jit(solution)/shard_map/ppermute | solution.py:320
  116.3 4.7 %collective-permute-start.16 = (f32[4,8,4480]{2,1,0:T(8,128)S(1)}, f32[4,8,4480]{2,1,0:T(8,128)S(1)}, u32[]{:S(2)}, u32[]{:S(2)}) collective-permute-start(f32[4,8,4480]{2,1,0:T(8,128)S(1)} %pad_maximum_fusion.mine), channel_id=1, source_target_pairs={{0,1},{1,0},{2,3},{3,2},{4,5},{5,4},{6,7},{7,6},{8,9},{9,8},{10,11... | collective-permute-start | bytes 1720328 | tf_op jit(solution)/shard_map/ppermute | solution.py:328
  121.1 0.9 copy-start.18
  127.0 1.3 collective-permute-start.17
  129.0 8.5 %collective-permute-start.29 = (bf16[8,256,384]{2,1,0:T(8,128)(2,1)S(1)}, bf16[8,256,384]{2,1,0:T(8,128)(2,1)S(1)}, u32[]{:S(2)}, u32[]{:S(2)}) collective-permute-start(bf16[8,256,384]{2,1,0:T(8,128)(2,1)S(1)} %shard_map.133), channel_id=1, source_target_pairs={{0,1},{1,0},{2,3},{3,2},{4,5},{5,4},{6,7},{7,6},{8,9},{9,8},{10,11... | collective-permute-start | bytes 4718600 | tf_op jit(solution)/shard_map/ppermute | solution.py:328
  129.5 3.6 %collective-permute-start.18 = (f32[128,128]{1,0:T(8,128)S(1)}, f32[128,128]{1,0:T(8,128)S(1)}, u32[]{:S(2)}, u32[]{:S(2)}) collective-permute-start(f32[128,128]{1,0:T(8,128)S(1)} %add.74), channel_id=1, source_target_pairs={{0,8},{8,0},{1,9},{9,1},{2,10},{10,2},{3,11},{11,3},{4,12},{12,4},... | collective-permute-start | bytes 196616 | tf_op jit(solution)/shard_map/ppermute | solution.py:328
  133.1 4.4 %collective-permute-start.19 = (f32[128,128]{1,0:T(8,128)S(1)}, f32[128,128]{1,0:T(8,128)S(1)}, u32[]{:S(2)}, u32[]{:S(2)}) collective-permute-start(f32[128,128]{1,0:T(8,128)S(1)} %add.75.own), channel_id=1, source_target_pairs={{0,2},{2,4},{4,6},{6,0},{1,3},{3,5},{5,7},{7,1},{8,10},{10,12},{12... | collective-permute-start | bytes 196616 | tf_op jit(solution)/shard_map/ppermute | solution.py:320
  134.0 7.7 %copy-start.3 = (bf16[4096,128]{1,0:T(8,128)(2,1)S(1)}, bf16[4096,128]{1,0:T(8,128)(2,1)}, u32[]{:S(2)}) copy-start(bf16[4096,128]{1,0:T(8,128)(2,1)} %wv.3) | copy-start | bytes 3145732
  134.0 7.6 %collective-permute-start.20 = (f32[128,128]{1,0:T(8,128)S(1)}, f32[128,128]{1,0:T(8,128)S(1)}, u32[]{:S(2)}, u32[]{:S(2)}) collective-permute-start(f32[128,128]{1,0:T(8,128)S(1)} %add.75.own), channel_id=1, source_target_pairs={{0,4},{2,6},{4,0},{6,2},{1,5},{3,7},{5,1},{7,3},{8,12},{10,14},{12... | collective-permute-start | bytes 196616 | tf_op jit(solution)/shard_map/ppermute | solution.py:320
  135.4 6.2 %collective-permute-start.21 = (f32[128,128]{1,0:T(8,128)S(1)}, f32[128,128]{1,0:T(8,128)S(1)}, u32[]{:S(2)}, u32[]{:S(2)}) collective-permute-start(f32[128,128]{1,0:T(8,128)S(1)} %add.75.own), channel_id=1, source_target_pairs={{0,6},{2,0},{4,2},{6,4},{1,7},{3,1},{5,3},{7,5},{8,14},{10,8},{12,... | collective-permute-start | bytes 196616 | tf_op jit(solution)/shard_map/ppermute | solution.py:320
  137.9 17.7 %collective-permute-start.30 = (bf16[2,256,384]{2,1,0:T(8,128)(2,1)S(1)}, bf16[2,256,384]{2,1,0:T(8,128)(2,1)S(1)}, u32[]{:S(2)}, u32[]{:S(2)}) collective-permute-start(bf16[2,256,384]{2,1,0:T(8,128)(2,1)S(1)} %get-tuple-element.61), channel_id=1, source_target_pairs={{0,2},{2,4},{4,6},{6,0},{1,3},{3,5},{5,7},{7,1},{8,10},{10,12},{12... | collective-permute-start | bytes 1179656 | tf_op jit(solution)/shard_map/ppermute | solution.py:320
  138.0 19.5 %collective-permute-start.31 = (bf16[2,256,384]{2,1,0:T(8,128)(2,1)S(1)}, bf16[2,256,384]{2,1,0:T(8,128)(2,1)S(1)}, u32[]{:S(2)}, u32[]{:S(2)}) collective-permute-start(bf16[2,256,384]{2,1,0:T(8,128)(2,1)S(1)} %get-tuple-element.62), channel_id=1, source_target_pairs={{0,4},{2,6},{4,0},{6,2},{1,5},{3,7},{5,1},{7,3},{8,12},{10,14},{12... | collective-permute-start | bytes 1179656 | tf_op jit(solution)/shard_map/ppermute | solution.py:320
  139.6 18.5 %collective-permute-start.32 = (bf16[2,256,384]{2,1,0:T(8,128)(2,1)S(1)}, bf16[2,256,384]{2,1,0:T(8,128)(2,1)S(1)}, u32[]{:S(2)}, u32[]{:S(2)}) collective-permute-start(bf16[2,256,384]{2,1,0:T(8,128)(2,1)S(1)} %get-tuple-element.63), channel_id=1, source_target_pairs={{0,6},{2,0},{4,2},{6,4},{1,7},{3,1},{5,3},{7,5},{8,14},{10,8},{12,... | collective-permute-start | bytes 1179656 | tf_op jit(solution)/shard_map/ppermute | solution.py:320
  142.4 5.4 %collective-permute-start.22 = (bf16[32,2048]{1,0:T(8,128)(2,1)S(1)}, bf16[32,2048]{1,0:T(8,128)(2,1)S(1)}, u32[]{:S(2)}, u32[]{:S(2)}) collective-permute-start(bf16[32,2048]{1,0:T(8,128)(2,1)S(1)} %get-tuple-element.50), channel_id=1, source_target_pairs={{0,16},{16,32},{32,48},{48,0},{1,17},{17,33},{33,49},{49,1},{2,18}... | collective-permute-start | bytes 393224 | tf_op jit(solution)/shard_map/ppermute | solution.py:320
  144.1 5.7 %collective-permute-start.23 = (bf16[32,2048]{1,0:T(8,128)(2,1)S(1)}, bf16[32,2048]{1,0:T(8,128)(2,1)S(1)}, u32[]{:S(2)}, u32[]{:S(2)}) collective-permute-start(bf16[32,2048]{1,0:T(8,128)(2,1)S(1)} %get-tuple-element.51), channel_id=1, source_target_pairs={{0,32},{16,48},{32,0},{48,16},{1,33},{17,49},{33,1},{49,17},{2,34}... | collective-permute-start | bytes 393224 | tf_op jit(solution)/shard_map/ppermute | solution.py:320
  147.8 5.4 %collective-permute-start.24 = (bf16[32,2048]{1,0:T(8,128)(2,1)S(1)}, bf16[32,2048]{1,0:T(8,128)(2,1)S(1)}, u32[]{:S(2)}, u32[]{:S(2)}) collective-permute-start(bf16[32,2048]{1,0:T(8,128)(2,1)S(1)} %get-tuple-element.52), channel_id=1, source_target_pairs={{0,48},{16,0},{32,16},{48,32},{1,49},{17,1},{33,17},{49,33},{2,50}... | collective-permute-start | bytes 393224 | tf_op jit(solution)/shard_map/ppermute | solution.py:320
  153.3 7.4 %collective-permute-start.25 = (f32[8,2048]{1,0:T(8,128)S(1)}, f32[8,2048]{1,0:T(8,128)S(1)}, u32[]{:S(2)}, u32[]{:S(2)}) collective-permute-start(f32[8,2048]{1,0:T(8,128)S(1)} %get-tuple-element.54), channel_id=1, source_target_pairs={{0,128},{64,192},{128,0},{192,64},{1,129},{65,193},{129,1},{193,65... | collective-permute-start | bytes 196616 | tf_op jit(solution)/shard_map/ppermute | solution.py:320
  153.9 6.9 %collective-permute-start.26 = (f32[8,2048]{1,0:T(8,128)S(1)}, f32[8,2048]{1,0:T(8,128)S(1)}, u32[]{:S(2)}, u32[]{:S(2)}) collective-permute-start(f32[8,2048]{1,0:T(8,128)S(1)} %get-tuple-element.55), channel_id=1, source_target_pairs={{0,64},{64,128},{128,192},{192,0},{1,65},{65,129},{129,193},{193,1... | collective-permute-start | bytes 196616 | tf_op jit(solution)/shard_map/ppermute | solution.py:320
  155.5 7.0 %collective-permute-start.27 = (f32[8,2048]{1,0:T(8,128)S(1)}, f32[8,2048]{1,0:T(8,128)S(1)}, u32[]{:S(2)}, u32[]{:S(2)}) collective-permute-start(f32[8,2048]{1,0:T(8,128)S(1)} %get-tuple-element.56), channel_id=1, source_target_pairs={{0,192},{64,0},{128,64},{192,128},{1,193},{65,1},{129,65},{193,129... | collective-permute-start | bytes 196616 | tf_op jit(solution)/shard_map/ppermute | solution.py:320
  158.2 9.8 %copy-start.16 = (bf16[8,4096]{1,0:T(8,128)(2,1)S(1)}, bf16[8,4096]{1,0:T(8,128)(2,1)}, u32[]{:S(2)}) copy-start(bf16[8,4096]{1,0:T(8,128)(2,1)} %context.1) | copy-start | bytes 196612
  158.5 10.3 %collective-permute-start.33 = (bf16[256,384]{1,0:T(8,128)(2,1)S(1)}, bf16[256,384]{1,0:T(8,128)(2,1)S(1)}, u32[]{:S(2)}, u32[]{:S(2)}) collective-permute-start(bf16[256,384]{1,0:T(8,128)(2,1)S(1)} %get-tuple-element.65), channel_id=1, source_target_pairs={{0,8},{8,0},{1,9},{9,1},{2,10},{10,2},{3,11},{11,3},{4,12},{12,4},... | collective-permute-start | bytes 589832 | tf_op jit(solution)/shard_map/ppermute | solution.py:328
  162.6 6.2 %copy-start.20 = (f32[128,256]{1,0:T(8,128)S(1)}, f32[128,256]{1,0:T(8,128)}, u32[]{:S(2)}) copy-start(f32[128,256]{1,0:T(8,128)} %copy-done.19) | copy-start | bytes 393220
  162.6 5.4 %collective-permute-start.28 = (f32[8,2048]{1,0:T(8,128)S(1)}, f32[8,2048]{1,0:T(8,128)S(1)}, u32[]{:S(2)}, u32[]{:S(2)}) collective-permute-start(f32[8,2048]{1,0:T(8,128)S(1)} %add_add_fusion.mine), channel_id=1, source_target_pairs={{0,1},{1,0},{2,3},{3,2},{4,5},{5,4},{6,7},{7,6},{8,9},{9,8},{10,11... | collective-permute-start | bytes 196616 | tf_op jit(solution)/shard_map/ppermute | solution.py:328

commit v2 on v0

--- a/solution.py
+++ b/solution.py
@@ -87,7 +87,7 @@
     return ctx_exps / total, own_exps / total
 
 
-def call(kernel, out_shape, in_specs, scratch=(), vmem=16, flops=10**9):
+def call(kernel, out_shape, in_specs, scratch=(), vmem=16, flops=10**9, accessed=0):
     in_specs = [
         pl.BlockSpec(memory_space=pl.ANY if s == "a" else pltpu.VMEM) for s in in_specs
     ]
@@ -98,7 +98,7 @@
         out_specs=jax.tree.map(lambda _: pl.BlockSpec(memory_space=pltpu.VMEM), out_shape),
         scratch_shapes=scratch,
         compiler_params=pltpu.CompilerParams(vmem_limit_bytes=vmem * 2**20),
-        cost_estimate=pl.CostEstimate(flops=flops, bytes_accessed=4 * 10**6, transcendentals=0),
+        cost_estimate=pl.CostEstimate(flops=flops, bytes_accessed=accessed, transcendentals=0),
     )
 
 
@@ -106,19 +106,35 @@
     return jax.ShapeDtypeStruct(dims, dtype)
 
 
-def forward_kernel(gain, partners, wq, wk, wv, wo, ctx, z0, z1, z2, z3, *refs):
-    qkv, own, branch, mix, normed, ctx_columns, weights, last, sems = refs
+def block_kernel(rows, context, out):
+    pos = position()
+    tok, feat = rows.shape
+    out[:tok, :] = rows[...]
+    here = ((pos[2] * 4 + pos[3]) * 2 + pos[4]) * feat
+    part = wide(context[:, pl.ds(pl.multiple_of(here, feat), feat)])
+    out[tok:, :] = jnp.concatenate([part, jnp.zeros_like(part)], axis=0).astype(bf16)
+
+
+def forward_kernel(gain, partners, wq, wk, wv, wo, ctx, *refs):
+    pieces, refs = refs[:4], refs[4:]
+    qkv, own, branch, mix, normed, ctx_columns, weights, last, stacks, sems = refs
     pos = position()
     fetch = [
         pltpu.make_async_copy(w, weights.at[:, pl.ds(i * HD, HD)], sems.at[i])
         for i, w in enumerate((wq, wk, wv))
     ]
     fetch.append(pltpu.make_async_copy(wo, last, sems.at[3]))
-    for copy in fetch:
+    arrive = [
+        pltpu.make_async_copy(piece, stacks.at[i], sems.at[4 + i]) for i, piece in enumerate(pieces)
+    ]
+    for copy in arrive + fetch:
         copy.start()
-    tok, feat = qkv.shape[0], z0.shape[2]
+    tok, feat = qkv.shape[0], stacks.shape[3]
+    for copy in arrive:
+        copy.wait()
     blocks = []
-    for along_x, ref in enumerate((z0, z1, z2, z3)):
+    for along_x in range(4):
+        ref = stacks.at[along_x]
         blocks += [(ref, i, along_x, i) for i in range(4)]
         for i in range(4):
             place = ((pos[0] - i) & 3) * 4 + ((pos[1] - along_x) & 3)
@@ -181,18 +197,19 @@
     grads[:, 2 * HD :] = grad_v.astype(bf16)
 
 
-def loss_kernel(wo, mine, theirs, ctx, own, *refs):
+def loss_kernel(wo, ctx, own, *refs):
+    messages, refs = refs[:8], refs[8:]
     loss, grad_out, grads, grad_ctx_keys, grad_ctx_values, pooled, mix, weights, extra, slope, up = refs
     pos = position()
     width = wo.shape[1]
     co, y, dp = pos[4], pos[3], (pos[2] * 4 + pos[3]) * 2 + pos[4]
     for i in range(8):
-        messages, core = (mine, co) if i < 4 else (theirs, 1 - co)
+        message, core = messages[i], co if i < 4 else 1 - co
         here = pl.ds(pl.multiple_of((core * 4 + ((y - i % 4) & 3)) * 8, 8), 8)
-        pooled[here, :] = messages[i % 4, :, :width]
-        mix[here, :] = messages[i % 4, :, width : width + HD]
-        weights[here, :] = messages[i % 4, :, width + HD : width + 2 * HD]
-        extra[here, :] = messages[i % 4, :, width + 2 * HD :]
+        pooled[here, :] = message[:, :width]
+        mix[here, :] = message[:, width : width + HD]
+        weights[here, :] = message[:, width + HD : width + 2 * HD]
+        extra[here, :] = message[:, width + 2 * HD :]
     n = pooled.shape[0]
     vectors = pooled[...]
     length = jnp.sqrt(jnp.sum(vectors * vectors, axis=1, keepdims=True) + 1e-06)
@@ -236,10 +253,10 @@
     backward(own, ctx, upstream, grads, grad_ctx_keys)
 
 
-def context_kernel(own, one, two, three, values, wk, wv, total, out0, out1, out2, out3, part):
+def context_kernel(one, two, values, wk, wv, total, out0, out1, out2, out3, part):
     pos = position()
     half = part.shape[1]
-    grad = (own[...] + two[...]) + (one[...] + three[...])
+    grad = one[...] + two[...]
     grad = jnp.concatenate([grad, values[...]], axis=1)
     total[...] = grad
     here = pl.ds(pl.multiple_of(pos[4] * half, half), half)
@@ -257,7 +274,7 @@
     total[...] = (own[...] + wide(two[...])) + (wide(one[...]) + wide(three[...]))
     for k, out in enumerate((out0, out1, out2, out3)):
         at = (pos[0] + k) & 3
-        out[...] = total[pl.ds(pl.multiple_of(at * 8, 8), 8), :]
+        out[...] = total[pl.ds(pl.multiple_of(at * 8, 8), 8), :].astype(out.dtype)
 
 
 def finish_kernel(context, gain, mine, theirs, out):
@@ -357,8 +374,7 @@
     width = w_query.shape[0]
     gain_row = gain.reshape(1, width)
 
-    ctx_part = lax.dynamic_slice_in_dim(context, lax.axis_index(DP) * feat, feat, 1)
-    block = jnp.concatenate([doc_states, ctx_part, jnp.zeros_like(ctx_part)], axis=0)
+    block = call(block_kernel, shape(tok + 16, feat, dtype=bf16), ["v"] * 2)(doc_states, context)
     block = jnp.stack([block] + others(block, "zh"))
     rows = [block] + others(block, "x")
 
@@ -382,11 +398,12 @@
             shape(tok, width, dtype=bf16),
             shape(HD, feat),
         ),
-        ["v"] * 2 + ["a"] * 4 + ["v"] * 5,
+        ["v"] * 2 + ["a"] * 4 + ["v"] + ["a"] * 4,
         scratch=[
             pltpu.VMEM((width, 3 * HD), bf16),
             pltpu.VMEM((HD, width), bf16),
-            pltpu.SemaphoreType.DMA((4,)),
+            pltpu.VMEM((4,) + block.shape, bf16),
+            pltpu.SemaphoreType.DMA((8,)),
         ],
         vmem=24,
     )(gain_row, partners[:, None], w_query, w_key, w_value, w_out, ctx_kv, *rows)
@@ -394,7 +411,7 @@
     pooled = own_mean + ring_sum(ring_sum(branch, "x"), "zh")
     message = jnp.concatenate([pooled, mix], axis=1)
     message = pair(message, "zl")
-    messages = jnp.stack([message] + others(message, "y"))
+    messages = [message] + others(message, "y")
     total = 64
     loss, grad_out, grads, grad_ctx_keys, grad_ctx_values = call(
         loss_kernel,
@@ -405,7 +422,7 @@
             shape(HD, HD),
             shape(HD, HD),
         ),
-        ["v"] * 5,
+        ["v"] * 11,
         scratch=[
             pltpu.VMEM((total, width), f32),
             pltpu.VMEM((total, HD), f32),
@@ -415,29 +432,27 @@
             pltpu.VMEM((total, HD), f32),
         ],
         vmem=24,
-    )(w_out, messages, other(messages, "co"), ctx_kv, qkv)
+    )(w_out, ctx_kv, qkv, *messages, *[other(m, "co") for m in messages])
 
     half = width // 2
     rows = 4 * context.shape[0]
-    came = other(grad_ctx_keys, "co")
-    came, grads = lax.optimization_barrier((came, grads))
-    grad_ctx_keys = grad_ctx_keys + came
-    grad_ctx_keys = grad_ctx_keys + other(grad_ctx_keys, "zl")
-    by_y = others(grad_ctx_keys, "y")
+    one, two, three = others(grad_ctx_keys, "y")
+    by_y = (grad_ctx_keys + two) + (one + three)
+    grad_ctx_keys = by_y + other(by_y, "co")
     grad_ctx, part, *sent = call(
         context_kernel,
         (shape(HD, 2 * HD), shape(rows, half)) + (shape(rows, half, dtype=bf16),) * 3,
-        ["v"] * 7,
+        ["v"] * 5,
         scratch=[pltpu.VMEM((4 * rows, half), f32)],
-    )(grad_ctx_keys, *by_y, grad_ctx_values, w_key, w_value)
+    )(grad_ctx_keys, other(grad_ctx_keys, "zl"), grad_ctx_values, w_key, w_value)
     came = [shift(a, "x", k) for k, a in zip((1, 2, 3), sent)]
     part, *sent = call(
         middle_kernel,
-        (shape(rows // 4, half),) * 4,
+        (shape(rows // 4, half),) + (shape(rows // 4, half, dtype=bf16),) * 3,
         ["v"] * 4,
         scratch=[pltpu.VMEM((rows, half), f32)],
     )(part, *came)
-    one, two, three = [shift(a, "zh", k) for k, a in zip((1, 2, 3), sent)]
+    one, two, three = [wide(shift(a, "zh", k)) for k, a in zip((1, 2, 3), sent)]
     part = (part + two) + (one + three)
     grad_context = call(finish_kernel, shape(*context.shape), ["v"] * 4, flops=10**9)(
         context, gain_row, part, other(part, "co")
@@ -451,7 +466,7 @@
         )(normed, grads)
         for side in (1, 0)
     )
-    came, _ = lax.optimization_barrier((other(theirs, "co"), by_y[0]))
+    came, _ = lax.optimization_barrier((other(theirs, "co"), by_y))
     mine, *sent = call(
         weight_y_kernel,
         (shape(2, feat, 3 * HD),) + (shape(2, feat, 3 * HD, dtype=bf16),) * 3,

time: 156 us -> 155 us (level)
  waiting for transfers between devices: 46.3 us -> 40.4 us
  starting transfers between devices: 81.7 us -> 85.8 us
  local copies, waits for them, and re-layouts: 6.64 us -> 8.77 us
  other arithmetic: 4.14 us -> 2.02 us
    ppermute x7 -> x10, waiting for transfers between devices: 10.4 us -> 5.53 us  [other(): return lax.ppermute(a, axis, [(0, 1), (1, 0)])]
    unnamed x28 -> x32, local copies, waits for them, and re-layouts: 4.78 us -> 7.82 us
    ppermute x7 -> x10, starting transfers between devices: 14.8 us -> 17.2 us  [other(): return lax.ppermute(a, axis, [(0, 1), (1, 0)])]
    ppermute x27, starting transfers between devices: 52.9 us -> 54.6 us  [shift(): return lax.ppermute(a, axis, [(i, (i + k) % 4) for i in range(4)])]
  transfers between devices with their start and end apart: 36 -> 39, of which waited for: 20 -> 21; matrix products, arithmetic and copies ran while one was open for 2% -> 1% of each run, Pallas kernels for 2% -> 2%
where the time goes in v2:
time: 155 us; the launch traced here: 153 us
  starting transfers between devices  85.8 us (55%)
  waiting for transfers between devices  40.4 us (26%)
  Pallas kernels  14.6 us (9%)
  local copies, waits for them, and re-layouts  8.77 us (6%)
  other arithmetic  2.02 us (1%)
    ppermute x27, starting transfers between devices, shift(): return lax.ppermute(a, axis, [(i, (i + k) % 4) for i in range(4)])  54.6 us
    ppermute x27, waiting for transfers between devices, shift(): return lax.ppermute(a, axis, [(i, (i + k) % 4) for i in range(4)])  26.9 us
    ppermute x10, starting transfers between devices, other(): return lax.ppermute(a, axis, [(0, 1), (1, 0)])  17.2 us
    all_to_all x1, starting transfers between devices, spread(): return lax.all_to_all(copies, axis, 0, 0)  9.54 us
    unnamed x32, local copies, waits for them, and re-layouts  7.82 us
    all_to_all x1, waiting for transfers between devices, spread(): return lax.all_to_all(copies, axis, 0, 0)  5.76 us
    ppermute x10, waiting for transfers between devices, other(): return lax.ppermute(a, axis, [(0, 1), (1, 0)])  5.53 us
    pallas_call x1, Pallas kernels, shards(): call(loss_kernel, (shape(1, 1), shape(HD, feat), shape(tok, 3 * HD, dtype...  4.94 us
  transfers between devices with their start and end apart: 39, of which 21 were waited for; matrix products, arithmetic and copies ran while one was open for 1% of the time, Pallas kernels for 2%

profile of v2, /device:TPU:1, one launch (start us, length us, event | category | flops | bytes accessed | tf_op | source)
XLA Modules:
  0.0 153.2 jit_solution(6863975459245700520)
XLA Ops:
  0.7 1.0 copy-done.10
  1.6 0.8 copy-done.13
  2.5 3.9 %collective-permute-start.1 = (bf16[272,256]{1,0:T(8,128)(2,1)S(1)}, bf16[272,256]{1,0:T(8,128)(2,1)S(1)}, u32[]{:S(2)}, u32[]{:S(2)}) collective-permute-start(bf16[272,256]{1,0:T(8,128)(2,1)S(1)} %shard_map.127), channel_id=1, source_target_pairs={{0,64},{64,128},{128,192},{192,0},{1,65},{65,129},{129,193},{193,1... | collective-permute-start | bytes 417800 | tf_op jit(solution)/shard_map/ppermute | solution.py:336
  6.4 5.1 %collective-permute-start.2 = (bf16[272,256]{1,0:T(8,128)(2,1)S(1)}, bf16[272,256]{1,0:T(8,128)(2,1)S(1)}, u32[]{:S(2)}, u32[]{:S(2)}) collective-permute-start(bf16[272,256]{1,0:T(8,128)(2,1)S(1)} %shard_map.127), channel_id=1, source_target_pairs={{0,128},{64,192},{128,0},{192,64},{1,129},{65,193},{129,1},{193,65... | collective-permute-start | bytes 417800 | tf_op jit(solution)/shard_map/ppermute | solution.py:336
  11.5 2.4 %collective-permute-start.3 = (bf16[272,256]{1,0:T(8,128)(2,1)S(1)}, bf16[272,256]{1,0:T(8,128)(2,1)S(1)}, u32[]{:S(2)}, u32[]{:S(2)}) collective-permute-start(bf16[272,256]{1,0:T(8,128)(2,1)S(1)} %shard_map.127), channel_id=1, source_target_pairs={{0,192},{64,0},{128,64},{192,128},{1,193},{65,1},{129,65},{193,129... | collective-permute-start | bytes 417800 | tf_op jit(solution)/shard_map/ppermute | solution.py:336
  13.9 4.5 %collective-permute-start = (bf16[8,4096]{1,0:T(8,128)(2,1)S(1)}, bf16[8,4096]{1,0:T(8,128)(2,1)S(1)}, u32[]{:S(2)}, u32[]{:S(2)}) collective-permute-start(bf16[8,4096]{1,0:T(8,128)(2,1)S(1)} %copy-done.13), channel_id=1, source_target_pairs={{0,0},{1,16},{2,32},{3,48},{4,64},{5,80},{6,96},{7,112},{8,128},{9... | collective-permute-start | bytes 196616 | tf_op jit(solution)/shard_map/ppermute | solution.py:382
  18.4 2.2 %collective-permute-done = bf16[8,4096]{1,0:T(8,128)(2,1)S(1)} collective-permute-done((bf16[8,4096]{1,0:T(8,128)(2,1)S(1)}, bf16[8,4096]{1,0:T(8,128)(2,1)S(1)}, u32[]{:S(2)}, u32[]{:S(2)}) %collective-permute-start) | collective-permute-done | bytes 65568 | tf_op jit(solution)/shard_map/ppermute | solution.py:382
  20.7 4.5 %collective-permute-done.3 = bf16[272,256]{1,0:T(8,128)(2,1)S(1)} collective-permute-done((bf16[272,256]{1,0:T(8,128)(2,1)S(1)}, bf16[272,256]{1,0:T(8,128)(2,1)S(1)}, u32[]{:S(2)}, u32[]{:S(2)}) %collective-permute-start.3) | collective-permute-done | bytes 139296 | tf_op jit(solution)/shard_map/ppermute | solution.py:336
  25.3 1.3 collective-permute-start.4
  26.6 2.5 %collective-permute-start.5 = (bf16[4,272,256]{2,1,0:T(8,128)(2,1)S(1)}, bf16[4,272,256]{2,1,0:T(8,128)(2,1)}, u32[]{:S(2)}, u32[]{:S(2)}) collective-permute-start(bf16[4,272,256]{2,1,0:T(8,128)(2,1)S(1)} %pad_maximum_fusion.refs_0_), channel_id=1, source_target_pairs={{0,32},{16,48},{32,0},{48,16},{1,33},{17,49},{33,1},{49,17},{2,34}... | collective-permute-start | bytes 1671176 | tf_op jit(solution)/shard_map/ppermute | solution.py:336
  29.0 1.2 collective-permute-start.6
  31.1 0.7 broadcast_in_dim.6
  31.8 9.5 %all-to-all-start = ((bf16[16,8,384]{2,1,0:T(8,128)(2,1)}), bf16[16,8,384]{2,1,0:T(8,128)(2,1)S(1)}, u32[]{:S(2)}, u32[]{:S(2)}) async-start(bf16[16,8,384]{2,1,0:T(8,128)(2,1)} %broadcast_in_dim.6), calls=%async_computation | async-start | bytes 196608 | tf_op jit(solution)/shard_map/all_to_all | solution.py:368
  41.4 5.8 %all-to-all-done = bf16[16,8,384]{2,1,0:T(8,128)(2,1)S(1)} async-done(((bf16[16,8,384]{2,1,0:T(8,128)(2,1)}), bf16[16,8,384]{2,1,0:T(8,128)(2,1)S(1)}, u32[]{:S(2)}, u32[]{:S(2)}) %all-to-all-start) | async-done | bytes 98336 | tf_op jit(solution)/shard_map/all_to_all | solution.py:368
  47.2 6.3 %collective-permute-done.5.refs_2_ = bf16[4,272,256]{2,1,0:T(8,128)(2,1)} collective-permute-done((bf16[4,272,256]{2,1,0:T(8,128)(2,1)S(1)}, bf16[4,272,256]{2,1,0:T(8,128)(2,1)}, u32[]{:S(2)}, u32[]{:S(2)}) %collective-permute-start.5) | collective-permute-done | bytes 557088 | tf_op jit(solution)/shard_map/ppermute | solution.py:336
  53.5 1.2 copy-done.2
  54.7 1.1 copy-done.5
  55.8 1.2 copy-done.6
  57.0 1.2 copy-done.7
  58.2 4.9 %shard_map.128 = (bf16[256,384]{1,0:T(8,128)(2,1)S(1)}, f32[4,4096]{1,0:T(4,128)S(1)}, f32[4,4096]{1,0:T(4,128)S(1)}, f32[4,384]{1,0:T(4,128)S(1)}, bf16[256,409...) custom-call(f32[1,4096]{1,0:T(1,128)S(1)} %bitcast.14, s32[4,1]{1,0:T(4,128)S(1)} %copy.16.partners, ...), custom_call_target="tpu_custom_call" | custom-call | flops 1000000000 | tf_op jit(solution)/shard_map/pallas_call | solution.py:391
  63.1 1.8 %collective-permute-start.7 = (f32[4,4096]{1,0:T(4,128)S(1)}, f32[4,4096]{1,0:T(4,128)S(1)}, u32[]{:S(2)}, u32[]{:S(2)}) collective-permute-start(f32[4,4096]{1,0:T(4,128)S(1)} %get-tuple-element.40), channel_id=1, source_target_pairs={{0,32},{16,48},{32,0},{48,16},{1,33},{17,49},{33,1},{49,17},{2,34}... | collective-permute-start | bytes 196616 | tf_op jit(solution)/shard_map/ppermute | solution.py:336
  65.0 1.4 collective-permute-start.8
  66.4 1.3 collective-permute-start.9
  67.8 2.1 %collective-permute-done.8 = f32[4,4096]{1,0:T(4,128)S(1)} collective-permute-done((f32[4,4096]{1,0:T(4,128)S(1)}, f32[4,4096]{1,0:T(4,128)S(1)}, u32[]{:S(2)}, u32[]{:S(2)}) %collective-permute-start.8) | collective-permute-done | bytes 65568 | tf_op jit(solution)/shard_map/ppermute | solution.py:336
  70.0 4.3 %collective-permute-start.10 = (f32[4,4096]{1,0:T(4,128)S(1)}, f32[4,4096]{1,0:T(4,128)S(1)}, u32[]{:S(2)}, u32[]{:S(2)}) collective-permute-start(f32[4,4096]{1,0:T(4,128)S(1)} %add_add_fusion.3), channel_id=1, source_target_pairs={{0,128},{64,192},{128,0},{192,64},{1,129},{65,193},{129,1},{193,65... | collective-permute-start | bytes 196616 | tf_op jit(solution)/shard_map/ppermute | solution.py:336
  74.3 7.0 %collective-permute-start.11 = (f32[4,4096]{1,0:T(4,128)S(1)}, f32[4,4096]{1,0:T(4,128)S(1)}, u32[]{:S(2)}, u32[]{:S(2)}) collective-permute-start(f32[4,4096]{1,0:T(4,128)S(1)} %add_add_fusion.3), channel_id=1, source_target_pairs={{0,64},{64,128},{128,192},{192,0},{1,65},{65,129},{129,193},{193,1... | collective-permute-start | bytes 196616 | tf_op jit(solution)/shard_map/ppermute | solution.py:336
  81.3 1.7 %collective-permute-done.11 = f32[4,4096]{1,0:T(4,128)S(1)} collective-permute-done((f32[4,4096]{1,0:T(4,128)S(1)}, f32[4,4096]{1,0:T(4,128)S(1)}, u32[]{:S(2)}, u32[]{:S(2)}) %collective-permute-start.11) | collective-permute-done | bytes 65568 | tf_op jit(solution)/shard_map/ppermute | solution.py:336
  83.0 2.7 %collective-permute-done.12 = f32[4,4096]{1,0:T(4,128)S(1)} collective-permute-done((f32[4,4096]{1,0:T(4,128)S(1)}, f32[4,4096]{1,0:T(4,128)S(1)}, u32[]{:S(2)}, u32[]{:S(2)}) %collective-permute-start.12) | collective-permute-done | bytes 65568 | tf_op jit(solution)/shard_map/ppermute | solution.py:336
  85.7 0.6 pad_maximum_fusion.1
  86.3 3.5 %collective-permute-done.13 = f32[4,4480]{1,0:T(4,128)} collective-permute-done((f32[4,4480]{1,0:T(4,128)}, f32[4,4480]{1,0:T(4,128)}, u32[]{:S(2)}, u32[]{:S(2)}) %collective-permute-start.13) | collective-permute-done | bytes 71712 | tf_op jit(solution)/shard_map/ppermute | solution.py:344
  89.8 1.0 maximum_select_fusion.refs_0_
  91.2 1.5 collective-permute-start.15
  92.7 1.0 collective-permute-start.16
  93.7 4.9 %collective-permute-start.17 = (f32[8,4480]{1,0:T(8,128)S(1)}, f32[8,4480]{1,0:T(8,128)S(1)}, u32[]{:S(2)}, u32[]{:S(2)}) collective-permute-start(f32[8,4480]{1,0:T(8,128)S(1)} %maximum_select_fusion.refs_0_), channel_id=1, source_target_pairs={{0,1},{1,0},{2,3},{3,2},{4,5},{5,4},{6,7},{7,6},{8,9},{9,8},{10,11... | collective-permute-start | bytes 430088 | tf_op jit(solution)/shard_map/ppermute | solution.py:344
  98.5 4.5 %collective-permute-start.18 = (f32[8,4480]{1,0:T(8,128)S(1)}, f32[8,4480]{1,0:T(8,128)S(1)}, u32[]{:S(2)}, u32[]{:S(2)}) collective-permute-start(f32[8,4480]{1,0:T(8,128)S(1)} %collective-permute-done.14.refs_1_), channel_id=1, source_target_pairs={{0,1},{1,0},{2,3},{3,2},{4,5},{5,4},{6,7},{7,6},{8,9},{9,8},{10,11... | collective-permute-start | bytes 430088 | tf_op jit(solution)/shard_map/ppermute | solution.py:344
  103.1 0.9 collective-permute-start.20
  104.4 0.5 collective-permute-done.20.refs_7_
  105.0 1.2 copy-done.8
  106.2 4.9 %shard_map.129 = (f32[1,1]{1,0:T(1,128)}, f32[128,256]{1,0:T(8,128)}, bf16[256,384]{1,0:T(8,128)(2,1)S(1)}, f32[128,128]{1,0:T(8,128)S(1)}, f32[128,128]{1,0:T(8,128)S(1)}) custom-call(bf16[128,4096]{1,0:T(8,128)(2,1)S(1)} %copy-done.8, bf16[128,384]{1,0:T(8,128)(2,1)S(1)} %bitcast.13, bf16[256,384]{1,0:T(8,128)(2,1)S(1)} %get-tuple-element.38.own, ...), custom_call_target="tpu_custom_call" | custom-call | flops 1000000000 | tf_op jit(solution)/shard_map/pallas_call | solution.py:416
  111.1 0.8 shard_map.134
  111.9 0.5 collective-permute-start.33
  112.4 0.4 collective-permute-start.21
  112.7 2.4 %collective-permute-start.22 = (f32[128,128]{1,0:T(8,128)S(1)}, f32[128,128]{1,0:T(8,128)S(1)}, u32[]{:S(2)}, u32[]{:S(2)}) collective-permute-start(f32[128,128]{1,0:T(8,128)S(1)} %get-tuple-element.43), channel_id=1, source_target_pairs={{0,2},{2,4},{4,6},{6,0},{1,3},{3,5},{5,7},{7,1},{8,10},{10,12},{12... | collective-permute-start | bytes 196616 | tf_op jit(solution)/shard_map/ppermute | solution.py:336
  115.4 2.0 %collective-permute-done.21 = f32[128,128]{1,0:T(8,128)S(1)} collective-permute-done((f32[128,128]{1,0:T(8,128)S(1)}, f32[128,128]{1,0:T(8,128)S(1)}, u32[]{:S(2)}, u32[]{:S(2)}) %collective-permute-start.21) | collective-permute-done | bytes 65568 | tf_op jit(solution)/shard_map/ppermute | solution.py:336
  117.4 1.9 %collective-permute-done.22 = f32[128,128]{1,0:T(8,128)S(1)} collective-permute-done((f32[128,128]{1,0:T(8,128)S(1)}, f32[128,128]{1,0:T(8,128)S(1)}, u32[]{:S(2)}, u32[]{:S(2)}) %collective-permute-start.22) | collective-permute-done | bytes 65568 | tf_op jit(solution)/shard_map/ppermute | solution.py:336
  119.3 0.9 collective-permute-start.24
  120.2 0.8 shard_map.133.mine
  121.7 3.5 %collective-permute-start.35 = (bf16[2,256,384]{2,1,0:T(8,128)(2,1)S(1)}, bf16[2,256,384]{2,1,0:T(8,128)(2,1)S(1)}, u32[]{:S(2)}, u32[]{:S(2)}) collective-permute-start(bf16[2,256,384]{2,1,0:T(8,128)(2,1)S(1)} %get-tuple-element.58), channel_id=1, source_target_pairs={{0,4},{2,6},{4,0},{6,2},{1,5},{3,7},{5,1},{7,3},{8,12},{10,14},{12... | collective-permute-start | bytes 1179656 | tf_op jit(solution)/shard_map/ppermute | solution.py:336
  125.2 0.8 shard_map.130
  126.0 1.2 collective-permute-start.26
  127.2 3.0 %collective-permute-start.27 = (bf16[32,2048]{1,0:T(8,128)(2,1)S(1)}, bf16[32,2048]{1,0:T(8,128)(2,1)S(1)}, u32[]{:S(2)}, u32[]{:S(2)}) collective-permute-start(bf16[32,2048]{1,0:T(8,128)(2,1)S(1)} %get-tuple-element.47), channel_id=1, source_target_pairs={{0,32},{16,48},{32,0},{48,16},{1,33},{17,49},{33,1},{49,17},{2,34}... | collective-permute-start | bytes 393224 | tf_op jit(solution)/shard_map/ppermute | solution.py:336
  130.2 1.5 collective-permute-done.26.one
  131.7 1.5 collective-permute-start.28
  133.2 1.9 %collective-permute-done.27.two = bf16[32,2048]{1,0:T(8,128)(2,1)S(1)} collective-permute-done((bf16[32,2048]{1,0:T(8,128)(2,1)S(1)}, bf16[32,2048]{1,0:T(8,128)(2,1)S(1)}, u32[]{:S(2)}, u32[]{:S(2)}) %collective-permute-start.27) | collective-permute-done | bytes 131104 | tf_op jit(solution)/shard_map/ppermute | solution.py:336
  135.1 0.7 collective-permute-done.28.three
  135.9 3.8 %collective-permute-start.29 = (bf16[8,2048]{1,0:T(8,128)(2,1)S(1)}, bf16[8,2048]{1,0:T(8,128)(2,1)S(1)}, u32[]{:S(2)}, u32[]{:S(2)}) collective-permute-start(bf16[8,2048]{1,0:T(8,128)(2,1)S(1)} %get-tuple-element.50), channel_id=1, source_target_pairs={{0,128},{64,192},{128,0},{192,64},{1,129},{65,193},{129,1},{193,65... | collective-permute-start | bytes 98312 | tf_op jit(solution)/shard_map/ppermute | solution.py:336
  139.7 1.4 collective-permute-start.30
  141.1 2.2 %collective-permute-start.31 = (bf16[8,2048]{1,0:T(8,128)(2,1)S(1)}, bf16[8,2048]{1,0:T(8,128)(2,1)S(1)}, u32[]{:S(2)}, u32[]{:S(2)}) collective-permute-start(bf16[8,2048]{1,0:T(8,128)(2,1)S(1)} %get-tuple-element.52), channel_id=1, source_target_pairs={{0,192},{64,0},{128,64},{192,128},{1,193},{65,1},{129,65},{193,129... | collective-permute-start | bytes 98312 | tf_op jit(solution)/shard_map/ppermute | solution.py:336
  143.7 0.9 collective-permute-done.30
  144.6 0.5 collective-permute-done.31
  145.2 5.3 %collective-permute-start.32 = (f32[8,2048]{1,0:T(8,128)S(1)}, f32[8,2048]{1,0:T(8,128)S(1)}, u32[]{:S(2)}, u32[]{:S(2)}) collective-permute-start(f32[8,2048]{1,0:T(8,128)S(1)} %add_add_fusion.mine), channel_id=1, source_target_pairs={{0,1},{1,0},{2,3},{3,2},{4,5},{5,4},{6,7},{7,6},{8,9},{9,8},{10,11... | collective-permute-start | bytes 196616 | tf_op jit(solution)/shard_map/ppermute | solution.py:344
  150.5 0.9 collective-permute-done.32.theirs
  151.4 0.8 shard_map.132
  152.2 0.9 shard_map.137
  (76 shorter events, 3.8 us)
Async XLA Ops:
  0.6 29.8 %copy-start.9 = (f32[4096]{0:T(1024)S(1)}, f32[4096]{0:T(1024)}, u32[]{:S(2)}) copy-start(f32[4096]{0:T(1024)} %param.10) | copy-start | bytes 49156
  0.6 29.8 %copy-start.1 = (bf16[4096,128]{1,0:T(8,128)(2,1)S(1)}, bf16[4096,128]{1,0:T(8,128)(2,1)}, u32[]{:S(2)}) copy-start(bf16[4096,128]{1,0:T(8,128)(2,1)} %wv.3) | copy-start | bytes 3145732
  0.7 1.0 copy-start.10
  1.6 0.8 copy-start.13
  2.5 28.2 %copy-start = (bf16[4096,128]{1,0:T(8,128)(2,1)S(1)}, bf16[4096,128]{1,0:T(8,128)(2,1)}, u32[]{:S(2)}) copy-start(bf16[4096,128]{1,0:T(8,128)(2,1)} %wk.3) | copy-start | bytes 3145732
  2.5 18.2 %collective-permute-start.1 = (bf16[272,256]{1,0:T(8,128)(2,1)S(1)}, bf16[272,256]{1,0:T(8,128)(2,1)S(1)}, u32[]{:S(2)}, u32[]{:S(2)}) collective-permute-start(bf16[272,256]{1,0:T(8,128)(2,1)S(1)} %shard_map.127), channel_id=1, source_target_pairs={{0,64},{64,128},{128,192},{192,0},{1,65},{65,129},{129,193},{193,1... | collective-permute-start | bytes 417800 | tf_op jit(solution)/shard_map/ppermute | solution.py:336
  6.4 14.3 %collective-permute-start.2 = (bf16[272,256]{1,0:T(8,128)(2,1)S(1)}, bf16[272,256]{1,0:T(8,128)(2,1)S(1)}, u32[]{:S(2)}, u32[]{:S(2)}) collective-permute-start(bf16[272,256]{1,0:T(8,128)(2,1)S(1)} %shard_map.127), channel_id=1, source_target_pairs={{0,128},{64,192},{128,0},{192,64},{1,129},{65,193},{129,1},{193,65... | collective-permute-start | bytes 417800 | tf_op jit(solution)/shard_map/ppermute | solution.py:336
  11.5 13.6 %collective-permute-start.3 = (bf16[272,256]{1,0:T(8,128)(2,1)S(1)}, bf16[272,256]{1,0:T(8,128)(2,1)S(1)}, u32[]{:S(2)}, u32[]{:S(2)}) collective-permute-start(bf16[272,256]{1,0:T(8,128)(2,1)S(1)} %shard_map.127), channel_id=1, source_target_pairs={{0,192},{64,0},{128,64},{192,128},{1,193},{65,1},{129,65},{193,129... | collective-permute-start | bytes 417800 | tf_op jit(solution)/shard_map/ppermute | solution.py:336
  13.9 6.7 %collective-permute-start = (bf16[8,4096]{1,0:T(8,128)(2,1)S(1)}, bf16[8,4096]{1,0:T(8,128)(2,1)S(1)}, u32[]{:S(2)}, u32[]{:S(2)}) collective-permute-start(bf16[8,4096]{1,0:T(8,128)(2,1)S(1)} %copy-done.13), channel_id=1, source_target_pairs={{0,0},{1,16},{2,32},{3,48},{4,64},{5,80},{6,96},{7,112},{8,128},{9... | collective-permute-start | bytes 196616 | tf_op jit(solution)/shard_map/ppermute | solution.py:382
  25.2 28.3 %copy-start.4 = (bf16[4,272,256]{2,1,0:T(8,128)(2,1)}, bf16[4,272,256]{2,1,0:T(8,128)(2,1)S(1)}, u32[]{:S(2)}) copy-start(bf16[4,272,256]{2,1,0:T(8,128)(2,1)S(1)} %pad_maximum_fusion.refs_0_) | copy-start | bytes 1671172
  25.2 16.1 %copy-start.15 = (s32[4]{0:T(128)S(1)}, s32[4]{0:T(128)}, u32[]{:S(2)}) copy-start(s32[4]{0:T(128)} %param.15) | copy-start | bytes 52
  25.3 21.9 %collective-permute-start.4 = (bf16[4,272,256]{2,1,0:T(8,128)(2,1)S(1)}, bf16[4,272,256]{2,1,0:T(8,128)(2,1)}, u32[]{:S(2)}, u32[]{:S(2)}) collective-permute-start(bf16[4,272,256]{2,1,0:T(8,128)(2,1)S(1)} %pad_maximum_fusion.refs_0_), channel_id=1, source_target_pairs={{0,16},{16,32},{32,48},{48,0},{1,17},{17,33},{33,49},{49,1},{2,18}... | collective-permute-start | bytes 1671176 | tf_op jit(solution)/shard_map/ppermute | solution.py:336
  26.6 27.0 %collective-permute-start.5 = (bf16[4,272,256]{2,1,0:T(8,128)(2,1)S(1)}, bf16[4,272,256]{2,1,0:T(8,128)(2,1)}, u32[]{:S(2)}, u32[]{:S(2)}) collective-permute-start(bf16[4,272,256]{2,1,0:T(8,128)(2,1)S(1)} %pad_maximum_fusion.refs_0_), channel_id=1, source_target_pairs={{0,32},{16,48},{32,0},{48,16},{1,33},{17,49},{33,1},{49,17},{2,34}... | collective-permute-start | bytes 1671176 | tf_op jit(solution)/shard_map/ppermute | solution.py:336
  29.0 24.5 %collective-permute-start.6 = (bf16[4,272,256]{2,1,0:T(8,128)(2,1)S(1)}, bf16[4,272,256]{2,1,0:T(8,128)(2,1)}, u32[]{:S(2)}, u32[]{:S(2)}) collective-permute-start(bf16[4,272,256]{2,1,0:T(8,128)(2,1)S(1)} %pad_maximum_fusion.refs_0_), channel_id=1, source_target_pairs={{0,48},{16,0},{32,16},{48,32},{1,49},{17,1},{33,17},{49,33},{2,50}... | collective-permute-start | bytes 1671176 | tf_op jit(solution)/shard_map/ppermute | solution.py:336
  31.8 15.4 %all-to-all-start = ((bf16[16,8,384]{2,1,0:T(8,128)(2,1)}), bf16[16,8,384]{2,1,0:T(8,128)(2,1)S(1)}, u32[]{:S(2)}, u32[]{:S(2)}) async-start(bf16[16,8,384]{2,1,0:T(8,128)(2,1)} %broadcast_in_dim.6), calls=%async_computation | async-start | bytes 196608 | tf_op jit(solution)/shard_map/all_to_all | solution.py:368
  53.5 1.2 copy-start.2
  54.7 1.1 copy-start.5
  55.8 1.2 copy-start.6
  57.0 1.2 copy-start.7
  63.1 22.6 %copy-start.11 = (f32[128,256]{1,0:T(8,128)}, f32[128,256]{1,0:T(8,128)S(1)}, u32[]{:S(2)}) copy-start(f32[128,256]{1,0:T(8,128)S(1)} %get-tuple-element.62.ctx_columns) | copy-start | bytes 393220
  63.1 4.7 %collective-permute-start.7 = (f32[4,4096]{1,0:T(4,128)S(1)}, f32[4,4096]{1,0:T(4,128)S(1)}, u32[]{:S(2)}, u32[]{:S(2)}) collective-permute-start(f32[4,4096]{1,0:T(4,128)S(1)} %get-tuple-element.40), channel_id=1, source_target_pairs={{0,32},{16,48},{32,0},{48,16},{1,33},{17,49},{33,1},{49,17},{2,34}... | collective-permute-start | bytes 196616 | tf_op jit(solution)/shard_map/ppermute | solution.py:336
  65.0 5.0 %collective-permute-start.8 = (f32[4,4096]{1,0:T(4,128)S(1)}, f32[4,4096]{1,0:T(4,128)S(1)}, u32[]{:S(2)}, u32[]{:S(2)}) collective-permute-start(f32[4,4096]{1,0:T(4,128)S(1)} %get-tuple-element.40), channel_id=1, source_target_pairs={{0,16},{16,32},{32,48},{48,0},{1,17},{17,33},{33,49},{49,1},{2,18}... | collective-permute-start | bytes 196616 | tf_op jit(solution)/shard_map/ppermute | solution.py:336
  66.4 3.6 %collective-permute-start.9 = (f32[4,4096]{1,0:T(4,128)S(1)}, f32[4,4096]{1,0:T(4,128)S(1)}, u32[]{:S(2)}, u32[]{:S(2)}) collective-permute-start(f32[4,4096]{1,0:T(4,128)S(1)} %get-tuple-element.40), channel_id=1, source_target_pairs={{0,48},{16,0},{32,16},{48,32},{1,49},{17,1},{33,17},{49,33},{2,50}... | collective-permute-start | bytes 196616 | tf_op jit(solution)/shard_map/ppermute | solution.py:336
  70.0 11.3 %collective-permute-start.10 = (f32[4,4096]{1,0:T(4,128)S(1)}, f32[4,4096]{1,0:T(4,128)S(1)}, u32[]{:S(2)}, u32[]{:S(2)}) collective-permute-start(f32[4,4096]{1,0:T(4,128)S(1)} %add_add_fusion.3), channel_id=1, source_target_pairs={{0,128},{64,192},{128,0},{192,64},{1,129},{65,193},{129,1},{193,65... | collective-permute-start | bytes 196616 | tf_op jit(solution)/shard_map/ppermute | solution.py:336
  74.3 8.7 %collective-permute-start.11 = (f32[4,4096]{1,0:T(4,128)S(1)}, f32[4,4096]{1,0:T(4,128)S(1)}, u32[]{:S(2)}, u32[]{:S(2)}) collective-permute-start(f32[4,4096]{1,0:T(4,128)S(1)} %add_add_fusion.3), channel_id=1, source_target_pairs={{0,64},{64,128},{128,192},{192,0},{1,65},{65,129},{129,193},{193,1... | collective-permute-start | bytes 196616 | tf_op jit(solution)/shard_map/ppermute | solution.py:336
  81.3 4.3 %collective-permute-start.12 = (f32[4,4096]{1,0:T(4,128)S(1)}, f32[4,4096]{1,0:T(4,128)S(1)}, u32[]{:S(2)}, u32[]{:S(2)}) collective-permute-start(f32[4,4096]{1,0:T(4,128)S(1)} %add_add_fusion.3), channel_id=1, source_target_pairs={{0,192},{64,0},{128,64},{192,128},{1,193},{65,1},{129,65},{193,129... | collective-permute-start | bytes 196616 | tf_op jit(solution)/shard_map/ppermute | solution.py:336
  86.3 3.5 %collective-permute-start.13 = (f32[4,4480]{1,0:T(4,128)}, f32[4,4480]{1,0:T(4,128)}, u32[]{:S(2)}, u32[]{:S(2)}) collective-permute-start(f32[4,4480]{1,0:T(4,128)} %pad_maximum_fusion.1), channel_id=1, source_target_pairs={{0,8},{8,0},{1,9},{9,1},{2,10},{10,2},{3,11},{11,3},{4,12},{12,4},... | collective-permute-start | bytes 215048 | tf_op jit(solution)/shard_map/ppermute | solution.py:344
  90.9 7.7 %collective-permute-start.14 = (f32[8,4480]{1,0:T(8,128)S(1)}, f32[8,4480]{1,0:T(8,128)S(1)}, u32[]{:S(2)}, u32[]{:S(2)}) collective-permute-start(f32[8,4480]{1,0:T(8,128)S(1)} %maximum_select_fusion.refs_0_), channel_id=1, source_target_pairs={{0,2},{2,4},{4,6},{6,0},{1,3},{3,5},{5,7},{7,1},{8,10},{10,12},{12... | collective-permute-start | bytes 430088 | tf_op jit(solution)/shard_map/ppermute | solution.py:336
  91.2 11.9 %collective-permute-start.15 = (f32[8,4480]{1,0:T(8,128)S(1)}, f32[8,4480]{1,0:T(8,128)S(1)}, u32[]{:S(2)}, u32[]{:S(2)}) collective-permute-start(f32[8,4480]{1,0:T(8,128)S(1)} %maximum_select_fusion.refs_0_), channel_id=1, source_target_pairs={{0,4},{2,6},{4,0},{6,2},{1,5},{3,7},{5,1},{7,3},{8,12},{10,14},{12... | collective-permute-start | bytes 430088 | tf_op jit(solution)/shard_map/ppermute | solution.py:336
  92.7 10.4 %collective-permute-start.16 = (f32[8,4480]{1,0:T(8,128)S(1)}, f32[8,4480]{1,0:T(8,128)S(1)}, u32[]{:S(2)}, u32[]{:S(2)}) collective-permute-start(f32[8,4480]{1,0:T(8,128)S(1)} %maximum_select_fusion.refs_0_), channel_id=1, source_target_pairs={{0,6},{2,0},{4,2},{6,4},{1,7},{3,1},{5,3},{7,5},{8,14},{10,8},{12,... | collective-permute-start | bytes 430088 | tf_op jit(solution)/shard_map/ppermute | solution.py:336
  93.7 10.3 %collective-permute-start.17 = (f32[8,4480]{1,0:T(8,128)S(1)}, f32[8,4480]{1,0:T(8,128)S(1)}, u32[]{:S(2)}, u32[]{:S(2)}) collective-permute-start(f32[8,4480]{1,0:T(8,128)S(1)} %maximum_select_fusion.refs_0_), channel_id=1, source_target_pairs={{0,1},{1,0},{2,3},{3,2},{4,5},{5,4},{6,7},{7,6},{8,9},{9,8},{10,11... | collective-permute-start | bytes 430088 | tf_op jit(solution)/shard_map/ppermute | solution.py:344
  98.5 5.5 %collective-permute-start.18 = (f32[8,4480]{1,0:T(8,128)S(1)}, f32[8,4480]{1,0:T(8,128)S(1)}, u32[]{:S(2)}, u32[]{:S(2)}) collective-permute-start(f32[8,4480]{1,0:T(8,128)S(1)} %collective-permute-done.14.refs_1_), channel_id=1, source_target_pairs={{0,1},{1,0},{2,3},{3,2},{4,5},{5,4},{6,7},{7,6},{8,9},{9,8},{10,11... | collective-permute-start | bytes 430088 | tf_op jit(solution)/shard_map/ppermute | solution.py:344
  103.1 1.4 collective-permute-start.19
  103.1 1.9 %collective-permute-start.20 = (f32[8,4480]{1,0:T(8,128)S(1)}, f32[8,4480]{1,0:T(8,128)S(1)}, u32[]{:S(2)}, u32[]{:S(2)}) collective-permute-start(f32[8,4480]{1,0:T(8,128)S(1)} %collective-permute-done.16.refs_3_), channel_id=1, source_target_pairs={{0,1},{1,0},{2,3},{3,2},{4,5},{5,4},{6,7},{7,6},{8,9},{9,8},{10,11... | collective-permute-start | bytes 430088 | tf_op jit(solution)/shard_map/ppermute | solution.py:344
  105.0 1.2 copy-start.8
  111.9 9.3 %collective-permute-start.33 = (bf16[8,256,384]{2,1,0:T(8,128)(2,1)S(1)}, bf16[8,256,384]{2,1,0:T(8,128)(2,1)S(1)}, u32[]{:S(2)}, u32[]{:S(2)}) collective-permute-start(bf16[8,256,384]{2,1,0:T(8,128)(2,1)S(1)} %shard_map.134), channel_id=1, source_target_pairs={{0,1},{1,0},{2,3},{3,2},{4,5},{5,4},{6,7},{7,6},{8,9},{9,8},{10,11... | collective-permute-start | bytes 4718600 | tf_op jit(solution)/shard_map/ppermute | solution.py:344
  112.4 5.1 %collective-permute-start.21 = (f32[128,128]{1,0:T(8,128)S(1)}, f32[128,128]{1,0:T(8,128)S(1)}, u32[]{:S(2)}, u32[]{:S(2)}) collective-permute-start(f32[128,128]{1,0:T(8,128)S(1)} %get-tuple-element.43), channel_id=1, source_target_pairs={{0,4},{2,6},{4,0},{6,2},{1,5},{3,7},{5,1},{7,3},{8,12},{10,14},{12... | collective-permute-start | bytes 196616 | tf_op jit(solution)/shard_map/ppermute | solution.py:336
  112.7 6.6 %collective-permute-start.22 = (f32[128,128]{1,0:T(8,128)S(1)}, f32[128,128]{1,0:T(8,128)S(1)}, u32[]{:S(2)}, u32[]{:S(2)}) collective-permute-start(f32[128,128]{1,0:T(8,128)S(1)} %get-tuple-element.43), channel_id=1, source_target_pairs={{0,2},{2,4},{4,6},{6,0},{1,3},{3,5},{5,7},{7,1},{8,10},{10,12},{12... | collective-permute-start | bytes 196616 | tf_op jit(solution)/shard_map/ppermute | solution.py:336
  115.1 4.2 %collective-permute-start.23 = (f32[128,128]{1,0:T(8,128)S(1)}, f32[128,128]{1,0:T(8,128)S(1)}, u32[]{:S(2)}, u32[]{:S(2)}) collective-permute-start(f32[128,128]{1,0:T(8,128)S(1)} %get-tuple-element.43), channel_id=1, source_target_pairs={{0,6},{2,0},{4,2},{6,4},{1,7},{3,1},{5,3},{7,5},{8,14},{10,8},{12,... | collective-permute-start | bytes 196616 | tf_op jit(solution)/shard_map/ppermute | solution.py:336
  119.3 1.8 %collective-permute-start.24 = (f32[128,128]{1,0:T(8,128)S(1)}, f32[128,128]{1,0:T(8,128)S(1)}, u32[]{:S(2)}, u32[]{:S(2)}) collective-permute-start(f32[128,128]{1,0:T(8,128)S(1)} %add_add_fusion.1), channel_id=1, source_target_pairs={{0,1},{1,0},{2,3},{3,2},{4,5},{5,4},{6,7},{7,6},{8,9},{9,8},{10,11... | collective-permute-start | bytes 196616 | tf_op jit(solution)/shard_map/ppermute | solution.py:344
  121.1 4.1 %copy-start.3 = (bf16[4096,128]{1,0:T(8,128)(2,1)S(1)}, bf16[4096,128]{1,0:T(8,128)(2,1)}, u32[]{:S(2)}) copy-start(bf16[4096,128]{1,0:T(8,128)(2,1)} %wv.3) | copy-start | bytes 3145732
  121.1 4.1 %collective-permute-start.25 = (f32[128,128]{1,0:T(8,128)S(1)}, f32[128,128]{1,0:T(8,128)S(1)}, u32[]{:S(2)}, u32[]{:S(2)}) collective-permute-start(f32[128,128]{1,0:T(8,128)S(1)} %add.78.one), channel_id=1, source_target_pairs={{0,8},{8,0},{1,9},{9,1},{2,10},{10,2},{3,11},{11,3},{4,12},{12,4},... | collective-permute-start | bytes 196616 | tf_op jit(solution)/shard_map/ppermute | solution.py:344
  121.6 19.5 %collective-permute-start.34 = (bf16[2,256,384]{2,1,0:T(8,128)(2,1)S(1)}, bf16[2,256,384]{2,1,0:T(8,128)(2,1)S(1)}, u32[]{:S(2)}, u32[]{:S(2)}) collective-permute-start(bf16[2,256,384]{2,1,0:T(8,128)(2,1)S(1)} %get-tuple-element.57), channel_id=1, source_target_pairs={{0,2},{2,4},{4,6},{6,0},{1,3},{3,5},{5,7},{7,1},{8,10},{10,12},{12... | collective-permute-start | bytes 1179656 | tf_op jit(solution)/shard_map/ppermute | solution.py:336
  121.7 21.6 %collective-permute-start.35 = (bf16[2,256,384]{2,1,0:T(8,128)(2,1)S(1)}, bf16[2,256,384]{2,1,0:T(8,128)(2,1)S(1)}, u32[]{:S(2)}, u32[]{:S(2)}) collective-permute-start(bf16[2,256,384]{2,1,0:T(8,128)(2,1)S(1)} %get-tuple-element.58), channel_id=1, source_target_pairs={{0,4},{2,6},{4,0},{6,2},{1,5},{3,7},{5,1},{7,3},{8,12},{10,14},{12... | collective-permute-start | bytes 1179656 | tf_op jit(solution)/shard_map/ppermute | solution.py:336
  125.2 18.1 %collective-permute-start.36 = (bf16[2,256,384]{2,1,0:T(8,128)(2,1)S(1)}, bf16[2,256,384]{2,1,0:T(8,128)(2,1)S(1)}, u32[]{:S(2)}, u32[]{:S(2)}) collective-permute-start(bf16[2,256,384]{2,1,0:T(8,128)(2,1)S(1)} %get-tuple-element.59), channel_id=1, source_target_pairs={{0,6},{2,0},{4,2},{6,4},{1,7},{3,1},{5,3},{7,5},{8,14},{10,8},{12,... | collective-permute-start | bytes 1179656 | tf_op jit(solution)/shard_map/ppermute | solution.py:336
  126.0 5.7 %collective-permute-start.26 = (bf16[32,2048]{1,0:T(8,128)(2,1)S(1)}, bf16[32,2048]{1,0:T(8,128)(2,1)S(1)}, u32[]{:S(2)}, u32[]{:S(2)}) collective-permute-start(bf16[32,2048]{1,0:T(8,128)(2,1)S(1)} %get-tuple-element.46), channel_id=1, source_target_pairs={{0,16},{16,32},{32,48},{48,0},{1,17},{17,33},{33,49},{49,1},{2,18}... | collective-permute-start | bytes 393224 | tf_op jit(solution)/shard_map/ppermute | solution.py:336
  127.2 7.9 %collective-permute-start.27 = (bf16[32,2048]{1,0:T(8,128)(2,1)S(1)}, bf16[32,2048]{1,0:T(8,128)(2,1)S(1)}, u32[]{:S(2)}, u32[]{:S(2)}) collective-permute-start(bf16[32,2048]{1,0:T(8,128)(2,1)S(1)} %get-tuple-element.47), channel_id=1, source_target_pairs={{0,32},{16,48},{32,0},{48,16},{1,33},{17,49},{33,1},{49,17},{2,34}... | collective-permute-start | bytes 393224 | tf_op jit(solution)/shard_map/ppermute | solution.py:336
  131.7 4.1 %collective-permute-start.28 = (bf16[32,2048]{1,0:T(8,128)(2,1)S(1)}, bf16[32,2048]{1,0:T(8,128)(2,1)S(1)}, u32[]{:S(2)}, u32[]{:S(2)}) collective-permute-start(bf16[32,2048]{1,0:T(8,128)(2,1)S(1)} %get-tuple-element.48), channel_id=1, source_target_pairs={{0,48},{16,0},{32,16},{48,32},{1,49},{17,1},{33,17},{49,33},{2,50}... | collective-permute-start | bytes 393224 | tf_op jit(solution)/shard_map/ppermute | solution.py:336
  135.9 7.8 %collective-permute-start.29 = (bf16[8,2048]{1,0:T(8,128)(2,1)S(1)}, bf16[8,2048]{1,0:T(8,128)(2,1)S(1)}, u32[]{:S(2)}, u32[]{:S(2)}) collective-permute-start(bf16[8,2048]{1,0:T(8,128)(2,1)S(1)} %get-tuple-element.50), channel_id=1, source_target_pairs={{0,128},{64,192},{128,0},{192,64},{1,129},{65,193},{129,1},{193,65... | collective-permute-start | bytes 98312 | tf_op jit(solution)/shard_map/ppermute | solution.py:336
  139.7 4.9 %collective-permute-start.30 = (bf16[8,2048]{1,0:T(8,128)(2,1)S(1)}, bf16[8,2048]{1,0:T(8,128)(2,1)S(1)}, u32[]{:S(2)}, u32[]{:S(2)}) collective-permute-start(bf16[8,2048]{1,0:T(8,128)(2,1)S(1)} %get-tuple-element.51), channel_id=1, source_target_pairs={{0,64},{64,128},{128,192},{192,0},{1,65},{65,129},{129,193},{193,1... | collective-permute-start | bytes 98312 | tf_op jit(solution)/shard_map/ppermute | solution.py:336
  141.1 4.0 %collective-permute-start.31 = (bf16[8,2048]{1,0:T(8,128)(2,1)S(1)}, bf16[8,2048]{1,0:T(8,128)(2,1)S(1)}, u32[]{:S(2)}, u32[]{:S(2)}) collective-permute-start(bf16[8,2048]{1,0:T(8,128)(2,1)S(1)} %get-tuple-element.52), channel_id=1, source_target_pairs={{0,192},{64,0},{128,64},{192,128},{1,193},{65,1},{129,65},{193,129... | collective-permute-start | bytes 98312 | tf_op jit(solution)/shard_map/ppermute | solution.py:336
  143.3 8.1 %copy-start.14 = (bf16[8,4096]{1,0:T(8,128)(2,1)S(1)}, bf16[8,4096]{1,0:T(8,128)(2,1)}, u32[]{:S(2)}) copy-start(bf16[8,4096]{1,0:T(8,128)(2,1)} %context.3) | copy-start | bytes 196612
  143.6 8.6 %collective-permute-start.37 = (bf16[256,384]{1,0:T(8,128)(2,1)S(1)}, bf16[256,384]{1,0:T(8,128)(2,1)S(1)}, u32[]{:S(2)}, u32[]{:S(2)}) collective-permute-start(bf16[256,384]{1,0:T(8,128)(2,1)S(1)} %get-tuple-element.61), channel_id=1, source_target_pairs={{0,8},{8,0},{1,9},{9,1},{2,10},{10,2},{3,11},{11,3},{4,12},{12,4},... | collective-permute-start | bytes 589832 | tf_op jit(solution)/shard_map/ppermute | solution.py:344
  145.2 7.1 %copy-start.12 = (f32[128,256]{1,0:T(8,128)S(1)}, f32[128,256]{1,0:T(8,128)}, u32[]{:S(2)}) copy-start(f32[128,256]{1,0:T(8,128)} %copy-done.11) | copy-start | bytes 393220
  145.2 6.2 %collective-permute-start.32 = (f32[8,2048]{1,0:T(8,128)S(1)}, f32[8,2048]{1,0:T(8,128)S(1)}, u32[]{:S(2)}, u32[]{:S(2)}) collective-permute-start(f32[8,2048]{1,0:T(8,128)S(1)} %add_add_fusion.mine), channel_id=1, source_target_pairs={{0,1},{1,0},{2,3},{3,2},{4,5},{5,4},{6,7},{7,6},{8,9},{9,8},{10,11... | collective-permute-start | bytes 196616 | tf_op jit(solution)/shard_map/ppermute | solution.py:344

commit v3 on v2

--- a/solution.py
+++ b/solution.py
@@ -115,17 +115,13 @@
     out[tok:, :] = jnp.concatenate([part, jnp.zeros_like(part)], axis=0).astype(bf16)
 
 
-def forward_kernel(gain, partners, wq, wk, wv, wo, ctx, *refs):
+def forward_kernel(gain, partners, weights, wo, ctx, *refs):
     pieces, refs = refs[:4], refs[4:]
-    qkv, own, branch, mix, normed, ctx_columns, weights, last, stacks, sems = refs
-    pos = position()
-    fetch = [
-        pltpu.make_async_copy(w, weights.at[:, pl.ds(i * HD, HD)], sems.at[i])
-        for i, w in enumerate((wq, wk, wv))
-    ]
-    fetch.append(pltpu.make_async_copy(wo, last, sems.at[3]))
+    qkv, own, branch, mix, normed, ctx_columns, last, stacks, sems = refs
+    pos = position()
+    fetch = [pltpu.make_async_copy(wo, last, sems.at[0])]
     arrive = [
-        pltpu.make_async_copy(piece, stacks.at[i], sems.at[4 + i]) for i, piece in enumerate(pieces)
+        pltpu.make_async_copy(piece, stacks.at[i], sems.at[1 + i]) for i, piece in enumerate(pieces)
     ]
     for copy in arrive + fetch:
         copy.start()
@@ -152,8 +148,6 @@
         squares = squares + jnp.sum(rows * rows, axis=1, keepdims=True)
     inv = lax.rsqrt(squares / (16 * feat) + EPS)
     total = jnp.zeros((tok, 3 * HD), f32)
-    for copy in fetch[:3]:
-        copy.wait()
     for ref, i, along_x, along_z in blocks:
         place = ((pos[0] - along_z) & 3) * 4 + ((pos[1] - along_x) & 3)
         here = pl.ds(pl.multiple_of(place * feat, feat), feat)
@@ -172,7 +166,7 @@
     mix[:, :HD] = mean[:docs]
     mix[:, HD : 2 * HD] = dot(averaging, ctx_weights)[:docs] * DOC_LEN
     mix[:, 2 * HD :] = jnp.broadcast_to(wide(partners[...]), (docs, HD))
-    fetch[3].wait()
+    fetch[0].wait()
     branch[...] = folded(dot(stacked_pieces(mean, 3), last[...]), 3)[:docs]
 
 
@@ -380,10 +374,11 @@
 
     swap = [(c * 16 + d, d * 16 + c) for c in range(16) for d in range(16)]
     named_rows = wide(lax.ppermute(context, EVERY, swap))
-    named_rows, _ = lax.optimization_barrier((named_rows, block))
+    projections = jnp.concatenate([w_query, w_key, w_value], axis=1)
+    named_rows, _, projections = lax.optimization_barrier((named_rows, block, projections))
     inv = inverse_rms(named_rows)
     named_rows = (named_rows * inv * gain).astype(bf16)
-    few = [dot(named_rows, w_key), dot(named_rows, w_value)] + hlo_split(inv, 3)
+    few = [dot(named_rows, projections)[:, HD:]] + hlo_split(inv, 3)
     few = jnp.concatenate([a.astype(bf16) for a in few], axis=1)
     few = jnp.pad(few, ((0, 0), (0, 3 * HD - few.shape[1])))
     ctx_kv = spread(few, DP, 16).reshape(-1, 3 * HD)
@@ -398,15 +393,14 @@
             shape(tok, width, dtype=bf16),
             shape(HD, feat),
         ),
-        ["v"] * 2 + ["a"] * 4 + ["v"] + ["a"] * 4,
+        ["v"] * 3 + ["a"] + ["v"] + ["a"] * 4,
         scratch=[
-            pltpu.VMEM((width, 3 * HD), bf16),
             pltpu.VMEM((HD, width), bf16),
             pltpu.VMEM((4,) + block.shape, bf16),
-            pltpu.SemaphoreType.DMA((8,)),
+            pltpu.SemaphoreType.DMA((5,)),
         ],
         vmem=24,
-    )(gain_row, partners[:, None], w_query, w_key, w_value, w_out, ctx_kv, *rows)
+    )(gain_row, partners[:, None], projections, w_out, ctx_kv, *rows)
 
     pooled = own_mean + ring_sum(ring_sum(branch, "x"), "zh")
     message = jnp.concatenate([pooled, mix], axis=1)

time: 155 us -> 152 us (0.981)
  local copies, waits for them, and re-layouts: 8.77 us -> 5.73 us
  Pallas kernels: 14.6 us -> 16.3 us
    unnamed x32 -> x28, local copies, waits for them, and re-layouts: 7.82 us -> 4.89 us
  transfers between devices with their start and end apart: 39 -> 39, of which waited for: 21 -> 20; matrix products, arithmetic and copies ran while one was open for 1% -> 1% of each run, Pallas kernels for 2% -> 3%
where the time goes in v3:
time: 152 us; the launch traced here: 151 us
  starting transfers between devices  85.4 us (56%)
  waiting for transfers between devices  40.3 us (27%)
  Pallas kernels  16.3 us (11%)
  local copies, waits for them, and re-layouts  5.73 us (4%)
  other arithmetic  1.75 us (1%)
    ppermute x27, starting transfers between devices, shift(): return lax.ppermute(a, axis, [(i, (i + k) % 4) for i in range(4)])  54.7 us
    ppermute x27, waiting for transfers between devices, shift(): return lax.ppermute(a, axis, [(i, (i + k) % 4) for i in range(4)])  27.3 us
    ppermute x10, starting transfers between devices, other(): return lax.ppermute(a, axis, [(0, 1), (1, 0)])  16.6 us
    all_to_all x1, starting transfers between devices, spread(): return lax.all_to_all(copies, axis, 0, 0)  9.54 us
    all_to_all x1, waiting for transfers between devices, spread(): return lax.all_to_all(copies, axis, 0, 0)  5.76 us
    ppermute x10, waiting for transfers between devices, other(): return lax.ppermute(a, axis, [(0, 1), (1, 0)])  5.21 us
    pallas_call x1, Pallas kernels, shards(): call(loss_kernel, (shape(1, 1), shape(HD, feat), shape(tok, 3 * HD, dtype...  4.94 us
    unnamed x28, local copies, waits for them, and re-layouts  4.89 us
  transfers between devices with their start and end apart: 39, of which 20 were waited for; matrix products, arithmetic and copies ran while one was open for 1% of the time, Pallas kernels for 3%

profile of v3, /device:TPU:1, one launch (start us, length us, event | category | flops | bytes accessed | tf_op | source)
XLA Modules:
  0.0 150.9 jit_solution(1172502274669841945)
XLA Ops:
  0.7 1.0 copy-done.9
  1.7 0.9 shard_map.127
  2.7 3.9 %collective-permute-start.1 = (bf16[272,256]{1,0:T(8,128)(2,1)S(1)}, bf16[272,256]{1,0:T(8,128)(2,1)S(1)}, u32[]{:S(2)}, u32[]{:S(2)}) collective-permute-start(bf16[272,256]{1,0:T(8,128)(2,1)S(1)} %shard_map.127), channel_id=1, source_target_pairs={{0,64},{64,128},{128,192},{192,0},{1,65},{65,129},{129,193},{193,1... | collective-permute-start | bytes 417800 | tf_op jit(solution)/shard_map/ppermute | solution.py:330
  6.6 5.1 %collective-permute-start.2 = (bf16[272,256]{1,0:T(8,128)(2,1)S(1)}, bf16[272,256]{1,0:T(8,128)(2,1)S(1)}, u32[]{:S(2)}, u32[]{:S(2)}) collective-permute-start(bf16[272,256]{1,0:T(8,128)(2,1)S(1)} %shard_map.127), channel_id=1, source_target_pairs={{0,128},{64,192},{128,0},{192,64},{1,129},{65,193},{129,1},{193,65... | collective-permute-start | bytes 417800 | tf_op jit(solution)/shard_map/ppermute | solution.py:330
  11.7 2.4 %collective-permute-start.3 = (bf16[272,256]{1,0:T(8,128)(2,1)S(1)}, bf16[272,256]{1,0:T(8,128)(2,1)S(1)}, u32[]{:S(2)}, u32[]{:S(2)}) collective-permute-start(bf16[272,256]{1,0:T(8,128)(2,1)S(1)} %shard_map.127), channel_id=1, source_target_pairs={{0,192},{64,0},{128,64},{192,128},{1,193},{65,1},{129,65},{193,129... | collective-permute-start | bytes 417800 | tf_op jit(solution)/shard_map/ppermute | solution.py:330
  14.1 4.5 %collective-permute-start = (bf16[8,4096]{1,0:T(8,128)(2,1)}, bf16[8,4096]{1,0:T(8,128)(2,1)S(1)}, u32[]{:S(2)}, u32[]{:S(2)}) collective-permute-start(bf16[8,4096]{1,0:T(8,128)(2,1)} %context.3), channel_id=1, source_target_pairs={{0,0},{1,16},{2,32},{3,48},{4,64},{5,80},{6,96},{7,112},{8,128},{9... | collective-permute-start | bytes 196616 | tf_op jit(solution)/shard_map/ppermute | solution.py:376
  18.6 0.4 pad_maximum_fusion.weights
  19.0 2.0 %collective-permute-done = bf16[8,4096]{1,0:T(8,128)(2,1)S(1)} collective-permute-done((bf16[8,4096]{1,0:T(8,128)(2,1)}, bf16[8,4096]{1,0:T(8,128)(2,1)S(1)}, u32[]{:S(2)}, u32[]{:S(2)}) %collective-permute-start) | collective-permute-done | bytes 65568 | tf_op jit(solution)/shard_map/ppermute | solution.py:376
  21.0 4.3 %collective-permute-done.3 = bf16[272,256]{1,0:T(8,128)(2,1)S(1)} collective-permute-done((bf16[272,256]{1,0:T(8,128)(2,1)S(1)}, bf16[272,256]{1,0:T(8,128)(2,1)S(1)}, u32[]{:S(2)}, u32[]{:S(2)}) %collective-permute-start.3) | collective-permute-done | bytes 139296 | tf_op jit(solution)/shard_map/ppermute | solution.py:330
  25.3 0.9 pad_maximum_fusion.1.refs_0_
  26.2 1.2 collective-permute-start.4
  27.4 2.5 %collective-permute-start.5 = (bf16[4,272,256]{2,1,0:T(8,128)(2,1)}, bf16[4,272,256]{2,1,0:T(8,128)(2,1)}, u32[]{:S(2)}, u32[]{:S(2)}) collective-permute-start(bf16[4,272,256]{2,1,0:T(8,128)(2,1)} %pad_maximum_fusion.1.refs_0_), channel_id=1, source_target_pairs={{0,32},{16,48},{32,0},{48,16},{1,33},{17,49},{33,1},{49,17},{2,34}... | collective-permute-start | bytes 1671176 | tf_op jit(solution)/shard_map/ppermute | solution.py:330
  29.9 1.2 collective-permute-start.6
  31.2 0.5 fusion
  31.9 0.7 broadcast_in_dim.6
  32.6 9.5 %all-to-all-start = ((bf16[16,8,384]{2,1,0:T(8,128)(2,1)}), bf16[16,8,384]{2,1,0:T(8,128)(2,1)S(1)}, u32[]{:S(2)}, u32[]{:S(2)}) async-start(bf16[16,8,384]{2,1,0:T(8,128)(2,1)} %broadcast_in_dim.6), calls=%async_computation | async-start | bytes 196608 | tf_op jit(solution)/shard_map/all_to_all | solution.py:362
  42.2 5.8 %all-to-all-done = bf16[16,8,384]{2,1,0:T(8,128)(2,1)S(1)} async-done(((bf16[16,8,384]{2,1,0:T(8,128)(2,1)}), bf16[16,8,384]{2,1,0:T(8,128)(2,1)S(1)}, u32[]{:S(2)}, u32[]{:S(2)}) %all-to-all-start) | async-done | bytes 98336 | tf_op jit(solution)/shard_map/all_to_all | solution.py:362
  48.0 6.3 %collective-permute-done.5.refs_2_ = bf16[4,272,256]{2,1,0:T(8,128)(2,1)} collective-permute-done((bf16[4,272,256]{2,1,0:T(8,128)(2,1)}, bf16[4,272,256]{2,1,0:T(8,128)(2,1)}, u32[]{:S(2)}, u32[]{:S(2)}) %collective-permute-start.5) | collective-permute-done | bytes 557088 | tf_op jit(solution)/shard_map/ppermute | solution.py:330
  54.2 1.2 copy-done.2
  55.5 4.7 %shard_map.128 = (bf16[256,384]{1,0:T(8,128)(2,1)S(1)}, f32[4,4096]{1,0:T(4,128)S(1)}, f32[4,4096]{1,0:T(4,128)S(1)}, f32[4,384]{1,0:T(4,128)S(1)}, bf16[256,409...) custom-call(f32[1,4096]{1,0:T(1,128)S(1)} %bitcast.14, s32[4,1]{1,0:T(4,128)S(1)} %copy.16.partners, ...), custom_call_target="tpu_custom_call" | custom-call | flops 1000000000 | tf_op jit(solution)/shard_map/pallas_call | solution.py:386
  60.2 1.3 copy-done
  61.6 2.1 %collective-permute-start.7 = (f32[4,4096]{1,0:T(4,128)S(1)}, f32[4,4096]{1,0:T(4,128)S(1)}, u32[]{:S(2)}, u32[]{:S(2)}) collective-permute-start(f32[4,4096]{1,0:T(4,128)S(1)} %get-tuple-element.42), channel_id=1, source_target_pairs={{0,32},{16,48},{32,0},{48,16},{1,33},{17,49},{33,1},{49,17},{2,34}... | collective-permute-start | bytes 196616 | tf_op jit(solution)/shard_map/ppermute | solution.py:330
  63.7 1.4 collective-permute-start.8
  65.1 1.3 collective-permute-start.9
  66.4 2.5 %collective-permute-done.8 = f32[4,4096]{1,0:T(4,128)S(1)} collective-permute-done((f32[4,4096]{1,0:T(4,128)S(1)}, f32[4,4096]{1,0:T(4,128)S(1)}, u32[]{:S(2)}, u32[]{:S(2)}) %collective-permute-start.8) | collective-permute-done | bytes 65568 | tf_op jit(solution)/shard_map/ppermute | solution.py:330
  68.9 4.1 %collective-permute-start.10 = (f32[4,4096]{1,0:T(4,128)S(1)}, f32[4,4096]{1,0:T(4,128)S(1)}, u32[]{:S(2)}, u32[]{:S(2)}) collective-permute-start(f32[4,4096]{1,0:T(4,128)S(1)} %add_add_fusion.3), channel_id=1, source_target_pairs={{0,128},{64,192},{128,0},{192,64},{1,129},{65,193},{129,1},{193,65... | collective-permute-start | bytes 196616 | tf_op jit(solution)/shard_map/ppermute | solution.py:330
  73.0 7.0 %collective-permute-start.11 = (f32[4,4096]{1,0:T(4,128)S(1)}, f32[4,4096]{1,0:T(4,128)S(1)}, u32[]{:S(2)}, u32[]{:S(2)}) collective-permute-start(f32[4,4096]{1,0:T(4,128)S(1)} %add_add_fusion.3), channel_id=1, source_target_pairs={{0,64},{64,128},{128,192},{192,0},{1,65},{65,129},{129,193},{193,1... | collective-permute-start | bytes 196616 | tf_op jit(solution)/shard_map/ppermute | solution.py:330
  80.0 1.7 %collective-permute-done.11 = f32[4,4096]{1,0:T(4,128)S(1)} collective-permute-done((f32[4,4096]{1,0:T(4,128)S(1)}, f32[4,4096]{1,0:T(4,128)S(1)}, u32[]{:S(2)}, u32[]{:S(2)}) %collective-permute-start.11) | collective-permute-done | bytes 65568 | tf_op jit(solution)/shard_map/ppermute | solution.py:330
  81.7 2.6 %collective-permute-done.12 = f32[4,4096]{1,0:T(4,128)S(1)} collective-permute-done((f32[4,4096]{1,0:T(4,128)S(1)}, f32[4,4096]{1,0:T(4,128)S(1)}, u32[]{:S(2)}, u32[]{:S(2)}) %collective-permute-start.12) | collective-permute-done | bytes 65568 | tf_op jit(solution)/shard_map/ppermute | solution.py:330
  84.5 3.2 %collective-permute-done.13 = f32[4,4480]{1,0:T(4,128)S(1)} collective-permute-done((f32[4,4480]{1,0:T(4,128)S(1)}, f32[4,4480]{1,0:T(4,128)S(1)}, u32[]{:S(2)}, u32[]{:S(2)}) %collective-permute-start.13) | collective-permute-done | bytes 71712 | tf_op jit(solution)/shard_map/ppermute | solution.py:338
  87.7 0.4 collective-permute-start.14
  88.1 1.8 %collective-permute-start.15 = (f32[8,4480]{1,0:T(8,128)S(1)}, f32[8,4480]{1,0:T(8,128)S(1)}, u32[]{:S(2)}, u32[]{:S(2)}) collective-permute-start(f32[8,4480]{1,0:T(8,128)S(1)} %maximum_select_fusion.refs_0_), channel_id=1, source_target_pairs={{0,4},{2,6},{4,0},{6,2},{1,5},{3,7},{5,1},{7,3},{8,12},{10,14},{12... | collective-permute-start | bytes 430088 | tf_op jit(solution)/shard_map/ppermute | solution.py:330
  89.9 0.7 collective-permute-start.16
  90.6 4.8 %collective-permute-start.17 = (f32[8,4480]{1,0:T(8,128)S(1)}, f32[8,4480]{1,0:T(8,128)S(1)}, u32[]{:S(2)}, u32[]{:S(2)}) collective-permute-start(f32[8,4480]{1,0:T(8,128)S(1)} %maximum_select_fusion.refs_0_), channel_id=1, source_target_pairs={{0,1},{1,0},{2,3},{3,2},{4,5},{5,4},{6,7},{7,6},{8,9},{9,8},{10,11... | collective-permute-start | bytes 430088 | tf_op jit(solution)/shard_map/ppermute | solution.py:338
  95.5 4.5 %collective-permute-start.18 = (f32[8,4480]{1,0:T(8,128)S(1)}, f32[8,4480]{1,0:T(8,128)S(1)}, u32[]{:S(2)}, u32[]{:S(2)}) collective-permute-start(f32[8,4480]{1,0:T(8,128)S(1)} %collective-permute-done.14.refs_1_), channel_id=1, source_target_pairs={{0,1},{1,0},{2,3},{3,2},{4,5},{5,4},{6,7},{7,6},{8,9},{9,8},{10,11... | collective-permute-start | bytes 430088 | tf_op jit(solution)/shard_map/ppermute | solution.py:338
  100.0 0.9 collective-permute-start.20
  101.3 0.5 collective-permute-done.20.refs_7_
  101.9 1.2 copy-done.3
  103.1 4.9 %shard_map.129 = (f32[1,1]{1,0:T(1,128)}, f32[128,256]{1,0:T(8,128)}, bf16[256,384]{1,0:T(8,128)(2,1)S(1)}, f32[128,128]{1,0:T(8,128)S(1)}, f32[128,128]{1,0:T(8,128)S(1)}) custom-call(bf16[128,4096]{1,0:T(8,128)(2,1)S(1)} %copy-done.3, bf16[128,384]{1,0:T(8,128)(2,1)S(1)} %bitcast.12, bf16[256,384]{1,0:T(8,128)(2,1)S(1)} %get-tuple-element.40.own, ...), custom_call_target="tpu_custom_call" | custom-call | flops 1000000000 | tf_op jit(solution)/shard_map/pallas_call | solution.py:410
  108.0 0.8 shard_map.134
  108.8 0.5 collective-permute-start.33
  109.3 0.4 collective-permute-start.21
  109.7 2.4 %collective-permute-start.22 = (f32[128,128]{1,0:T(8,128)S(1)}, f32[128,128]{1,0:T(8,128)S(1)}, u32[]{:S(2)}, u32[]{:S(2)}) collective-permute-start(f32[128,128]{1,0:T(8,128)S(1)} %get-tuple-element.45), channel_id=1, source_target_pairs={{0,2},{2,4},{4,6},{6,0},{1,3},{3,5},{5,7},{7,1},{8,10},{10,12},{12... | collective-permute-start | bytes 196616 | tf_op jit(solution)/shard_map/ppermute | solution.py:330
  112.3 2.0 %collective-permute-done.21 = f32[128,128]{1,0:T(8,128)S(1)} collective-permute-done((f32[128,128]{1,0:T(8,128)S(1)}, f32[128,128]{1,0:T(8,128)S(1)}, u32[]{:S(2)}, u32[]{:S(2)}) %collective-permute-start.21) | collective-permute-done | bytes 65568 | tf_op jit(solution)/shard_map/ppermute | solution.py:330
  114.3 1.9 %collective-permute-done.22 = f32[128,128]{1,0:T(8,128)S(1)} collective-permute-done((f32[128,128]{1,0:T(8,128)S(1)}, f32[128,128]{1,0:T(8,128)S(1)}, u32[]{:S(2)}, u32[]{:S(2)}) %collective-permute-start.22) | collective-permute-done | bytes 65568 | tf_op jit(solution)/shard_map/ppermute | solution.py:330
  116.3 0.9 collective-permute-start.24
  117.1 0.8 shard_map.133.mine
  118.6 3.5 %collective-permute-start.35 = (bf16[2,256,384]{2,1,0:T(8,128)(2,1)S(1)}, bf16[2,256,384]{2,1,0:T(8,128)(2,1)S(1)}, u32[]{:S(2)}, u32[]{:S(2)}) collective-permute-start(bf16[2,256,384]{2,1,0:T(8,128)(2,1)S(1)} %get-tuple-element.60), channel_id=1, source_target_pairs={{0,4},{2,6},{4,0},{6,2},{1,5},{3,7},{5,1},{7,3},{8,12},{10,14},{12... | collective-permute-start | bytes 1179656 | tf_op jit(solution)/shard_map/ppermute | solution.py:330
  122.2 0.8 shard_map.130
  122.9 1.2 collective-permute-start.26
  124.1 3.0 %collective-permute-start.27 = (bf16[32,2048]{1,0:T(8,128)(2,1)S(1)}, bf16[32,2048]{1,0:T(8,128)(2,1)S(1)}, u32[]{:S(2)}, u32[]{:S(2)}) collective-permute-start(bf16[32,2048]{1,0:T(8,128)(2,1)S(1)} %get-tuple-element.49), channel_id=1, source_target_pairs={{0,32},{16,48},{32,0},{48,16},{1,33},{17,49},{33,1},{49,17},{2,34}... | collective-permute-start | bytes 393224 | tf_op jit(solution)/shard_map/ppermute | solution.py:330
  127.2 1.5 collective-permute-done.26.one
  128.6 1.5 collective-permute-start.28
  130.1 1.9 %collective-permute-done.27.two = bf16[32,2048]{1,0:T(8,128)(2,1)S(1)} collective-permute-done((bf16[32,2048]{1,0:T(8,128)(2,1)S(1)}, bf16[32,2048]{1,0:T(8,128)(2,1)S(1)}, u32[]{:S(2)}, u32[]{:S(2)}) %collective-permute-start.27) | collective-permute-done | bytes 131104 | tf_op jit(solution)/shard_map/ppermute | solution.py:330
  132.0 0.7 collective-permute-done.28.three
  132.8 3.8 %collective-permute-start.29 = (bf16[8,2048]{1,0:T(8,128)(2,1)S(1)}, bf16[8,2048]{1,0:T(8,128)(2,1)S(1)}, u32[]{:S(2)}, u32[]{:S(2)}) collective-permute-start(bf16[8,2048]{1,0:T(8,128)(2,1)S(1)} %get-tuple-element.52), channel_id=1, source_target_pairs={{0,128},{64,192},{128,0},{192,64},{1,129},{65,193},{129,1},{193,65... | collective-permute-start | bytes 98312 | tf_op jit(solution)/shard_map/ppermute | solution.py:330
  136.7 1.7 %collective-permute-start.30 = (bf16[8,2048]{1,0:T(8,128)(2,1)S(1)}, bf16[8,2048]{1,0:T(8,128)(2,1)S(1)}, u32[]{:S(2)}, u32[]{:S(2)}) collective-permute-start(bf16[8,2048]{1,0:T(8,128)(2,1)S(1)} %get-tuple-element.53), channel_id=1, source_target_pairs={{0,64},{64,128},{128,192},{192,0},{1,65},{65,129},{129,193},{193,1... | collective-permute-start | bytes 98312 | tf_op jit(solution)/shard_map/ppermute | solution.py:330
  138.3 1.9 %collective-permute-start.31 = (bf16[8,2048]{1,0:T(8,128)(2,1)S(1)}, bf16[8,2048]{1,0:T(8,128)(2,1)S(1)}, u32[]{:S(2)}, u32[]{:S(2)}) collective-permute-start(bf16[8,2048]{1,0:T(8,128)(2,1)S(1)} %get-tuple-element.54), channel_id=1, source_target_pairs={{0,192},{64,0},{128,64},{192,128},{1,193},{65,1},{129,65},{193,129... | collective-permute-start | bytes 98312 | tf_op jit(solution)/shard_map/ppermute | solution.py:330
  140.7 0.9 collective-permute-done.30
  141.6 1.1 collective-permute-done.31
  142.7 4.8 %collective-permute-start.32 = (f32[8,2048]{1,0:T(8,128)S(1)}, f32[8,2048]{1,0:T(8,128)S(1)}, u32[]{:S(2)}, u32[]{:S(2)}) collective-permute-start(f32[8,2048]{1,0:T(8,128)S(1)} %add_add_fusion.mine), channel_id=1, source_target_pairs={{0,1},{1,0},{2,3},{3,2},{4,5},{5,4},{6,7},{7,6},{8,9},{9,8},{10,11... | collective-permute-start | bytes 196616 | tf_op jit(solution)/shard_map/ppermute | solution.py:338
  147.4 0.9 collective-permute-done.32.theirs
  148.3 1.6 %shard_map.132 = f32[8,4096]{1,0:T(8,128)} custom-call(bf16[8,4096]{1,0:T(8,128)(2,1)} %context.3, f32[1,4096]{1,0:T(1,128)S(1)} %bitcast.15, f32[8,2048]{1,0:T(8,128)S(1)} %add_add_fusion.mine, f32[8,2048]{1,0:T(8,128)S(1)} %collective-permute-done.32.theirs), custom_call_target="tpu_custom_call" | custom-call | flops 1000000000 | tf_op jit(solution)/shard_map/pallas_call | solution.py:451
  150.0 1.0 shard_map.137
  (72 shorter events, 2.8 us)
Async XLA Ops:
  0.6 17.9 %copy-start.6 = (bf16[4096,128]{1,0:T(8,128)(2,1)S(1)}, bf16[4096,128]{1,0:T(8,128)(2,1)}, u32[]{:S(2)}) copy-start(bf16[4096,128]{1,0:T(8,128)(2,1)} %wk.1) | copy-start | bytes 3145732
  0.6 17.9 %copy-start.4 = (bf16[4096,128]{1,0:T(8,128)(2,1)S(1)}, bf16[4096,128]{1,0:T(8,128)(2,1)}, u32[]{:S(2)}) copy-start(bf16[4096,128]{1,0:T(8,128)(2,1)} %wv.1) | copy-start | bytes 3145732
  0.7 1.1 copy-start.9
  1.7 16.9 %copy-start.12 = (bf16[4096,128]{1,0:T(8,128)(2,1)S(1)}, bf16[4096,128]{1,0:T(8,128)(2,1)}, u32[]{:S(2)}) copy-start(bf16[4096,128]{1,0:T(8,128)(2,1)} %param.11) | copy-start | bytes 3145732
  2.7 28.5 %copy-start.8 = (f32[4096]{0:T(1024)S(1)}, f32[4096]{0:T(1024)}, u32[]{:S(2)}) copy-start(f32[4096]{0:T(1024)} %param.10) | copy-start | bytes 49156
  2.7 18.4 %collective-permute-start.1 = (bf16[272,256]{1,0:T(8,128)(2,1)S(1)}, bf16[272,256]{1,0:T(8,128)(2,1)S(1)}, u32[]{:S(2)}, u32[]{:S(2)}) collective-permute-start(bf16[272,256]{1,0:T(8,128)(2,1)S(1)} %shard_map.127), channel_id=1, source_target_pairs={{0,64},{64,128},{128,192},{192,0},{1,65},{65,129},{129,193},{193,1... | collective-permute-start | bytes 417800 | tf_op jit(solution)/shard_map/ppermute | solution.py:330
  6.6 14.5 %collective-permute-start.2 = (bf16[272,256]{1,0:T(8,128)(2,1)S(1)}, bf16[272,256]{1,0:T(8,128)(2,1)S(1)}, u32[]{:S(2)}, u32[]{:S(2)}) collective-permute-start(bf16[272,256]{1,0:T(8,128)(2,1)S(1)} %shard_map.127), channel_id=1, source_target_pairs={{0,128},{64,192},{128,0},{192,64},{1,129},{65,193},{129,1},{193,65... | collective-permute-start | bytes 417800 | tf_op jit(solution)/shard_map/ppermute | solution.py:330
  11.7 13.6 %collective-permute-start.3 = (bf16[272,256]{1,0:T(8,128)(2,1)S(1)}, bf16[272,256]{1,0:T(8,128)(2,1)S(1)}, u32[]{:S(2)}, u32[]{:S(2)}) collective-permute-start(bf16[272,256]{1,0:T(8,128)(2,1)S(1)} %shard_map.127), channel_id=1, source_target_pairs={{0,192},{64,0},{128,64},{192,128},{1,193},{65,1},{129,65},{193,129... | collective-permute-start | bytes 417800 | tf_op jit(solution)/shard_map/ppermute | solution.py:330
  14.1 7.0 %collective-permute-start = (bf16[8,4096]{1,0:T(8,128)(2,1)}, bf16[8,4096]{1,0:T(8,128)(2,1)S(1)}, u32[]{:S(2)}, u32[]{:S(2)}) collective-permute-start(bf16[8,4096]{1,0:T(8,128)(2,1)} %context.3), channel_id=1, source_target_pairs={{0,0},{1,16},{2,32},{3,48},{4,64},{5,80},{6,96},{7,112},{8,128},{9... | collective-permute-start | bytes 196616 | tf_op jit(solution)/shard_map/ppermute | solution.py:376
  19.0 23.1 %copy-start.13 = (s32[4]{0:T(128)S(1)}, s32[4]{0:T(128)}, u32[]{:S(2)}) copy-start(s32[4]{0:T(128)} %param.15) | copy-start | bytes 52
  26.2 21.8 %collective-permute-start.4 = (bf16[4,272,256]{2,1,0:T(8,128)(2,1)}, bf16[4,272,256]{2,1,0:T(8,128)(2,1)}, u32[]{:S(2)}, u32[]{:S(2)}) collective-permute-start(bf16[4,272,256]{2,1,0:T(8,128)(2,1)} %pad_maximum_fusion.1.refs_0_), channel_id=1, source_target_pairs={{0,16},{16,32},{32,48},{48,0},{1,17},{17,33},{33,49},{49,1},{2,18}... | collective-permute-start | bytes 1671176 | tf_op jit(solution)/shard_map/ppermute | solution.py:330
  27.4 26.8 %collective-permute-start.5 = (bf16[4,272,256]{2,1,0:T(8,128)(2,1)}, bf16[4,272,256]{2,1,0:T(8,128)(2,1)}, u32[]{:S(2)}, u32[]{:S(2)}) collective-permute-start(bf16[4,272,256]{2,1,0:T(8,128)(2,1)} %pad_maximum_fusion.1.refs_0_), channel_id=1, source_target_pairs={{0,32},{16,48},{32,0},{48,16},{1,33},{17,49},{33,1},{49,17},{2,34}... | collective-permute-start | bytes 1671176 | tf_op jit(solution)/shard_map/ppermute | solution.py:330
  29.9 24.4 %collective-permute-start.6 = (bf16[4,272,256]{2,1,0:T(8,128)(2,1)}, bf16[4,272,256]{2,1,0:T(8,128)(2,1)}, u32[]{:S(2)}, u32[]{:S(2)}) collective-permute-start(bf16[4,272,256]{2,1,0:T(8,128)(2,1)} %pad_maximum_fusion.1.refs_0_), channel_id=1, source_target_pairs={{0,48},{16,0},{32,16},{48,32},{1,49},{17,1},{33,17},{49,33},{2,50}... | collective-permute-start | bytes 1671176 | tf_op jit(solution)/shard_map/ppermute | solution.py:330
  32.6 15.4 %all-to-all-start = ((bf16[16,8,384]{2,1,0:T(8,128)(2,1)}), bf16[16,8,384]{2,1,0:T(8,128)(2,1)S(1)}, u32[]{:S(2)}, u32[]{:S(2)}) async-start(bf16[16,8,384]{2,1,0:T(8,128)(2,1)} %broadcast_in_dim.6), calls=%async_computation | async-start | bytes 196608 | tf_op jit(solution)/shard_map/all_to_all | solution.py:362
  54.2 1.2 copy-start.2
  60.2 1.4 copy-start
  61.6 22.8 %copy-start.10 = (f32[128,256]{1,0:T(8,128)}, f32[128,256]{1,0:T(8,128)S(1)}, u32[]{:S(2)}) copy-start(f32[128,256]{1,0:T(8,128)S(1)} %get-tuple-element.64.ctx_columns) | copy-start | bytes 393220
  61.6 46.5 %copy-start.1 = (bf16[256,4096]{1,0:T(8,128)(2,1)S(1)}, bf16[256,4096]{1,0:T(8,128)(2,1)}, u32[]{:S(2)}) copy-start(bf16[256,4096]{1,0:T(8,128)(2,1)} %copy-done) | copy-start | bytes 6291460
  61.6 4.8 %collective-permute-start.7 = (f32[4,4096]{1,0:T(4,128)S(1)}, f32[4,4096]{1,0:T(4,128)S(1)}, u32[]{:S(2)}, u32[]{:S(2)}) collective-permute-start(f32[4,4096]{1,0:T(4,128)S(1)} %get-tuple-element.42), channel_id=1, source_target_pairs={{0,32},{16,48},{32,0},{48,16},{1,33},{17,49},{33,1},{49,17},{2,34}... | collective-permute-start | bytes 196616 | tf_op jit(solution)/shard_map/ppermute | solution.py:330
  63.7 5.2 %collective-permute-start.8 = (f32[4,4096]{1,0:T(4,128)S(1)}, f32[4,4096]{1,0:T(4,128)S(1)}, u32[]{:S(2)}, u32[]{:S(2)}) collective-permute-start(f32[4,4096]{1,0:T(4,128)S(1)} %get-tuple-element.42), channel_id=1, source_target_pairs={{0,16},{16,32},{32,48},{48,0},{1,17},{17,33},{33,49},{49,1},{2,18}... | collective-permute-start | bytes 196616 | tf_op jit(solution)/shard_map/ppermute | solution.py:330
  65.1 3.8 %collective-permute-start.9 = (f32[4,4096]{1,0:T(4,128)S(1)}, f32[4,4096]{1,0:T(4,128)S(1)}, u32[]{:S(2)}, u32[]{:S(2)}) collective-permute-start(f32[4,4096]{1,0:T(4,128)S(1)} %get-tuple-element.42), channel_id=1, source_target_pairs={{0,48},{16,0},{32,16},{48,32},{1,49},{17,1},{33,17},{49,33},{2,50}... | collective-permute-start | bytes 196616 | tf_op jit(solution)/shard_map/ppermute | solution.py:330
  68.9 11.1 %collective-permute-start.10 = (f32[4,4096]{1,0:T(4,128)S(1)}, f32[4,4096]{1,0:T(4,128)S(1)}, u32[]{:S(2)}, u32[]{:S(2)}) collective-permute-start(f32[4,4096]{1,0:T(4,128)S(1)} %add_add_fusion.3), channel_id=1, source_target_pairs={{0,128},{64,192},{128,0},{192,64},{1,129},{65,193},{129,1},{193,65... | collective-permute-start | bytes 196616 | tf_op jit(solution)/shard_map/ppermute | solution.py:330
  73.0 8.7 %collective-permute-start.11 = (f32[4,4096]{1,0:T(4,128)S(1)}, f32[4,4096]{1,0:T(4,128)S(1)}, u32[]{:S(2)}, u32[]{:S(2)}) collective-permute-start(f32[4,4096]{1,0:T(4,128)S(1)} %add_add_fusion.3), channel_id=1, source_target_pairs={{0,64},{64,128},{128,192},{192,0},{1,65},{65,129},{129,193},{193,1... | collective-permute-start | bytes 196616 | tf_op jit(solution)/shard_map/ppermute | solution.py:330
  80.0 4.3 %collective-permute-start.12 = (f32[4,4096]{1,0:T(4,128)S(1)}, f32[4,4096]{1,0:T(4,128)S(1)}, u32[]{:S(2)}, u32[]{:S(2)}) collective-permute-start(f32[4,4096]{1,0:T(4,128)S(1)} %add_add_fusion.3), channel_id=1, source_target_pairs={{0,192},{64,0},{128,64},{192,128},{1,193},{65,1},{129,65},{193,129... | collective-permute-start | bytes 196616 | tf_op jit(solution)/shard_map/ppermute | solution.py:330
  84.4 3.3 %collective-permute-start.13 = (f32[4,4480]{1,0:T(4,128)S(1)}, f32[4,4480]{1,0:T(4,128)S(1)}, u32[]{:S(2)}, u32[]{:S(2)}) collective-permute-start(f32[4,4480]{1,0:T(4,128)S(1)} %pad_maximum_fusion.2), channel_id=1, source_target_pairs={{0,8},{8,0},{1,9},{9,1},{2,10},{10,2},{3,11},{11,3},{4,12},{12,4},... | collective-permute-start | bytes 215048 | tf_op jit(solution)/shard_map/ppermute | solution.py:338
  87.7 7.7 %collective-permute-start.14 = (f32[8,4480]{1,0:T(8,128)S(1)}, f32[8,4480]{1,0:T(8,128)S(1)}, u32[]{:S(2)}, u32[]{:S(2)}) collective-permute-start(f32[8,4480]{1,0:T(8,128)S(1)} %maximum_select_fusion.refs_0_), channel_id=1, source_target_pairs={{0,2},{2,4},{4,6},{6,0},{1,3},{3,5},{5,7},{7,1},{8,10},{10,12},{12... | collective-permute-start | bytes 430088 | tf_op jit(solution)/shard_map/ppermute | solution.py:330
  88.1 11.8 %collective-permute-start.15 = (f32[8,4480]{1,0:T(8,128)S(1)}, f32[8,4480]{1,0:T(8,128)S(1)}, u32[]{:S(2)}, u32[]{:S(2)}) collective-permute-start(f32[8,4480]{1,0:T(8,128)S(1)} %maximum_select_fusion.refs_0_), channel_id=1, source_target_pairs={{0,4},{2,6},{4,0},{6,2},{1,5},{3,7},{5,1},{7,3},{8,12},{10,14},{12... | collective-permute-start | bytes 430088 | tf_op jit(solution)/shard_map/ppermute | solution.py:330
  89.9 10.1 %collective-permute-start.16 = (f32[8,4480]{1,0:T(8,128)S(1)}, f32[8,4480]{1,0:T(8,128)S(1)}, u32[]{:S(2)}, u32[]{:S(2)}) collective-permute-start(f32[8,4480]{1,0:T(8,128)S(1)} %maximum_select_fusion.refs_0_), channel_id=1, source_target_pairs={{0,6},{2,0},{4,2},{6,4},{1,7},{3,1},{5,3},{7,5},{8,14},{10,8},{12,... | collective-permute-start | bytes 430088 | tf_op jit(solution)/shard_map/ppermute | solution.py:330
  90.6 10.2 %collective-permute-start.17 = (f32[8,4480]{1,0:T(8,128)S(1)}, f32[8,4480]{1,0:T(8,128)S(1)}, u32[]{:S(2)}, u32[]{:S(2)}) collective-permute-start(f32[8,4480]{1,0:T(8,128)S(1)} %maximum_select_fusion.refs_0_), channel_id=1, source_target_pairs={{0,1},{1,0},{2,3},{3,2},{4,5},{5,4},{6,7},{7,6},{8,9},{9,8},{10,11... | collective-permute-start | bytes 430088 | tf_op jit(solution)/shard_map/ppermute | solution.py:338
  95.5 5.5 %collective-permute-start.18 = (f32[8,4480]{1,0:T(8,128)S(1)}, f32[8,4480]{1,0:T(8,128)S(1)}, u32[]{:S(2)}, u32[]{:S(2)}) collective-permute-start(f32[8,4480]{1,0:T(8,128)S(1)} %collective-permute-done.14.refs_1_), channel_id=1, source_target_pairs={{0,1},{1,0},{2,3},{3,2},{4,5},{5,4},{6,7},{7,6},{8,9},{9,8},{10,11... | collective-permute-start | bytes 430088 | tf_op jit(solution)/shard_map/ppermute | solution.py:338
  100.0 1.4 collective-permute-start.19
  100.0 1.9 %collective-permute-start.20 = (f32[8,4480]{1,0:T(8,128)S(1)}, f32[8,4480]{1,0:T(8,128)S(1)}, u32[]{:S(2)}, u32[]{:S(2)}) collective-permute-start(f32[8,4480]{1,0:T(8,128)S(1)} %collective-permute-done.16.refs_3_), channel_id=1, source_target_pairs={{0,1},{1,0},{2,3},{3,2},{4,5},{5,4},{6,7},{7,6},{8,9},{9,8},{10,11... | collective-permute-start | bytes 430088 | tf_op jit(solution)/shard_map/ppermute | solution.py:338
  101.9 1.2 copy-start.3
  108.8 9.3 %collective-permute-start.33 = (bf16[8,256,384]{2,1,0:T(8,128)(2,1)S(1)}, bf16[8,256,384]{2,1,0:T(8,128)(2,1)S(1)}, u32[]{:S(2)}, u32[]{:S(2)}) collective-permute-start(bf16[8,256,384]{2,1,0:T(8,128)(2,1)S(1)} %shard_map.134), channel_id=1, source_target_pairs={{0,1},{1,0},{2,3},{3,2},{4,5},{5,4},{6,7},{7,6},{8,9},{9,8},{10,11... | collective-permute-start | bytes 4718600 | tf_op jit(solution)/shard_map/ppermute | solution.py:338
  109.3 5.1 %collective-permute-start.21 = (f32[128,128]{1,0:T(8,128)S(1)}, f32[128,128]{1,0:T(8,128)S(1)}, u32[]{:S(2)}, u32[]{:S(2)}) collective-permute-start(f32[128,128]{1,0:T(8,128)S(1)} %get-tuple-element.45), channel_id=1, source_target_pairs={{0,4},{2,6},{4,0},{6,2},{1,5},{3,7},{5,1},{7,3},{8,12},{10,14},{12... | collective-permute-start | bytes 196616 | tf_op jit(solution)/shard_map/ppermute | solution.py:330
  109.7 6.5 %collective-permute-start.22 = (f32[128,128]{1,0:T(8,128)S(1)}, f32[128,128]{1,0:T(8,128)S(1)}, u32[]{:S(2)}, u32[]{:S(2)}) collective-permute-start(f32[128,128]{1,0:T(8,128)S(1)} %get-tuple-element.45), channel_id=1, source_target_pairs={{0,2},{2,4},{4,6},{6,0},{1,3},{3,5},{5,7},{7,1},{8,10},{10,12},{12... | collective-permute-start | bytes 196616 | tf_op jit(solution)/shard_map/ppermute | solution.py:330
  112.0 4.2 %collective-permute-start.23 = (f32[128,128]{1,0:T(8,128)S(1)}, f32[128,128]{1,0:T(8,128)S(1)}, u32[]{:S(2)}, u32[]{:S(2)}) collective-permute-start(f32[128,128]{1,0:T(8,128)S(1)} %get-tuple-element.45), channel_id=1, source_target_pairs={{0,6},{2,0},{4,2},{6,4},{1,7},{3,1},{5,3},{7,5},{8,14},{10,8},{12,... | collective-permute-start | bytes 196616 | tf_op jit(solution)/shard_map/ppermute | solution.py:330
  116.2 5.9 %copy-start.5 = (bf16[4096,128]{1,0:T(8,128)(2,1)S(1)}, bf16[4096,128]{1,0:T(8,128)(2,1)}, u32[]{:S(2)}) copy-start(bf16[4096,128]{1,0:T(8,128)(2,1)} %wv.1) | copy-start | bytes 3145732
  116.2 5.9 %copy-start.7 = (bf16[4096,128]{1,0:T(8,128)(2,1)S(1)}, bf16[4096,128]{1,0:T(8,128)(2,1)}, u32[]{:S(2)}) copy-start(bf16[4096,128]{1,0:T(8,128)(2,1)} %wk.1) | copy-start | bytes 3145732
  116.3 1.8 %collective-permute-start.24 = (f32[128,128]{1,0:T(8,128)S(1)}, f32[128,128]{1,0:T(8,128)S(1)}, u32[]{:S(2)}, u32[]{:S(2)}) collective-permute-start(f32[128,128]{1,0:T(8,128)S(1)} %add_add_fusion.1), channel_id=1, source_target_pairs={{0,1},{1,0},{2,3},{3,2},{4,5},{5,4},{6,7},{7,6},{8,9},{9,8},{10,11... | collective-permute-start | bytes 196616 | tf_op jit(solution)/shard_map/ppermute | solution.py:338
  118.0 4.1 %collective-permute-start.25 = (f32[128,128]{1,0:T(8,128)S(1)}, f32[128,128]{1,0:T(8,128)S(1)}, u32[]{:S(2)}, u32[]{:S(2)}) collective-permute-start(f32[128,128]{1,0:T(8,128)S(1)} %add.78.one), channel_id=1, source_target_pairs={{0,8},{8,0},{1,9},{9,1},{2,10},{10,2},{3,11},{11,3},{4,12},{12,4},... | collective-permute-start | bytes 196616 | tf_op jit(solution)/shard_map/ppermute | solution.py:338
  118.5 19.8 %collective-permute-start.34 = (bf16[2,256,384]{2,1,0:T(8,128)(2,1)S(1)}, bf16[2,256,384]{2,1,0:T(8,128)(2,1)S(1)}, u32[]{:S(2)}, u32[]{:S(2)}) collective-permute-start(bf16[2,256,384]{2,1,0:T(8,128)(2,1)S(1)} %get-tuple-element.59), channel_id=1, source_target_pairs={{0,2},{2,4},{4,6},{6,0},{1,3},{3,5},{5,7},{7,1},{8,10},{10,12},{12... | collective-permute-start | bytes 1179656 | tf_op jit(solution)/shard_map/ppermute | solution.py:330
  118.6 21.6 %collective-permute-start.35 = (bf16[2,256,384]{2,1,0:T(8,128)(2,1)S(1)}, bf16[2,256,384]{2,1,0:T(8,128)(2,1)S(1)}, u32[]{:S(2)}, u32[]{:S(2)}) collective-permute-start(bf16[2,256,384]{2,1,0:T(8,128)(2,1)S(1)} %get-tuple-element.60), channel_id=1, source_target_pairs={{0,4},{2,6},{4,0},{6,2},{1,5},{3,7},{5,1},{7,3},{8,12},{10,14},{12... | collective-permute-start | bytes 1179656 | tf_op jit(solution)/shard_map/ppermute | solution.py:330
  122.1 18.1 %collective-permute-start.36 = (bf16[2,256,384]{2,1,0:T(8,128)(2,1)S(1)}, bf16[2,256,384]{2,1,0:T(8,128)(2,1)S(1)}, u32[]{:S(2)}, u32[]{:S(2)}) collective-permute-start(bf16[2,256,384]{2,1,0:T(8,128)(2,1)S(1)} %get-tuple-element.61), channel_id=1, source_target_pairs={{0,6},{2,0},{4,2},{6,4},{1,7},{3,1},{5,3},{7,5},{8,14},{10,8},{12,... | collective-permute-start | bytes 1179656 | tf_op jit(solution)/shard_map/ppermute | solution.py:330
  122.9 5.7 %collective-permute-start.26 = (bf16[32,2048]{1,0:T(8,128)(2,1)S(1)}, bf16[32,2048]{1,0:T(8,128)(2,1)S(1)}, u32[]{:S(2)}, u32[]{:S(2)}) collective-permute-start(bf16[32,2048]{1,0:T(8,128)(2,1)S(1)} %get-tuple-element.48), channel_id=1, source_target_pairs={{0,16},{16,32},{32,48},{48,0},{1,17},{17,33},{33,49},{49,1},{2,18}... | collective-permute-start | bytes 393224 | tf_op jit(solution)/shard_map/ppermute | solution.py:330
  124.1 7.9 %collective-permute-start.27 = (bf16[32,2048]{1,0:T(8,128)(2,1)S(1)}, bf16[32,2048]{1,0:T(8,128)(2,1)S(1)}, u32[]{:S(2)}, u32[]{:S(2)}) collective-permute-start(bf16[32,2048]{1,0:T(8,128)(2,1)S(1)} %get-tuple-element.49), channel_id=1, source_target_pairs={{0,32},{16,48},{32,0},{48,16},{1,33},{17,49},{33,1},{49,17},{2,34}... | collective-permute-start | bytes 393224 | tf_op jit(solution)/shard_map/ppermute | solution.py:330
  128.6 4.1 %collective-permute-start.28 = (bf16[32,2048]{1,0:T(8,128)(2,1)S(1)}, bf16[32,2048]{1,0:T(8,128)(2,1)S(1)}, u32[]{:S(2)}, u32[]{:S(2)}) collective-permute-start(bf16[32,2048]{1,0:T(8,128)(2,1)S(1)} %get-tuple-element.50), channel_id=1, source_target_pairs={{0,48},{16,0},{32,16},{48,32},{1,49},{17,1},{33,17},{49,33},{2,50}... | collective-permute-start | bytes 393224 | tf_op jit(solution)/shard_map/ppermute | solution.py:330
  132.8 7.9 %collective-permute-start.29 = (bf16[8,2048]{1,0:T(8,128)(2,1)S(1)}, bf16[8,2048]{1,0:T(8,128)(2,1)S(1)}, u32[]{:S(2)}, u32[]{:S(2)}) collective-permute-start(bf16[8,2048]{1,0:T(8,128)(2,1)S(1)} %get-tuple-element.52), channel_id=1, source_target_pairs={{0,128},{64,192},{128,0},{192,64},{1,129},{65,193},{129,1},{193,65... | collective-permute-start | bytes 98312 | tf_op jit(solution)/shard_map/ppermute | solution.py:330
  136.7 4.9 %collective-permute-start.30 = (bf16[8,2048]{1,0:T(8,128)(2,1)S(1)}, bf16[8,2048]{1,0:T(8,128)(2,1)S(1)}, u32[]{:S(2)}, u32[]{:S(2)}) collective-permute-start(bf16[8,2048]{1,0:T(8,128)(2,1)S(1)} %get-tuple-element.53), channel_id=1, source_target_pairs={{0,64},{64,128},{128,192},{192,0},{1,65},{65,129},{129,193},{193,1... | collective-permute-start | bytes 98312 | tf_op jit(solution)/shard_map/ppermute | solution.py:330
  138.3 4.3 %collective-permute-start.31 = (bf16[8,2048]{1,0:T(8,128)(2,1)S(1)}, bf16[8,2048]{1,0:T(8,128)(2,1)S(1)}, u32[]{:S(2)}, u32[]{:S(2)}) collective-permute-start(bf16[8,2048]{1,0:T(8,128)(2,1)S(1)} %get-tuple-element.54), channel_id=1, source_target_pairs={{0,192},{64,0},{128,64},{192,128},{1,193},{65,1},{129,65},{193,129... | collective-permute-start | bytes 98312 | tf_op jit(solution)/shard_map/ppermute | solution.py:330
  140.3 9.7 %copy-start.11 = (f32[128,256]{1,0:T(8,128)S(1)}, f32[128,256]{1,0:T(8,128)}, u32[]{:S(2)}) copy-start(f32[128,256]{1,0:T(8,128)} %copy-done.10) | copy-start | bytes 393220
  140.6 9.4 %collective-permute-start.37 = (bf16[256,384]{1,0:T(8,128)(2,1)S(1)}, bf16[256,384]{1,0:T(8,128)(2,1)S(1)}, u32[]{:S(2)}, u32[]{:S(2)}) collective-permute-start(bf16[256,384]{1,0:T(8,128)(2,1)S(1)} %get-tuple-element.63), channel_id=1, source_target_pairs={{0,8},{8,0},{1,9},{9,1},{2,10},{10,2},{3,11},{11,3},{4,12},{12,4},... | collective-permute-start | bytes 589832 | tf_op jit(solution)/shard_map/ppermute | solution.py:338
  142.7 5.7 %collective-permute-start.32 = (f32[8,2048]{1,0:T(8,128)S(1)}, f32[8,2048]{1,0:T(8,128)S(1)}, u32[]{:S(2)}, u32[]{:S(2)}) collective-permute-start(f32[8,2048]{1,0:T(8,128)S(1)} %add_add_fusion.mine), channel_id=1, source_target_pairs={{0,1},{1,0},{2,3},{3,2},{4,5},{5,4},{6,7},{7,6},{8,9},{9,8},{10,11... | collective-permute-start | bytes 196616 | tf_op jit(solution)/shard_map/ppermute | solution.py:338
